TPU v7x, 32 devices: a whole 2x2x4 slice. The times are simulated.
32 devices in a mesh: ang: 8 (over z, x), sy: 2 (over y), sx: 2 (over core).
Axes of the slice: x: 2, y: 2, z: 4, core: 2. Of those that a mesh axis runs over, the one named last changes fastest.
Arguments:
- objects: bfloat16 [8, 2, 1024, 1024], P('ang', None, 'sy', 'sx'), may hold values from -4 to 4
- probe: float32 [2, 2, 256, 256], replicated, may hold values from -4 to 4
- data: bfloat16 [8, 2, 2, 2, 256, 256], P('ang', 'sy', 'sx'), may hold values from 0 to 4
- positions: int32 [8, 2, 2, 2, 2], P('ang', 'sy', 'sx'), may hold values from 0 to 384
- block_index: int32 [8, 16], replicated, may hold values from 0 to 63, as said below
- block_values: bfloat16 [8, 16, 128, 128], replicated, may hold values from -0.125 to 0.125
Outputs:
- object_grad: float32 [8, 2, 1024, 1024], P('ang', None, 'sy', 'sx')
- probe_grad: float32 [8, 2, 2, 256, 256], P('ang')
- vol_grad: float32 [2, 512, 2, 1024], P('sy', ('ang', 'sx'))
Inputs may be any that keep to these rules, and one draw needn't show every extreme that they name: `positions`: A position counts cells from 64 cells before the tile's first row or column. `block_index`: entry g names the angle g // 8 and the column block g % 8; every angle is named by exactly 16 entries.
All inputs are finite; a program needn't handle non-finite values.
Results may differ from a plain program's by a relative error of at most 0.011.
Values may be sent and summed in bfloat16 or wider, within the bound.
No kernel may reach another device: no remote copies, remote signals or barrier semaphores. Data moves between devices by JAX's collectives and lax.ppermute only.
A program may use at most 64 MiB of HBM per device.

v0:
```python
from functools import partial
import math

import jax
import jax.numpy as jnp
from jax import lax
from jax.sharding import PartitionSpec as P

PATCH = 256
RIM = 64
BLK = 128


def with_halo(cells, sides, width):
    for axis, dim in sides:
        count = lax.axis_size(axis)
        ends = count - 1
        head = lax.slice_in_dim(cells, 0, width, axis=dim)
        tail = lax.slice_in_dim(cells, cells.shape[dim] - width, cells.shape[dim], axis=dim)
        cells = jnp.concatenate(
            [
                lax.ppermute(tail, axis, [(i, (i + 1) % count) for i in range(ends)]),
                cells,
                lax.ppermute(head, axis, [((i + 1) % count, i) for i in range(ends)]),
            ],
            axis=dim,
        )
    return cells


def dft_parts(length):
    sample_ids = jnp.arange(length, dtype=jnp.int32)
    product = sample_ids[:, None] * sample_ids[None, :] % length
    phases = product.astype(jnp.float32) * (2.0 * math.pi / length)
    factor = 1.0 / math.sqrt(length)
    return (jnp.cos(phases) * factor, -jnp.sin(phases) * factor)


def dft_blocks(length):
    real_part, imag_part = dft_parts(length)
    forward = jnp.stack(
        [jnp.stack([real_part, -imag_part], 1), jnp.stack([imag_part, real_part], 1)], 0
    )
    backward = jnp.stack(
        [jnp.stack([real_part, imag_part], 1), jnp.stack([-imag_part, real_part], 1)], 0
    )
    return (forward.astype(jnp.bfloat16), backward.astype(jnp.bfloat16))


def ramp_table(width):
    column_ids = jnp.arange(width, dtype=jnp.int32)
    offsets = column_ids[None, :] - column_ids[:, None]
    odd_cells = offsets % 2 != 0
    scaled = offsets.astype(jnp.float32) * math.pi
    values = jnp.where(odd_cells, -1.0 / jnp.maximum(scaled * scaled, 1.0), 0.0)
    values = jnp.where(offsets == 0, 0.25, values)
    return values.astype(jnp.bfloat16)


def left_product(matrix, fields):
    return jnp.einsum("srtk,btkc->bsrc", matrix, fields, preferred_element_type=jnp.float32)


def right_product(fields, matrix):
    return jnp.einsum("btrc,tcsq->bsrq", fields, matrix, preferred_element_type=jnp.float32)


def cut_window(field, corner):
    return lax.dynamic_slice(
        field, (jnp.int32(0), corner[0], corner[1]), (field.shape[0], PATCH, PATCH)
    )


def patch_gradients(patches, measured, probe, forward, backward):
    patch_count = patches.shape[0]
    mode_count = probe.shape[0]
    side = patches.shape[2]
    object_real = patches[:, 0].astype(jnp.float32)[:, None]
    object_imag = patches[:, 1].astype(jnp.float32)[:, None]
    probe_real = probe[None, :, 0]
    probe_imag = probe[None, :, 1]
    exit_real = probe_real * object_real - probe_imag * object_imag
    exit_imag = probe_real * object_imag + probe_imag * object_real
    exit_waves = (
        jnp.stack([exit_real, exit_imag], 2)
        .reshape(patch_count * mode_count, 2, side, side)
        .astype(jnp.bfloat16)
    )
    half_done = left_product(forward, exit_waves).astype(jnp.bfloat16)
    far_field = right_product(half_done, backward).reshape(patch_count, mode_count, 2, side, side)
    intensity = jnp.sum(far_field * far_field, axis=(1, 2))
    misfit = intensity - measured.astype(jnp.float32)
    weighted = (
        (misfit[:, None, None] * far_field)
        .reshape(patch_count * mode_count, 2, side, side)
        .astype(jnp.bfloat16)
    )
    back_half = left_product(backward, weighted).astype(jnp.bfloat16)
    spread = right_product(back_half, forward).reshape(patch_count, mode_count, 2, side, side)
    chi_real = spread[:, :, 0]
    chi_imag = spread[:, :, 1]
    grad_real = jnp.sum(probe_real * chi_real + probe_imag * chi_imag, axis=1)
    grad_imag = jnp.sum(probe_real * chi_imag - probe_imag * chi_real, axis=1)
    patch_grad = jnp.stack([grad_real, grad_imag], 1)
    probe_real_part = jnp.sum(object_real * chi_real + object_imag * chi_imag, axis=0)
    probe_imag_part = jnp.sum(object_real * chi_imag - object_imag * chi_real, axis=0)
    probe_part = jnp.stack([probe_real_part, probe_imag_part], 1)
    return (patch_grad, probe_part)


def fold_rims(field, axis_at, extent):
    inside = lax.slice_in_dim(field, 2 * RIM, 2 * RIM + extent, axis=axis_at)
    leading = lax.slice_in_dim(field, 0, RIM, axis=axis_at)
    trailing = lax.slice_in_dim(field, extent + 3 * RIM, extent + 4 * RIM, axis=axis_at)
    widths_lead = [(0, 0)] * field.ndim
    widths_lead[axis_at] = (0, extent - RIM)
    widths_trail = [(0, 0)] * field.ndim
    widths_trail[axis_at] = (extent - RIM, 0)
    return inside + jnp.pad(leading, widths_lead) + jnp.pad(trailing, widths_trail)


def body(objects, probe, data, positions, block_index, block_values):
    forward, backward = dft_blocks(PATCH)
    tile_rows = objects.shape[2]
    tile_cols = objects.shape[3]
    padded = with_halo(objects[0], (("sy", 1), ("sx", 2)), RIM)
    starts = positions[0, 0, 0]
    patches = jax.vmap(partial(cut_window, padded))(starts)
    patch_grad, probe_part = patch_gradients(patches, data[0, 0, 0], probe, forward, backward)

    def place_patch(grad_piece, corner):
        empty = jnp.zeros(padded.shape, jnp.float32)
        return lax.dynamic_update_slice(empty, grad_piece, (jnp.int32(0), corner[0], corner[1]))

    running_sum = jnp.sum(jax.vmap(place_patch)(patch_grad, starts), axis=0)
    from_rows = with_halo(running_sum.astype(jnp.bfloat16), (("sy", 1),), RIM).astype(
        running_sum.dtype
    )
    row_folded = fold_rims(from_rows, 1, tile_rows)
    from_cols = with_halo(row_folded.astype(jnp.bfloat16), (("sx", 2),), RIM).astype(
        row_folded.dtype
    )
    object_grad = fold_rims(from_cols, 2, tile_cols)
    tile_count = lax.axis_size("sy") * lax.axis_size("sx")
    probe_total = lax.psum(probe_part.astype(jnp.bfloat16), ("sy", "sx")).astype(jnp.float32)
    probe_grad = (probe_total / math.sqrt(starts.shape[0] * tile_count))[None]
    line_blocks = block_values.shape[0]
    width_all = line_blocks * block_values.shape[2]
    angle_count = lax.axis_size("ang")
    column_parts = lax.axis_size("sx")
    rows_here = tile_rows // (angle_count * column_parts)
    ramp_matrix = ramp_table(width_all)
    sinogram = object_grad.astype(jnp.bfloat16)[None]
    ramp_split = ramp_matrix.reshape(column_parts, tile_cols, width_all)
    received = lax.all_to_all(sinogram, ("ang", "sx"), split_axis=2, concat_axis=0, tiled=True)
    shaped = received.reshape(angle_count, column_parts, received.shape[1], rows_here, tile_cols)
    result = jnp.einsum("ascrt,stv->acrv", shaped, ramp_split, preferred_element_type=jnp.float32)
    filtered = result.astype(jnp.bfloat16)
    line_data = filtered.reshape(filtered.shape[0], 2, rows_here, line_blocks, BLK)
    angle_of = block_index // line_blocks
    column_of = block_index % line_blocks
    picked = line_data[angle_of, :, :, column_of, :]
    volume = jnp.einsum(
        "bkcru,bkuv->rcbv", picked, block_values, preferred_element_type=jnp.float32
    )
    vol_grad = volume.reshape(1, rows_here, 2, width_all)
    return (object_grad[None], probe_grad, vol_grad)


def solution(mesh):
    placed = (
        P("ang", None, "sy", "sx"),
        P(),
        P("ang", "sy", "sx", None, None, None),
        P("ang", "sy", "sx", None, None),
        P(),
        P(),
    )
    return jax.shard_map(
        body,
        mesh=mesh,
        in_specs=placed,
        out_specs=(
            P("ang", None, "sy", "sx"),
            P("ang", None, None, None, None),
            P("sy", ("ang", "sx"), None, None),
        ),
        check_vma=False,
    )
```

profile of v0, /device:TPU:0, one launch (start us, length us, event | category | flops | bytes accessed | tf_op | source)
XLA Modules:
  0.0 181.1 jit_solution(15848655048342309975)
XLA Ops:
  7.2 1.1 fusion.84
  8.3 4.9 %collective-permute-start = (bf16[2,64,512]{2,1,0:T(8,128)(2,1)S(1)}, bf16[2,64,512]{2,1,0:T(8,128)(2,1)S(1)}, u32[]{:S(2)}, u32[]{:S(2)}) collective-permute-start(bf16[2,64,512]{2,1,0:T(8,128)(2,1)S(1)} %get-tuple-element.81), channel_id=1, source_target_pairs={{0,2},{1,3},{4,6},{5,7},{8,10},{9,11},{12,14},{13,15},{16,18},{17,... | collective-permute-start | bytes 393224 | tf_op jit(solution)/shard_map/ppermute | solution.py:22
  13.2 1.3 collective-permute-start.1
  14.5 1.0 fusion.59
  16.4 1.0 negate_convert_fusion
  18.3 1.3 slice_bitcast_fusion.3
  21.1 1.0 pad_maximum_fusion.5
  22.1 2.2 %collective-permute-start.2 = (bf16[2,640,64]{2,1,0:T(8,128)(2,1)}, bf16[2,640,64]{2,1,0:T(8,128)(2,1)}, u32[]{:S(2)}, u32[]{:S(2)}) collective-permute-start(bf16[2,640,64]{2,1,0:T(8,128)(2,1)} %get-tuple-element.77), channel_id=1, source_target_pairs={{0,1},{2,3},{4,5},{6,7},{8,9},{10,11},{12,13},{14,15},{16,17},{18,... | collective-permute-start | bytes 491528 | tf_op jit(solution)/shard_map/ppermute | solution.py:22
  24.3 1.5 collective-permute-start.3
  26.1 1.0 copy.66
  27.1 1.8 copy.70
  28.9 2.0 %maximum_bitcast_fusion.3 = (bf16[2,256,2,256,1]{3,1,2,0,4:T(8,128)(2,1)}, bf16[2,256,2,256,1]{3,1,2,0,4:T(8,128)(2,1)}) fusion(bf16[1,256,2,256]{3,1,2,0:T(8,128)(2,1)} %get-tuple-element.90, bf16[1,256,2,256]{3,1,2,0:T(8,128)(2,1)S(1)} %get-tuple-element.85, bf16[1,256,2,256]{3,1,2,0:T(8,128)(2,1)S(1)} %get-tuple-element.86, ...), kind=kLoop, calls=%fused_computation.73 | loop fusion | flops 524288 | bytes 2097152 | tf_op jit(solution)/shard_map/stack | solution.py:41
  30.9 2.2 %pad_maximum_fusion = bf16[2,640,640]{2,1,0:T(8,128)(2,1)S(1)} fusion(bf16[2,640,64]{2,1,0:T(8,128)(2,1)} %collective-permute-done.3, bf16[2,64,512]{2,1,0:T(8,128)(2,1)} %copy-done.11, bf16[2,512,512]{2,1,0:T(8,128)(2,1)S(1)} %bitcast.220, bf16[2,64,512]{2,1,0:T(8,128)(2,1)} %copy-done.10, bf16[2,640,64]{2,1,0:T(8,128)(2,1)} %collective-permute-done.2), kind=kLoop, calls=%fused_computation.46 | loop fusion | flops 8192000 | bytes 3276800 | tf_op jit(solution)/shard_map/concatenate | solution.py:20
  33.1 5.3 %while.2 = (s32[]{:T(128)}, bf16[2,640,640]{2,1,0:T(8,128)(2,1)S(1)}, s32[2,3]{1,0:T(2,128)S(1)}, bf16[2,2,256,256]{3,2,1,0:T(8,128)(2,1)}, s32[]{:T(128)}) while((s32[]{:T(128)}, bf16[2,640,640]{2,1,0:T(8,128)(2,1)S(1)}, s32[2,3]{1,0:T(2,128)S(1)}, bf16[2,2,256,256]{3,2,1,0:T(8,128)(2,1)}, s32[]{:T(128)}) %tuple.65), condition=%wide.while_cond, body=%wide.while_body.sunk | while | flops 2 | bytes 525929 | solution.py:69
  33.7 2.0 %bitcast_dynamic-update-slice_fusion.2 = bf16[2,2,256,256]{3,2,1,0:T(8,128)(2,1)} fusion(bf16[2,2,256,256]{3,2,1,0:T(8,128)(2,1)} %get-tuple-element.167, s32[]{:T(128)} %get-tuple-element.164, bf16[2,640,640]{2,1,0:T(8,128)(2,1)S(1)} %get-tuple-element.170, s32[]{:T(128)} %bitcast.206, s32[]{:T(128)} %bitcast.207), kind=kLoop, calls=%fused_computation.1.clone.1 | loop fusion | bytes 525824 | tf_op jit(solution)/shard_map/vmap()/gather
  36.4 2.0 %bitcast_dynamic-update-slice_fusion.2 = bf16[2,2,256,256]{3,2,1,0:T(8,128)(2,1)} fusion(bf16[2,2,256,256]{3,2,1,0:T(8,128)(2,1)} %get-tuple-element.167, s32[]{:T(128)} %get-tuple-element.164, bf16[2,640,640]{2,1,0:T(8,128)(2,1)S(1)} %get-tuple-element.170, s32[]{:T(128)} %bitcast.206, s32[]{:T(128)} %bitcast.207), kind=kLoop, calls=%fused_computation.1.clone.1 | loop fusion | bytes 525824 | tf_op jit(solution)/shard_map/vmap()/gather
  38.4 1.1 bitcast_convert_fusion.4
  40.0 1.3 subtract_convert_fusion
  41.3 5.0 %fusion.16 = (f32[4,256,256]{1,2,0:T(8,128)}, f32[2,256,4,256,1]{3,1,4,2,0:T(8,128)}) fusion(bf16[4,1,256,256]{2,3,1,0:T(8,128)(2,1)} %bitcast.228, bf16[4,1,256,256]{2,3,1,0:T(8,128)(2,1)} %bitcast.227, bf16[1,256,2,256]{3,1,2,0:T(8,128)(2,1)S(1)} %copy-done.9, bf16[1,256,2,256]{3,1,2,0:T(8,128)(2,1)S(1)} %copy-done.8, ...), kind=kOutput, calls=%fused_computation.31 | convolution fusion | flops 1078198272 | bytes 5242880 | tf_op jit(solution)/shard_map/btrc,tcsq->bsrq/dot_general | solution.py:65
  46.3 1.4 bitcast_reduce_fusion
  47.8 1.1 mul.359
  48.8 3.3 %fusion.37 = f32[2,256,4,256,1]{3,1,4,2,0:T(8,128)S(1)} fusion(bf16[2,256,2,256,1]{3,1,2,0,4:T(8,128)(2,1)} %get-tuple-element.95, bf16[1,256,2,256]{3,1,2,0:T(8,128)(2,1)S(1)} %get-tuple-element.86, bf16[1,256,2,256]{3,1,2,0:T(8,128)(2,1)} %copy-done.4, f32[2,256,4,256,1]{3,1,4,2,0:T(8,128)} %get-tuple-element.94, f32[4,256,256]{1,2,0:T(8,128)} %bitcast.221), kind=kOutput, calls=%fused_computation.52 | convolution fusion | flops 1076363264 | bytes 6291456 | tf_op jit(solution)/shard_map/btrc,tcsq->bsrq/dot_general | solution.py:65
  52.1 2.7 %add_reduce_fusion = (bf16[2,256,256]{1,2,0:T(8,128)(2,1)S(1)}, bf16[2,256,256]{1,2,0:T(8,128)(2,1)}, f32[2,256,256]{1,2,0:T(8,128)S(1)}, f32[2,256,256]{1,2,0:T(8,128)S(1)}) fusion(f32[2,2,2,256,256]{3,4,1,0,2:T(8,128)S(1)} %bitcast.217, f32[2,256,256]{1,2,0:T(8,128)} %copy-done.3, f32[2,256,256]{1,2,0:T(8,128)} %copy-done.2, ...), kind=kLoop, calls=%fused_computation.68 | loop fusion | flops 3670016 | bytes 5767168 | tf_op jit(solution)/shard_map/reduce_sum | solution.py:105
  55.0 3.1 %broadcast_in_dim.40 = f32[2,2,640,640]{3,2,1,0:T(8,128)} broadcast(f32[]{:T(128)} %constant.69.clone.1), dimensions={} | broadcast | bytes 6553604 | tf_op jit(solution)/shard_map/vmap(vmap())/broadcast_in_dim;vmap()/broadcast_in_dim | solution.py:133
  58.1 33.1 %while.3 = (s32[]{:T(128)}, f32[2,2,640,640]{3,2,1,0:T(8,128)}, s32[2,4]{1,0:T(2,128)S(1)}, f32[2,2,256,256]{2,3,0,1:T(8,128)S(1)}, s32[]{:T(128)}, /*index=5*/s32[4]{0:T(128)S(1)}, s32[]{:T(128)}) while((s32[]{:T(128)}, f32[2,2,640,640]{3,2,1,0:T(8,128)}, s32[2,4]{1,0:T(2,128)S(1)}, f32[2,2,256,256]{2,3,0,1:T(8,128)S(1)}, s32[]{:T(128)}, ...), condition=%wide.while_cond.1, body=%wide.while_body.1.sunk | while | flops 131101 | bytes 4718791 | solution.py:133
  58.8 3.3 %and_reduce_fusion.2 = pred[]{:T(512)} fusion(s32[4]{0:T(128)S(1)} %get-tuple-element.193, s32[1]{0:T(128)} %bitcast.211, s32[1]{0:T(128)} %bitcast.212, s32[1]{0:T(128)} %bitcast.213, s32[1]{0:T(128)} %bitcast.214), kind=kLoop, calls=%fused_computation.4.clone.1 | loop fusion | flops 27 | bytes 33 | tf_op jit(solution)/shard_map/vmap(vmap())/scatter
  62.3 3.9 %dynamic-slice_select_fusion.2 = f32[1,2,256,256]{3,2,1,0:T(8,128)S(1)} fusion(f32[1,2,256,256]{3,2,1,0:T(8,128)S(1)} %copy.126, f32[2,2,640,640]{3,2,1,0:T(8,128)} %get-tuple-element.182, s32[]{:T(128)} %bitcast.208, s32[]{:T(128)} %bitcast.209, s32[]{:T(128)} %bitcast.210, pred[]{:T(512)} %and_reduce_fusion.2), kind=kLoop, calls=%fused_computation.3.clone.1 | loop fusion | flops 131072 | bytes 1572877 | tf_op jit(solution)/shard_map/vmap(vmap())/scatter
  66.3 8.5 %dynamic-update-slice.8 = f32[2,2,640,640]{3,2,1,0:T(8,128)} dynamic-update-slice(f32[2,2,640,640]{3,2,1,0:T(8,128)} %get-tuple-element.182, f32[1,2,256,256]{3,2,1,0:T(8,128)S(1)} %dynamic-slice_select_fusion.2, s32[]{:T(128)} %bitcast.208, s32[]{:T(128)} %constant.70.clone.1..sunk, s32[]{:T(128)} %bitcast.209, s32[]{:T(128)} %bitcast.210) | dynamic-update-slice | bytes 1048580 | tf_op jit(solution)/shard_map/vmap(vmap())/scatter
  75.4 3.3 %and_reduce_fusion.2 = pred[]{:T(512)} fusion(s32[4]{0:T(128)S(1)} %get-tuple-element.193, s32[1]{0:T(128)} %bitcast.211, s32[1]{0:T(128)} %bitcast.212, s32[1]{0:T(128)} %bitcast.213, s32[1]{0:T(128)} %bitcast.214), kind=kLoop, calls=%fused_computation.4.clone.1 | loop fusion | flops 27 | bytes 33 | tf_op jit(solution)/shard_map/vmap(vmap())/scatter
  79.0 3.9 %dynamic-slice_select_fusion.2 = f32[1,2,256,256]{3,2,1,0:T(8,128)S(1)} fusion(f32[1,2,256,256]{3,2,1,0:T(8,128)S(1)} %copy.126, f32[2,2,640,640]{3,2,1,0:T(8,128)} %get-tuple-element.182, s32[]{:T(128)} %bitcast.208, s32[]{:T(128)} %bitcast.209, s32[]{:T(128)} %bitcast.210, pred[]{:T(512)} %and_reduce_fusion.2), kind=kLoop, calls=%fused_computation.3.clone.1 | loop fusion | flops 131072 | bytes 1572877 | tf_op jit(solution)/shard_map/vmap(vmap())/scatter
  82.9 8.3 %dynamic-update-slice.8 = f32[2,2,640,640]{3,2,1,0:T(8,128)} dynamic-update-slice(f32[2,2,640,640]{3,2,1,0:T(8,128)} %get-tuple-element.182, f32[1,2,256,256]{3,2,1,0:T(8,128)S(1)} %dynamic-slice_select_fusion.2, s32[]{:T(128)} %bitcast.208, s32[]{:T(128)} %constant.70.clone.1..sunk, s32[]{:T(128)} %bitcast.209, s32[]{:T(128)} %bitcast.210) | dynamic-update-slice | bytes 1048580 | tf_op jit(solution)/shard_map/vmap(vmap())/scatter
  91.2 3.8 %reduce_sum.66 = bf16[2,640,640]{2,1,0:T(8,128)(2,1)S(1)} reduce(f32[2,2,640,640]{3,2,1,0:T(8,128)} %get-tuple-element.16, f32[]{:T(128)} %constant.69.clone.1), dimensions={0}, to_apply=%region_5.6 | reduce | flops 819200 | bytes 8192004 | tf_op jit(solution)/shard_map/reduce_sum | solution.py:135
  95.0 4.6 %collective-permute-start.4 = (bf16[2,64,640]{2,1,0:T(8,128)(2,1)S(1)}, bf16[2,64,640]{2,1,0:T(8,128)(2,1)S(1)}, u32[]{:S(2)}, u32[]{:S(2)}) collective-permute-start(bf16[2,64,640]{2,1,0:T(8,128)(2,1)S(1)} %get-tuple-element.73), channel_id=1, source_target_pairs={{0,2},{1,3},{4,6},{5,7},{8,10},{9,11},{12,14},{13,15},{16,18},{17,... | collective-permute-start | bytes 491528 | tf_op jit(solution)/shard_map/ppermute | solution.py:22
  99.6 1.3 collective-permute-start.5
  100.9 3.2 %collective-permute-done.4 = bf16[2,64,640]{2,1,0:T(8,128)(2,1)S(1)} collective-permute-done((bf16[2,64,640]{2,1,0:T(8,128)(2,1)S(1)}, bf16[2,64,640]{2,1,0:T(8,128)(2,1)S(1)}, u32[]{:S(2)}, u32[]{:S(2)}) %collective-permute-start.4) | collective-permute-done | bytes 163872 | tf_op jit(solution)/shard_map/ppermute | solution.py:22
  104.1 4.3 %collective-permute-done.5 = bf16[2,64,640]{2,1,0:T(8,128)(2,1)S(1)} collective-permute-done((bf16[2,64,640]{2,1,0:T(8,128)(2,1)S(1)}, bf16[2,64,640]{2,1,0:T(8,128)(2,1)S(1)}, u32[]{:S(2)}, u32[]{:S(2)}) %collective-permute-start.5) | collective-permute-done | bytes 163872 | tf_op jit(solution)/shard_map/ppermute | solution.py:24
  109.6 1.8 %collective-permute-start.6 = (bf16[2,512,64]{2,1,0:T(8,128)(2,1)S(1)}, bf16[2,512,64]{2,1,0:T(8,128)(2,1)S(1)}, u32[]{:S(2)}, u32[]{:S(2)}) collective-permute-start(bf16[2,512,64]{2,1,0:T(8,128)(2,1)S(1)} %get-tuple-element.75), channel_id=1, source_target_pairs={{0,1},{2,3},{4,5},{6,7},{8,9},{10,11},{12,13},{14,15},{16,17},{18,... | collective-permute-start | bytes 393224 | tf_op jit(solution)/shard_map/ppermute | solution.py:22
  111.4 1.3 collective-permute-start.7
  112.7 2.1 %collective-permute-done.7 = bf16[2,512,64]{2,1,0:T(8,128)(2,1)S(1)} collective-permute-done((bf16[2,512,64]{2,1,0:T(8,128)(2,1)S(1)}, bf16[2,512,64]{2,1,0:T(8,128)(2,1)S(1)}, u32[]{:S(2)}, u32[]{:S(2)}) %collective-permute-start.7) | collective-permute-done | bytes 131104 | tf_op jit(solution)/shard_map/ppermute | solution.py:24
  115.6 1.8 convert_bitcast_fusion
  117.4 2.1 %copy.75 = bf16[1,2,512,512]{3,1,0,2:T(2,128)(2,1)} copy(bf16[1,2,512,512]{3,2,1,0:T(8,128)(2,1)S(1)} %get-tuple-element.69) | data formatting | bytes 2097152 | tf_op jit(solution)/shard_map/broadcast_in_dim | solution.py:153
  119.4 5.5 %all-to-all-start = ((bf16[1,2,512,512]{3,1,0,2:T(2,128)(2,1)}), bf16[1,2,512,512]{3,1,0,2:T(2,128)(2,1)S(1)}, u32[]{:S(2)}, u32[]{:S(2)}) async-start(bf16[1,2,512,512]{3,1,0,2:T(2,128)(2,1)} %copy.75), calls=%async_computation | async-start | bytes 2097152 | tf_op jit(solution)/shard_map/all_to_all | solution.py:155
  126.2 36.0 %all-reduce.4.cloned.1.call-done = bf16[2,2,256,256]{2,3,0,1:T(8,128)(2,1)} async-done(((bf16[2,2,256,256]{2,3,0,1:T(8,128)(2,1)}), bf16[2,2,256,256]{2,3,0,1:T(8,128)(2,1)}) %all-reduce.4.cloned.1.call-update) | async-done | bytes 524304 | tf_op jit(solution)/shard_map/psum | solution.py:145
  162.3 1.1 multiply_bitcast_fusion
  163.4 1.3 copy.82
  164.9 3.9 %fusion.29 = bf16[8,2,4,8,8,128]{5,4,3,2,1,0:T(8,128)(2,1)S(1)} fusion(s32[2,512]{1,0:T(2,128)S(1)} %multiply_add_fusion, bf16[8,2,2,32,512]{4,3,1,0,2:T(8,128)(2,1)S(1)} %bitcast.224), kind=kOutput, calls=%fused_computation.48 | convolution fusion | flops 1097334784 | bytes 2101248 | tf_op jit(solution)/shard_map/ascrt,stv->acrv/dot_general | solution.py:157
  169.0 1.1 gather_fusion
  170.1 3.1 %fusion.34 = f32[32,2,8,128]{3,0,1,2:T(8,128)S(1)} fusion(bf16[8,16,2,32,128]{4,3,2,1,0:T(8,128)(2,1)S(1)} %bitcast.216, bf16[8,16,128,128]{3,2,1,0:T(8,128)(2,1)} %param.11), kind=kOutput, calls=%fused_computation.51 | convolution fusion | flops 268435456 | bytes 6553600 | tf_op jit(solution)/shard_map/bkcru,bkuv->rcbv/dot_general | solution.py:163
  (80 shorter events, 11.7 us)
Async XLA Ops:
  7.2 12.4 %copy-start.15 = (s32[3]{0:T(128)S(1)}, s32[3]{0:T(128)}, u32[]{:S(2)}) copy-start(s32[3]{0:T(128)} %constant.72.clone.1) | copy-start | bytes 40
  7.2 13.9 %copy-start = (bf16[1,2,512,512]{3,2,1,0:T(8,128)(2,1)S(1)}, bf16[1,2,512,512]{3,2,1,0:T(8,128)(2,1)}, u32[]{:S(2)}) copy-start(bf16[1,2,512,512]{3,2,1,0:T(8,128)(2,1)} %param.6) | copy-start | bytes 3145732
  8.3 12.2 %collective-permute-start = (bf16[2,64,512]{2,1,0:T(8,128)(2,1)S(1)}, bf16[2,64,512]{2,1,0:T(8,128)(2,1)S(1)}, u32[]{:S(2)}, u32[]{:S(2)}) collective-permute-start(bf16[2,64,512]{2,1,0:T(8,128)(2,1)S(1)} %get-tuple-element.81), channel_id=1, source_target_pairs={{0,2},{1,3},{4,6},{5,7},{8,10},{9,11},{12,14},{13,15},{16,18},{17,... | collective-permute-start | bytes 393224 | tf_op jit(solution)/shard_map/ppermute | solution.py:22
  13.2 7.3 %collective-permute-start.1 = (bf16[2,64,512]{2,1,0:T(8,128)(2,1)S(1)}, bf16[2,64,512]{2,1,0:T(8,128)(2,1)S(1)}, u32[]{:S(2)}, u32[]{:S(2)}) collective-permute-start(bf16[2,64,512]{2,1,0:T(8,128)(2,1)S(1)} %get-tuple-element.82), channel_id=1, source_target_pairs={{2,0},{3,1},{6,4},{7,5},{10,8},{11,9},{14,12},{15,13},{18,16},{19,... | collective-permute-start | bytes 393224 | tf_op jit(solution)/shard_map/ppermute | solution.py:24
  20.4 10.5 %copy-start.4 = (bf16[1,256,2,256]{3,1,2,0:T(8,128)(2,1)}, bf16[1,256,2,256]{3,1,2,0:T(8,128)(2,1)S(1)}, u32[]{:S(2)}) copy-start(bf16[1,256,2,256]{3,1,2,0:T(8,128)(2,1)S(1)} %get-tuple-element.89) | copy-start | bytes 786436
  20.4 10.5 %copy-start.7 = (bf16[1,256,2,256]{3,1,2,0:T(8,128)(2,1)}, bf16[1,256,2,256]{3,1,2,0:T(8,128)(2,1)S(1)}, u32[]{:S(2)}) copy-start(bf16[1,256,2,256]{3,1,2,0:T(8,128)(2,1)S(1)} %get-tuple-element.85) | copy-start | bytes 786436
  20.4 0.7 copy-start.10
  21.1 1.0 copy-start.11
  22.1 8.8 %collective-permute-start.2 = (bf16[2,640,64]{2,1,0:T(8,128)(2,1)}, bf16[2,640,64]{2,1,0:T(8,128)(2,1)}, u32[]{:S(2)}, u32[]{:S(2)}) collective-permute-start(bf16[2,640,64]{2,1,0:T(8,128)(2,1)} %get-tuple-element.77), channel_id=1, source_target_pairs={{0,1},{2,3},{4,5},{6,7},{8,9},{10,11},{12,13},{14,15},{16,17},{18,... | collective-permute-start | bytes 491528 | tf_op jit(solution)/shard_map/ppermute | solution.py:22
  24.3 6.6 %collective-permute-start.3 = (bf16[2,640,64]{2,1,0:T(8,128)(2,1)}, bf16[2,640,64]{2,1,0:T(8,128)(2,1)}, u32[]{:S(2)}, u32[]{:S(2)}) collective-permute-start(bf16[2,640,64]{2,1,0:T(8,128)(2,1)} %get-tuple-element.78), channel_id=1, source_target_pairs={{1,0},{3,2},{5,4},{7,6},{9,8},{11,10},{13,12},{15,14},{17,16},{19,... | collective-permute-start | bytes 491528 | tf_op jit(solution)/shard_map/ppermute | solution.py:24
  33.1 6.9 %copy-start.1 = (f32[2,256,256]{1,2,0:T(8,128)S(1)}, f32[2,256,256]{1,2,0:T(8,128)}, u32[]{:S(2)}) copy-start(f32[2,256,256]{1,2,0:T(8,128)} %copy.66) | copy-start | bytes 1572868
  39.6 1.7 copy-start.8
  39.6 1.7 copy-start.9
  39.8 6.5 %copy-start.2 = (f32[2,256,256]{1,2,0:T(8,128)}, f32[2,256,256]{1,2,0:T(8,128)S(1)}, u32[]{:S(2)}) copy-start(f32[2,256,256]{1,2,0:T(8,128)S(1)} %copy.65) | copy-start | bytes 1572868
  40.0 6.3 %copy-start.3 = (f32[2,256,256]{1,2,0:T(8,128)}, f32[2,256,256]{1,2,0:T(8,128)S(1)}, u32[]{:S(2)}) copy-start(f32[2,256,256]{1,2,0:T(8,128)S(1)} %copy.67) | copy-start | bytes 1572868
  41.3 6.4 %copy-start.5 = (bf16[1,1,1,2,256,256]{4,5,3,2,1,0:T(8,128)(2,1)S(1)}, bf16[1,1,1,2,256,256]{4,5,3,2,1,0:T(8,128)(2,1)}, u32[]{:S(2)}) copy-start(bf16[1,1,1,2,256,256]{4,5,3,2,1,0:T(8,128)(2,1)} %copy.70) | copy-start | bytes 786436
  54.9 3.2 %copy-start.12 = (s32[4]{0:T(128)S(1)}, s32[4]{0:T(128)}, u32[]{:S(2)}) copy-start(s32[4]{0:T(128)} %constant.297) | copy-start | bytes 52
  95.0 9.1 %collective-permute-start.4 = (bf16[2,64,640]{2,1,0:T(8,128)(2,1)S(1)}, bf16[2,64,640]{2,1,0:T(8,128)(2,1)S(1)}, u32[]{:S(2)}, u32[]{:S(2)}) collective-permute-start(bf16[2,64,640]{2,1,0:T(8,128)(2,1)S(1)} %get-tuple-element.73), channel_id=1, source_target_pairs={{0,2},{1,3},{4,6},{5,7},{8,10},{9,11},{12,14},{13,15},{16,18},{17,... | collective-permute-start | bytes 491528 | tf_op jit(solution)/shard_map/ppermute | solution.py:22
  99.6 8.8 %collective-permute-start.5 = (bf16[2,64,640]{2,1,0:T(8,128)(2,1)S(1)}, bf16[2,64,640]{2,1,0:T(8,128)(2,1)S(1)}, u32[]{:S(2)}, u32[]{:S(2)}) collective-permute-start(bf16[2,64,640]{2,1,0:T(8,128)(2,1)S(1)} %get-tuple-element.74), channel_id=1, source_target_pairs={{2,0},{3,1},{6,4},{7,5},{10,8},{11,9},{14,12},{15,13},{18,16},{19,... | collective-permute-start | bytes 491528 | tf_op jit(solution)/shard_map/ppermute | solution.py:24
  108.4 0.7 copy-start.14
  109.6 3.1 %collective-permute-start.6 = (bf16[2,512,64]{2,1,0:T(8,128)(2,1)S(1)}, bf16[2,512,64]{2,1,0:T(8,128)(2,1)S(1)}, u32[]{:S(2)}, u32[]{:S(2)}) collective-permute-start(bf16[2,512,64]{2,1,0:T(8,128)(2,1)S(1)} %get-tuple-element.75), channel_id=1, source_target_pairs={{0,1},{2,3},{4,5},{6,7},{8,9},{10,11},{12,13},{14,15},{16,17},{18,... | collective-permute-start | bytes 393224 | tf_op jit(solution)/shard_map/ppermute | solution.py:22
  111.4 3.4 %collective-permute-start.7 = (bf16[2,512,64]{2,1,0:T(8,128)(2,1)S(1)}, bf16[2,512,64]{2,1,0:T(8,128)(2,1)S(1)}, u32[]{:S(2)}, u32[]{:S(2)}) collective-permute-start(bf16[2,512,64]{2,1,0:T(8,128)(2,1)S(1)} %get-tuple-element.76), channel_id=1, source_target_pairs={{1,0},{3,2},{5,4},{7,6},{9,8},{11,10},{13,12},{15,14},{17,16},{19,... | collective-permute-start | bytes 393224 | tf_op jit(solution)/shard_map/ppermute | solution.py:24
  117.3 7.9 %copy-start.6 = (bf16[2,256,256]{1,2,0:T(8,128)(2,1)S(1)}, bf16[2,256,256]{1,2,0:T(8,128)(2,1)}, u32[]{:S(2)}) copy-start(bf16[2,256,256]{1,2,0:T(8,128)(2,1)} %get-tuple-element.40) | copy-start | bytes 786436
  117.4 8.8 %copy-start.13 = (s32[8,16]{1,0:T(8,128)S(1)}, s32[8,16]{1,0:T(8,128)}, u32[]{:S(2)}) copy-start(s32[8,16]{1,0:T(8,128)} %param.10) | copy-start | bytes 1540
  119.4 45.3 %all-to-all-start = ((bf16[1,2,512,512]{3,1,0,2:T(2,128)(2,1)}), bf16[1,2,512,512]{3,1,0,2:T(2,128)(2,1)S(1)}, u32[]{:S(2)}, u32[]{:S(2)}) async-start(bf16[1,2,512,512]{3,1,0,2:T(2,128)(2,1)} %copy.75), calls=%async_computation | async-start | bytes 2097152 | tf_op jit(solution)/shard_map/all_to_all | solution.py:155
  125.0 37.3 %all-reduce.4.cloned.1.call-start = ((), (), s32[]{:S(2)}) async-start(), calls=%async_computation.1 | async-start | bytes 1048576 | tf_op jit(solution)/shard_map/psum | solution.py:145
Sparse Core Ops, SparseCore 0:
  128.7 33.5 all-reduce.3
where the time goes:
time: 182 us; the launch traced here: 181 us
  waiting for transfers between devices  45.7 us (25%)
  local copies, waits for them, and re-layouts  40.9 us (22%)
  other arithmetic  39.9 us (22%)
  starting transfers between devices  24.6 us (14%)
  matrix products  15.4 us (8%)
  between operations  14.4 us (8%)
    psum x1, waiting for transfers between devices, body(): lax.psum(probe_part.astype(jnp.bfloat16), ('sy', 'sx')).astype(jnp.float32)  36 us
    scatter x10, local copies, waits for them, and re-layouts  18.5 us
    scatter x4, other arithmetic  14.5 us
    ppermute x4, starting transfers between devices, with_halo(): lax.ppermute(tail, axis, [(i, (i + 1) % count) for i in range(ends)])  13.5 us
    dot_general x2, matrix products, right_product(): jnp.einsum('btrc,tcsq->bsrq', fields, matrix, preferred_element_type=jnp....  8.37 us
    ppermute x4, waiting for transfers between devices, with_halo(): lax.ppermute(head, axis, [((i + 1) % count, i) for i in range(ends)])  6.41 us
    all_to_all x1, starting transfers between devices, body(): lax.all_to_all(sinogram, ('ang', 'sx'), split_axis=2, concat_axis=0, tile...  5.54 us
    ppermute x4, starting transfers between devices, with_halo(): lax.ppermute(head, axis, [((i + 1) % count, i) for i in range(ends)])  5.34 us
  transfers between devices with their start and end apart: 10, of which 4 were waited for; matrix products, arithmetic and copies ran while one was open for 8% of the time, Pallas kernels for 0%

commit v1 on v0

v1 whole, which is shorter than its diff:
```python
from functools import partial
import math

import jax
import jax.numpy as jnp
import ml_dtypes
import numpy as np
from jax import lax
from jax.experimental import pallas as pl
from jax.experimental.pallas import tpu as pltpu
from jax.sharding import PartitionSpec as P

PATCH = 256
RIM = 64
BLK = 128
SWAP = [(0, 1), (1, 0)]
CROSS = [(0, 3), (3, 0), (1, 2), (2, 1)]
MIB = 1 << 20

VMEM = pl.BlockSpec(memory_space=pltpu.VMEM)
SMEM = pl.BlockSpec(memory_space=pltpu.SMEM)
HBM = pl.BlockSpec(memory_space=pl.ANY)


def dft_blocks(length):
    ids = np.arange(length)
    phases = (ids[:, None] * ids[None, :] % length) * (2.0 * math.pi / length)
    factor = 1.0 / math.sqrt(length)
    re, im = np.cos(phases) * factor, -np.sin(phases) * factor
    forward = np.block([[re, -im], [im, re]])
    backward = np.block([[re, im], [-im, re]])
    return np.stack([forward, backward]).astype(np.float32).astype(ml_dtypes.bfloat16)


def ramp_table(width):
    ids = np.arange(width)
    offsets = ids[None, :] - ids[:, None]
    scaled = offsets.astype(np.float64) * math.pi
    values = np.where(offsets % 2 != 0, -1.0 / np.maximum(scaled * scaled, 1.0), 0.0)
    values = np.where(offsets == 0, 0.25, values)
    return values.astype(np.float32).astype(ml_dtypes.bfloat16)


def shape(dims, dtype=jnp.bfloat16):
    return jax.ShapeDtypeStruct(dims, dtype)


def call(kernel, outs, ins, specs, scratch=(), limit=32, flops=0, moved=0):
    return pl.pallas_call(
        kernel,
        out_shape=outs,
        in_specs=specs,
        out_specs=jax.tree.map(lambda _: VMEM, outs),
        scratch_shapes=list(scratch),
        compiler_params=pltpu.CompilerParams(vmem_limit_bytes=limit * MIB),
        cost_estimate=pl.CostEstimate(flops=flops, bytes_accessed=moved, transcendentals=0),
    )(*ins)


def aligned(value, step):
    return pl.multiple_of(value, step)


def edge_kernel(obj, to_y, to_x, to_d):
    sy, sx = lax.axis_index("sy"), lax.axis_index("sx")
    rows, cols = obj.shape[1], obj.shape[2]
    r = aligned((1 - sy) * (rows - RIM), RIM)
    c = aligned((1 - sx) * (cols - BLK), BLK)
    to_y[...] = obj[:, pl.ds(r, RIM), :]
    to_x[...] = obj[:, :, pl.ds(c, BLK)]
    to_d[...] = obj[:, pl.ds(r, RIM), pl.ds(c, BLK)]


def weight_kernel(count, index, values, ramp, out, total, found):
    me = lax.axis_index("ang")
    lines, per = index.shape
    total[...] = jnp.zeros_like(total)

    def scan(e, n):
        hit = index[e // per, e % per] // lines == me

        @pl.when(hit & (n < count))
        def _():
            found[n] = e

        return n + hit.astype(jnp.int32)

    lax.fori_loop(0, lines * per, scan, jnp.int32(0))

    def add(i, carry):
        e = found[i]
        b, k = e // per, e % per
        col = aligned(index[b, k] % lines * BLK, BLK)
        to = aligned(b * BLK, BLK)
        total[:, pl.ds(to, BLK)] += jnp.dot(
            ramp[:, pl.ds(col, BLK)], values[b, k], preferred_element_type=jnp.float32
        )
        return carry

    lax.fori_loop(0, count, add, 0)
    out[...] = total[...].astype(out.dtype)


def strip_select(half, rows, h, dtype):
    i = lax.broadcasted_iota(jnp.int32, (rows // 2, rows), 0)
    j = lax.broadcasted_iota(jnp.int32, (rows // 2, rows), 1)
    return (j == i // h * 2 * h + half * h + i % h).astype(dtype)


def pick_strips(ref, c, row, rows, lanes, half, h):
    if h % 8 == 0:
        parts = [
            ref[c, pl.ds(aligned(row + q * 2 * h + half * h, 8), h), lanes]
            for q in range(rows // (2 * h))
        ]
        return jnp.concatenate(parts, axis=0).astype(jnp.bfloat16)
    whole = ref[c, pl.ds(aligned(row, 8), rows), lanes].astype(jnp.bfloat16)
    chosen = strip_select(half, rows, h, jnp.bfloat16)
    return jnp.dot(chosen, whole, preferred_element_type=jnp.float32).astype(jnp.bfloat16)


def add_strips(ref, c, row, rows, lanes, half, h, terms):
    if h % 8 == 0:
        for q in range(rows // (2 * h)):
            at = pl.ds(aligned(row + q * 2 * h + half * h, 8), h)
            ref[c, at, lanes] += terms[q * h : (q + 1) * h]
        return
    chosen = strip_select(half, rows, h, jnp.float32)
    at = pl.ds(aligned(row, 8), rows)
    ref[c, at, lanes] += lax.dot_general(
        chosen, terms, (((0,), (0,)), ((), ())), precision=lax.Precision.HIGHEST,
        preferred_element_type=jnp.float32,
    )


def rows_from(value, shift):
    rows, lanes = value.shape[0] - 8, value.shape[1]
    turned = pltpu.roll(value.reshape(rows // 8 + 1, 8, lanes), (8 - shift) % 8, 1)
    keep = lax.broadcasted_iota(jnp.int32, (rows // 8, 8, lanes), 1) < 8 - shift
    return jnp.where(keep, turned[:-1], turned[1:]).reshape(rows, lanes)


def rows_to(value, shift):
    rows, lanes = value.shape
    turned = pltpu.roll(value.reshape(rows // 8, 8, lanes), shift, 1)
    none = jnp.zeros((1, 8, lanes), value.dtype)
    keep = lax.broadcasted_iota(jnp.int32, (rows // 8 + 1, 8, lanes), 1) >= shift
    here = jnp.concatenate([turned, none], axis=0)
    before = jnp.concatenate([none, turned], axis=0)
    return jnp.where(keep, here, before).reshape(rows + 8, lanes)


def patch_kernel(
    h, pos, obj, from_y, from_x, from_d, probe, data, dft,
    grad, own, to_x, rim_x, to_y, to_d, probe_keep, probe_send,
    frame, total, stack, probe_total,
):
    sy, sx = lax.axis_index("sy"), lax.axis_index("sx")
    rows, cols = obj.shape[1], obj.shape[2]
    modes = probe.shape[0]
    patches = data.shape[0]
    f32, bf16 = jnp.float32, jnp.bfloat16
    last = RIM + rows
    row_in = aligned((1 - sy) * last, RIM)
    row_out = aligned(sy * last, RIM)
    col_in = aligned((1 - sx) * (BLK + cols), BLK)
    col_out = aligned(sx * (BLK + cols), BLK)
    inner = pl.ds(BLK, cols)
    for c in range(2):
        frame[c, RIM:last, BLK : BLK + cols] = obj[c].astype(f32)
        frame[c, pl.ds(row_out, RIM), :] = jnp.zeros((RIM, frame.shape[2]), f32)
        frame[c, :, pl.ds(col_out, BLK)] = jnp.zeros((frame.shape[1], BLK), f32)
        frame[c, RIM:last, pl.ds(col_in, BLK)] = from_x[c].astype(f32)
        frame[c, pl.ds(row_in, RIM), inner] = from_y[c].astype(f32)
        frame[c, pl.ds(row_in, RIM), pl.ds(col_in, BLK)] = from_d[c].astype(f32)
    total[...] = jnp.zeros_like(total)
    lane = lax.broadcasted_iota(jnp.int32, (PATCH, BLK), 1)
    spans = PATCH // BLK

    def place(p):
        u, v = pos[p, 0], pos[p, 1] + (BLK - RIM)
        start = aligned(v // BLK * BLK, BLK)
        top = aligned(u // 8 * 8, 8)
        return top, u - top, start, v - start

    def window(p):
        top, down, start, shift = place(p)
        out = []
        for c in range(2):
            cuts = [frame[c, pl.ds(top, PATCH + 8), pl.ds(aligned(start + k * BLK, BLK), BLK)] for k in range(spans + 1)]
            blocks = [pltpu.roll(rows_from(cut, down), (BLK - shift) % BLK, 1) for cut in cuts]
            keep = lane < BLK - shift
            out.append(
                jnp.concatenate([jnp.where(keep, blocks[k], blocks[k + 1]) for k in range(spans)], axis=1)
            )
        return out

    windows = [window(p) for p in range(patches)]
    for p in range(patches):
        o_re, o_im = windows[p]
        for m in range(modes):
            p_re, p_im = probe[m, 0], probe[m, 1]
            at = slice((p * modes + m) * PATCH, (p * modes + m + 1) * PATCH)
            stack[0:PATCH, at] = (p_re * o_re - p_im * o_im).astype(bf16)
            stack[PATCH:, at] = (p_re * o_im + p_im * o_re).astype(bf16)

    def transform(left, right, p):
        at = slice(p * modes * PATCH, (p + 1) * modes * PATCH)
        half = jnp.dot(dft[left], stack[:, at], preferred_element_type=f32).astype(bf16)
        out = []
        for m in range(modes):
            cut = slice(m * PATCH, (m + 1) * PATCH)
            wide = jnp.concatenate([half[:PATCH, cut], half[PATCH:, cut]], axis=1)
            out.append(jnp.dot(wide, dft[right], preferred_element_type=f32))
        return out

    for p in range(patches):
        far = transform(0, 1, p)
        misfit = sum(f[:, :PATCH] * f[:, :PATCH] + f[:, PATCH:] * f[:, PATCH:] for f in far)
        misfit = misfit - data[p].astype(f32)
        for m in range(modes):
            at = slice((p * modes + m) * PATCH, (p * modes + m + 1) * PATCH)
            stack[0:PATCH, at] = (misfit * far[m][:, :PATCH]).astype(bf16)
            stack[PATCH:, at] = (misfit * far[m][:, PATCH:]).astype(bf16)

    for p in range(patches):
        chi = transform(1, 0, p)
        o_re, o_im = windows[p]
        g_re = g_im = 0.0
        for m in range(modes):
            c_re, c_im = chi[m][:, :PATCH], chi[m][:, PATCH:]
            p_re, p_im = probe[m, 0], probe[m, 1]
            g_re += p_re * c_re + p_im * c_im
            g_im += p_re * c_im - p_im * c_re
            q_re, q_im = o_re * c_re + o_im * c_im, o_re * c_im - o_im * c_re
            if p == 0:
                probe_total[m, 0], probe_total[m, 1] = q_re, q_im
            else:
                probe_total[m, 0] += q_re
                probe_total[m, 1] += q_im
        top, down, start, shift = place(p)
        for c, g in enumerate((g_re, g_im)):
            turned = [pltpu.roll(g[:, k * BLK : (k + 1) * BLK], shift, 1) for k in range(spans)]
            none = jnp.zeros_like(turned[0])
            keep = lane >= shift
            for k in range(spans + 1):
                here = turned[k] if k < spans else none
                before = turned[k - 1] if k else none
                to = pl.ds(aligned(start + k * BLK, BLK), BLK)
                total[c, pl.ds(top, PATCH + 8), to] += rows_to(jnp.where(keep, here, before), down)

    out_block = pl.ds(col_in, BLK)
    width = cols + BLK
    for c in range(2):
        grad[c] = total[c, RIM:last, BLK : BLK + cols]
        for half, wide in ((sx, own), (1 - sx, to_x)):
            wide[c, :, 0:cols] = pick_strips(total, c, RIM, rows, inner, half, h)
            wide[c, :, cols:width] = pick_strips(total, c, RIM, rows, out_block, half, h)
        for half, wide in ((sx, to_y), (1 - sx, to_d)):
            wide[c, :, 0:cols] = pick_strips(total, c, row_in, RIM, inner, half, h)
            wide[c, :, cols:width] = pick_strips(total, c, row_in, RIM, out_block, half, h)
        rim_x[c] = own[c, :, cols:width]
        probe_keep[c] = probe_total[sx, c]
        probe_send[c] = probe_total[1 - sx, c].astype(bf16)


def project_kernel(
    h, group, own, from_x, from_y, from_d, weight, to_core, keep, *outs_and_scratch
):
    outs, (rows_all, chunks) = outs_and_scratch[:-2], outs_and_scratch[-2:]
    sy, sx, me = lax.axis_index("sy"), lax.axis_index("sx"), lax.axis_index("ang")
    f32, bf16 = jnp.float32, jnp.bfloat16
    rows = own.shape[1]
    cols = own.shape[2] - BLK
    rims = from_y.shape[1]
    count = rows // h
    mine, other = pl.ds(aligned(sx * cols, BLK), cols), pl.ds(aligned((1 - sx) * cols, BLK), cols)
    rim_mine = pl.ds(aligned(sx * (cols - BLK) + (1 - sx) * cols, BLK), BLK)
    rim_other = pl.ds(aligned(sx * cols + (1 - sx) * (cols - BLK), BLK), BLK)
    at = pl.ds(aligned((1 - sy) * (rows - rims), rims), rims)
    edge = pl.ds(aligned(sx * (cols - BLK), BLK), BLK)
    for c in range(2):
        rows_all[c, :, mine] = own[c, :, 0:cols].astype(f32)
        rows_all[c, :, other] = from_x[c, :, 0:cols].astype(f32)
        rows_all[c, :, rim_mine] += own[c, :, cols:].astype(f32)
        rows_all[c, :, rim_other] += from_x[c, :, cols:].astype(f32)
        rows_all[c, at, mine] += from_y[c, :, 0:cols].astype(f32)
        rows_all[c, at, other] += from_d[c, :, 0:cols].astype(f32)
        rows_all[c, at, rim_mine] += from_y[c, :, cols:].astype(f32)
        rows_all[c, at, rim_other] += from_d[c, :, cols:].astype(f32)
        to_core[c] = from_d[c, :, 0:cols]
        to_core[c, :, edge] = (from_d[c, :, edge].astype(f32) + from_y[c, :, cols:].astype(f32)).astype(bf16)
        part = jnp.dot(rows_all[c].astype(bf16), weight[...], preferred_element_type=f32)
        for j in range(count):
            chunks[j, c * h : (c + 1) * h, :] = part[j * h : (j + 1) * h]
    keep[...] = chunks[me]
    for d in range(1, group):
        outs[d - 1][...] = chunks[me ^ d].astype(bf16)
    for d in range(group):
        for k in range(1, count // group):
            piece = chunks[me ^ d ^ (k * group)]
            ref = outs[group - 1 + d]
            ref[(k - 1) * 2 * h : k * 2 * h, :] = piece.astype(ref.dtype)


def fold_kernel(h, grad, from_x, rim_x, from_y, from_d, from_core, out):
    sy, sx = lax.axis_index("sy"), lax.axis_index("sx")
    f32 = jnp.float32
    rows, cols = grad.shape[1], grad.shape[2]
    edge = pl.ds(aligned((1 - sx) * (cols - BLK), BLK), BLK)
    row = aligned((1 - sy) * (rows - RIM), RIM)
    every = pl.ds(0, cols)
    for c in range(2):
        out[c] = grad[c]
        add_strips(out, c, 0, rows, edge, sx, h, from_x[c, :, cols:].astype(f32))
        add_strips(out, c, 0, rows, edge, 1 - sx, h, rim_x[c].astype(f32))
        add_strips(out, c, row, RIM, every, sx, h, from_y[c, :, 0:cols].astype(f32))
        add_strips(out, c, row, RIM, edge, sx, h, from_d[c, :, cols:].astype(f32))
        add_strips(out, c, row, RIM, every, 1 - sx, h, from_core[c].astype(f32))


def far_kernel(count, *refs):
    out = refs[-1]
    total = refs[0][...]
    for ref in refs[1:-1]:
        total += ref[...].astype(jnp.float32)
    total = total.astype(out.dtype)
    out[...] = total


def last_kernel(h, *refs):
    out = refs[-1]
    total = refs[0][...]
    for ref in refs[1:-1]:
        total += ref[...].astype(jnp.float32)
    for c in range(2):
        out[:, c, :] = total[c * h : (c + 1) * h]


def probe_kernel(scale, mine, other, out):
    sx = lax.axis_index("sx")
    out[sx] = mine[...].astype(jnp.float32) * scale
    out[1 - sx] = other[...].astype(jnp.float32) * scale


def body(objects, probe, data, positions, block_index, block_values):
    f32, bf16 = jnp.float32, jnp.bfloat16
    obj, measured, pos = objects[0], data[0, 0, 0], positions[0, 0, 0]
    rows, cols = obj.shape[1], obj.shape[2]
    modes, patches = probe.shape[0], measured.shape[0]
    n = lax.axis_size("ang")
    tiles = lax.axis_size("sy") * lax.axis_size("sx")
    h = rows // (n * lax.axis_size("sx"))
    strip_rows = rows // 2
    lines = block_values.shape[0]
    width = lines * BLK
    group = 1
    while group * group < n:
        group *= 2

    to_y, to_x, to_d = call(
        edge_kernel,
        (shape((2, RIM, cols)), shape((2, rows, BLK)), shape((2, RIM, BLK))),
        (obj,), [VMEM], moved=2 * MIB,
    )
    halo_y = lax.ppermute(to_y, "sy", SWAP)
    halo_d = lax.ppermute(to_d, ("sy", "sx"), CROSS)
    halo_x = lax.ppermute(to_x, "sx", SWAP)

    entries = block_index.size // n
    weight = call(
        partial(weight_kernel, entries),
        shape((width, width)),
        (block_index, block_values, jnp.asarray(ramp_table(width))),
        [SMEM, VMEM, VMEM],
        [pltpu.VMEM((width, width), f32), pltpu.SMEM((entries,), jnp.int32)],
        flops=2 * entries * width * BLK * BLK * 4, moved=8 * MIB,
    )

    wide = cols + BLK
    grad, own, to_x, rim_x, to_y, to_d, probe_keep, probe_send = call(
        partial(patch_kernel, h),
        (
            shape((2, rows, cols), f32),
            shape((2, strip_rows, wide)),
            shape((2, strip_rows, wide)),
            shape((2, strip_rows, BLK)),
            shape((2, RIM // 2, wide)),
            shape((2, RIM // 2, wide)),
            shape((2, PATCH, PATCH), f32),
            shape((2, PATCH, PATCH)),
        ),
        (pos, obj, halo_y, halo_x, halo_d, probe, measured, jnp.asarray(dft_blocks(PATCH))),
        [SMEM] + [VMEM] * 7,
        [
            pltpu.VMEM((2, rows + 2 * RIM + 8, cols + 2 * BLK), f32),
            pltpu.VMEM((2, rows + 2 * RIM + 8, cols + 2 * BLK), f32),
            pltpu.VMEM((2 * PATCH, patches * modes * PATCH), bf16),
            pltpu.VMEM((modes, 2, PATCH, PATCH), f32),
        ],
        limit=48, flops=patches * modes * 32 * PATCH**3, moved=8 * MIB,
    )

    from_x = lax.ppermute(to_x, "sx", SWAP)
    from_y = lax.ppermute(to_y, "sy", SWAP)
    from_d = lax.ppermute(to_d, ("sy", "sx"), CROSS)
    from_rim = lax.ppermute(rim_x, "sx", SWAP)
    probe_x = lax.ppermute(probe_send, "sx", SWAP)
    probe_mine = (probe_keep + probe_x.astype(f32)).astype(bf16)
    probe_y = lax.ppermute(probe_mine, "sy", SWAP)
    probe_mine = (probe_mine.astype(f32) + probe_y.astype(f32)).astype(bf16)
    probe_other = lax.ppermute(probe_mine, "sx", SWAP)

    far = n // group - 1
    outs = call(
        partial(project_kernel, h, group),
        (shape((2, RIM // 2, cols)), shape((2 * h, width), f32))
        + (shape((2 * h, width)),) * (group - 1)
        + (shape((far * 2 * h, width), f32),)
        + (shape((far * 2 * h, width)),) * (group - 1),
        (own, from_x, from_y, from_d, weight),
        [VMEM] * 5,
        [pltpu.VMEM((2, strip_rows, width), f32), pltpu.VMEM((n, 2 * h, width), f32)],
        flops=4 * strip_rows * width * width, moved=8 * MIB,
    )
    to_core, keep, near, away = outs[0], outs[1], outs[2 : 1 + group], outs[1 + group :]

    def swap(array, d):
        return lax.ppermute(array, "ang", [(i, i ^ d) for i in range(n)])

    got = [swap(away[d], d) for d in range(group - 1, 0, -1)]
    near_got = [swap(near[d - 1], d) for d in range(group - 1, 0, -1)]
    across = call(
        partial(far_kernel, far), shape((far * 2 * h, width)), [away[0]] + got, [VMEM] * group,
        moved=MIB,
    )
    across_got = [swap(across[(k - 1) * 2 * h : k * 2 * h], k * group) for k in range(1, far + 1)]
    from_core = lax.ppermute(to_core, "sx", SWAP)
    object_grad = call(
        partial(fold_kernel, h),
        shape((2, rows, cols), f32),
        (grad, from_x, from_rim, from_y, from_d, from_core),
        [VMEM] * 6, moved=6 * MIB,
    )
    probe_grad = call(
        partial(probe_kernel, 1.0 / math.sqrt(patches * tiles)),
        shape((modes, 2, PATCH, PATCH), f32),
        (probe_mine, probe_other),
        [VMEM] * 2, moved=2 * MIB,
    )
    vol = call(
        partial(last_kernel, h),
        shape((h, 2, width), f32),
        [keep] + near_got + across_got,
        [VMEM] * (group + far), moved=MIB,
    )
    return (object_grad[None], probe_grad[None], vol[None])


def solution(mesh):
    placed = (
        P("ang", None, "sy", "sx"),
        P(),
        P("ang", "sy", "sx", None, None, None),
        P("ang", "sy", "sx", None, None),
        P(),
        P(),
    )
    return jax.shard_map(
        body,
        mesh=mesh,
        in_specs=placed,
        out_specs=(
            P("ang", None, "sy", "sx"),
            P("ang", None, None, None, None),
            P("sy", ("ang", "sx"), None, None),
        ),
        check_vma=False,
    )
```

time: 182 us -> 56 us (0.31)
  other arithmetic: 39.9 us -> 0.12 us
  local copies, waits for them, and re-layouts: 40.9 us -> 5.31 us
  waiting for transfers between devices: 45.7 us -> 11.7 us
  Pallas kernels: 0 us -> 20.7 us
  matrix products: 15.4 us -> 0 us
  between operations: 14.4 us -> 0.74 us
  starting transfers between devices: 24.6 us -> 17.2 us
    psum x1 -> x0, waiting for transfers between devices: 36 us -> none  [body(): lax.psum(probe_part.astype(jnp.bfloat16), ('sy', 'sx')).astype(jnp.float32)]
    pallas_call x0 -> x8, Pallas kernels: none -> 20.7 us  [call(): pl.pallas_call(kernel, out_shape=outs, in_specs=specs, out_specs=jax.tree...]
    scatter x10 -> x0, local copies, waits for them, and re-layouts: 18.5 us -> none
    dot_general x4 -> x0, matrix products: 15.4 us -> none  [the longest x2 8.37 us: right_product(): jnp.einsum('btrc,tcsq->bsrq', fields, matrix, preferred_element_type=jnp....]
    scatter x5 -> x0, other arithmetic: 14.6 us -> none
    another operation x8 -> x0, other arithmetic: 7.96 us -> none
    reduce_sum x3 -> x0, other arithmetic: 7.82 us -> none  [the longest x1 3.75 us: body(): running_sum = jnp.sum(jax.vmap(place_patch)(patch_grad, starts), axis=0)]
    gather x7 -> x0, local copies, waits for them, and re-layouts: 6.38 us -> none
  transfers between devices with their start and end apart: 10 -> 18, of which waited for: 4 -> 6; matrix products, arithmetic and copies ran while one was open for 8% -> 0% of each run, Pallas kernels for 0% -> 23%
where the time goes in v1:
time: 56 us; the launch traced here: 55.8 us
  Pallas kernels  20.7 us (37%)
  starting transfers between devices  17.2 us (31%)
  waiting for transfers between devices  11.7 us (21%)
  local copies, waits for them, and re-layouts  5.31 us (9%)
  between operations  0.74 us (1%)
    pallas_call x8, Pallas kernels, call(): pl.pallas_call(kernel, out_shape=outs, in_specs=specs, out_specs=jax.tree...  20.7 us
    ppermute x7, starting transfers between devices, swap(): return lax.ppermute(array, 'ang', [(i, i ^ d) for i in range(n)])  9.65 us
    ppermute x7, waiting for transfers between devices, swap(): return lax.ppermute(array, 'ang', [(i, i ^ d) for i in range(n)])  7.23 us
    unnamed x18, local copies, waits for them, and re-layouts  5.31 us
    ppermute x1, waiting for transfers between devices, body(): halo_d = lax.ppermute(to_d, ('sy', 'sx'), CROSS)  4.46 us
    ppermute x1, starting transfers between devices, body(): halo_y = lax.ppermute(to_y, 'sy', SWAP)  2.59 us
    ppermute x1, starting transfers between devices, body(): from_y = lax.ppermute(to_y, 'sy', SWAP)  1.66 us
    ppermute x1, starting transfers between devices, body(): probe_y = lax.ppermute(probe_mine, 'sy', SWAP)  1.59 us
  transfers between devices with their start and end apart: 18, of which 6 were waited for; matrix products, arithmetic and copies ran while one was open for 0% of the time, Pallas kernels for 23%

profile of v1, /device:TPU:0, one launch (start us, length us, event | category | flops | bytes accessed | tf_op | source)
XLA Modules:
  0.0 55.8 jit_solution(10394976936334225128)
XLA Ops:
  0.6 0.0 copy-start.3
  0.6 1.2 %copy-done.3 = bf16[1,2,512,512]{3,2,1,0:T(8,128)(2,1)S(1)} copy-done((bf16[1,2,512,512]{3,2,1,0:T(8,128)(2,1)S(1)}, bf16[1,2,512,512]{3,2,1,0:T(8,128)(2,1)}, u32[]{:S(2)}) %copy-start.3) | copy-done | bytes 1048600
  1.9 0.1 shard_map.103
  1.9 0.5 collective-permute-start.1
  2.4 2.6 %collective-permute-start = (bf16[2,64,512]{2,1,0:T(8,128)(2,1)S(1)}, bf16[2,64,512]{2,1,0:T(8,128)(2,1)S(1)}, u32[]{:S(2)}, u32[]{:S(2)}) collective-permute-start(bf16[2,64,512]{2,1,0:T(8,128)(2,1)S(1)} %get-tuple-element.23), channel_id=1, source_target_pairs={{0,2},{2,0},{1,3},{3,1},{4,6},{6,4},{5,7},{7,5},{8,10},{10,8},{9,1... | collective-permute-start | bytes 393224 | tf_op jit(solution)/shard_map/ppermute | solution.py:366
  5.0 0.1 collective-permute-start.2
  5.1 4.5 %collective-permute-done.2.from_d = bf16[2,64,128]{2,1,0:T(8,128)(2,1)S(1)} collective-permute-done((bf16[2,64,128]{2,1,0:T(8,128)(2,1)S(1)}, bf16[2,64,128]{2,1,0:T(8,128)(2,1)S(1)}, u32[]{:S(2)}, u32[]{:S(2)}) %collective-permute-start.2) | collective-permute-done | bytes 32800 | tf_op jit(solution)/shard_map/ppermute | solution.py:367
  9.6 0.0 collective-permute-done.from_y
  9.6 0.0 collective-permute-done.1.from_x
  9.6 1.2 %copy-done.4 = bf16[1,2,512,512]{3,2,1,0:T(8,128)(2,1)S(1)} copy-done((bf16[1,2,512,512]{3,2,1,0:T(8,128)(2,1)S(1)}, bf16[1,2,512,512]{3,2,1,0:T(8,128)(2,1)}, u32[]{:S(2)}) %copy-start.4) | copy-done | bytes 1048600
  10.8 1.2 %copy-done.6 = f32[2,2,256,256]{3,2,1,0:T(8,128)S(1)} copy-done((f32[2,2,256,256]{3,2,1,0:T(8,128)S(1)}, f32[2,2,256,256]{3,2,1,0:T(8,128)}, u32[]{:S(2)}) %copy-start.6) | copy-done | bytes 1048600
  12.0 0.9 %copy-done.7 = bf16[1,1,1,2,256,256]{5,4,3,2,1,0:T(8,128)(2,1)S(1)} copy-done((bf16[1,1,1,2,256,256]{5,4,3,2,1,0:T(8,128)(2,1)S(1)}, bf16[1,1,1,2,256,256]{5,4,3,2,1,0:T(8,128)(2,1)}, u32[]{:S(2)}) %copy-start.7) | copy-done | bytes 262168
  13.0 0.7 %copy-done.8 = s32[1,1,1,2,2]{4,3,2,1,0:T(2,128)S(1)} copy-done((s32[1,1,1,2,2]{4,3,2,1,0:T(2,128)S(1)}, s32[1,1,1,2,2]{4,3,2,1,0:T(2,128)}, u32[]{:S(2)}) %copy-start.8) | copy-done | bytes 40
  13.7 7.1 %shard_map.104 = (f32[2,512,512]{2,1,0:T(8,128)}, bf16[2,256,640]{2,1,0:T(8,128)(2,1)S(1)}, bf16[2,256,640]{2,1,0:T(8,128)(2,1)S(1)}, bf16[2,256,128]{2,1,0:T(8,...) custom-call(s32[2,2]{1,0:T(2,128)S(1)} %bitcast.9, ...), custom_call_target="tpu_custom_call" | custom-call | flops 2147483648 | bytes 8388608 | tf_op jit(solution)/shard_map/pallas_call | solution.py:49
  20.7 0.1 collective-permute-start.8
  20.8 0.4 collective-permute-start.3
  21.2 1.7 %collective-permute-start.5 = (bf16[2,32,640]{2,1,0:T(8,128)(2,1)S(1)}, bf16[2,32,640]{2,1,0:T(8,128)(2,1)S(1)}, u32[]{:S(2)}, u32[]{:S(2)}) collective-permute-start(bf16[2,32,640]{2,1,0:T(8,128)(2,1)S(1)} %get-tuple-element.29), channel_id=1, source_target_pairs={{0,2},{2,0},{1,3},{3,1},{4,6},{6,4},{5,7},{7,5},{8,10},{10,8},{9,1... | collective-permute-start | bytes 245768 | tf_op jit(solution)/shard_map/ppermute | solution.py:405
  22.9 0.0 collective-permute-start.6
  22.9 0.1 add_convert_fusion.1
  23.0 1.6 %collective-permute-start.9 = (bf16[2,256,256]{2,1,0:T(8,128)(2,1)S(1)}, bf16[2,256,256]{2,1,0:T(8,128)(2,1)S(1)}, u32[]{:S(2)}, u32[]{:S(2)}) collective-permute-start(bf16[2,256,256]{2,1,0:T(8,128)(2,1)S(1)} %add_convert_fusion.1), channel_id=1, source_target_pairs={{0,2},{2,0},{1,3},{3,1},{4,6},{6,4},{5,7},{7,5},{8,10},{10,8},{9,1... | collective-permute-start | bytes 786440 | tf_op jit(solution)/shard_map/ppermute | solution.py:410
  24.6 8.2 %shard_map.105.weight = bf16[1024,1024]{1,0:T(8,128)(2,1)S(1)} custom-call(s32[8,16]{1,0:T(8,128)S(1)} %copy-done.5, bf16[8,16,128,128]{3,2,1,0:T(8,128)(2,1)S(1)} %copy-done, bf16[1024,1024]{1,0:T(8,128)(2,1)S(1)} %copy-done.2), custom_call_target="tpu_custom_call" | custom-call | flops 2147483648 | bytes 8388608 | tf_op jit(solution)/shard_map/pallas_call | solution.py:49
  32.8 0.0 collective-permute-done.3.from_x
  32.8 0.0 copy-start.1
  32.9 1.7 %shard_map.106 = (bf16[2,32,512]{2,1,0:T(8,128)(2,1)S(1)}, f32[64,1024]{1,0:T(8,128)S(1)}, bf16[64,1024]{1,0:T(8,128)(2,1)S(1)}, bf16[64,1024]{1,0:T(8,128)(2,1)...) custom-call(bf16[2,256,640]{2,1,0:T(8,128)(2,1)S(1)} %get-tuple-elem, ...), custom_call_target="tpu_custom_call" | custom-call | flops 1073741824 | bytes 8388608 | tf_op jit(solution)/shard_map/pallas_call | solution.py:49
  34.6 2.6 %collective-permute-start.14 = (bf16[64,1024]{1,0:T(8,128)(2,1)S(1)}, bf16[64,1024]{1,0:T(8,128)(2,1)S(1)}, u32[]{:S(2)}, u32[]{:S(2)}) collective-permute-start(bf16[64,1024]{1,0:T(8,128)(2,1)S(1)} %get-tuple-element.40), channel_id=1, source_target_pairs={{0,12},{4,8},{8,4},{12,0},{16,28},{20,24},{24,20},{28,16},{1,13},{... | collective-permute-start | bytes 393224 | tf_op jit(solution)/shard_map/ppermute | solution.py:429
  37.2 0.4 collective-permute-start.15
  37.6 0.5 collective-permute-start.16
  38.1 0.0 collective-permute-done.9
  38.1 0.1 add_convert_fusion.mine
  38.2 0.1 collective-permute-start.10
  38.3 0.5 collective-permute-start.4
  38.8 3.1 %collective-permute-done.14.refs_1_ = bf16[64,1024]{1,0:T(8,128)(2,1)S(1)} collective-permute-done((bf16[64,1024]{1,0:T(8,128)(2,1)S(1)}, bf16[64,1024]{1,0:T(8,128)(2,1)S(1)}, u32[]{:S(2)}, u32[]{:S(2)}) %collective-permute-start.14) | collective-permute-done | bytes 131104 | tf_op jit(solution)/shard_map/ppermute | solution.py:429
  41.9 0.0 collective-permute-start.7
  41.9 2.3 %collective-permute-done.15.refs_2_ = bf16[64,1024]{1,0:T(8,128)(2,1)S(1)} collective-permute-done((bf16[64,1024]{1,0:T(8,128)(2,1)S(1)}, bf16[64,1024]{1,0:T(8,128)(2,1)S(1)}, u32[]{:S(2)}, u32[]{:S(2)}) %collective-permute-start.15) | collective-permute-done | bytes 131104 | tf_op jit(solution)/shard_map/ppermute | solution.py:429
  44.2 1.5 %collective-permute-start.11 = (bf16[64,1024]{1,0:T(8,128)(2,1)S(1)}, bf16[64,1024]{1,0:T(8,128)(2,1)S(1)}, u32[]{:S(2)}, u32[]{:S(2)}) collective-permute-start(bf16[64,1024]{1,0:T(8,128)(2,1)S(1)} %get-tuple-element.36), channel_id=1, source_target_pairs={{0,12},{4,8},{8,4},{12,0},{16,28},{20,24},{24,20},{28,16},{1,13},{... | collective-permute-start | bytes 393224 | tf_op jit(solution)/shard_map/ppermute | solution.py:429
  45.7 0.0 collective-permute-done.16.refs_3_
  45.7 0.4 collective-permute-start.12
  46.1 0.1 shard_map.109
  46.2 1.6 %collective-permute-start.13 = (bf16[64,1024]{1,0:T(8,128)(2,1)S(1)}, bf16[64,1024]{1,0:T(8,128)(2,1)S(1)}, u32[]{:S(2)}, u32[]{:S(2)}) collective-permute-start(bf16[64,1024]{1,0:T(8,128)(2,1)S(1)} %get-tuple-element.38), channel_id=1, source_target_pairs={{0,4},{4,0},{8,12},{12,8},{16,20},{20,16},{24,28},{28,24},{1,5},{5... | collective-permute-start | bytes 393224 | tf_op jit(solution)/shard_map/ppermute | solution.py:429
  47.8 0.0 collective-permute-done.7.from_core
  47.8 2.5 %collective-permute-start.17 = (bf16[64,1024]{1,0:T(8,128)(2,1)S(1)}, bf16[64,1024]{1,0:T(8,128)(2,1)S(1)}, u32[]{:S(2)}, u32[]{:S(2)}) collective-permute-start(bf16[64,1024]{1,0:T(8,128)(2,1)S(1)} %shard_map.109), channel_id=1, source_target_pairs={{0,16},{4,20},{8,24},{12,28},{16,0},{20,4},{24,8},{28,12},{1,17},{... | collective-permute-start | bytes 393224 | tf_op jit(solution)/shard_map/ppermute | solution.py:429
  50.3 1.7 %shard_map.107 = f32[2,512,512]{2,1,0:T(8,128)} custom-call(f32[2,512,512]{2,1,0:T(8,128)S(1)} %copy-done.1, bf16[2,256,640]{2,1,0:T(8,128)(2,1)S(1)} %collective-permute-done.3.from_x, bf16[2,256,128]{2,1,0:T(8,128)(2,1)S(1)} %collective-permute-done.4.rim_x, bf16[2,32,640]{2,1,0:T(8,128)(2,1)S(1)} %collective-permute-done.5.from_y, ...), custom_call_target="tpu_custom_call" | custom-call | bytes 6291456 | tf_op jit(solution)/shard_map/pallas_call | solution.py:49
  52.0 1.1 %shard_map.108 = f32[2,2,256,256]{3,2,1,0:T(8,128)} custom-call(bf16[2,256,256]{2,1,0:T(8,128)(2,1)S(1)} %add_convert_fusion.mine, bf16[2,256,256]{2,1,0:T(8,128)(2,1)S(1)} %collective-permute-done.10.other), custom_call_target="tpu_custom_call" | custom-call | bytes 2097152 | tf_op jit(solution)/shard_map/pallas_call | solution.py:49
  53.1 1.2 %collective-permute-done.11.refs_1_ = bf16[64,1024]{1,0:T(8,128)(2,1)S(1)} collective-permute-done((bf16[64,1024]{1,0:T(8,128)(2,1)S(1)}, bf16[64,1024]{1,0:T(8,128)(2,1)S(1)}, u32[]{:S(2)}, u32[]{:S(2)}) %collective-permute-start.11) | collective-permute-done | bytes 131104 | tf_op jit(solution)/shard_map/ppermute | solution.py:429
  54.2 0.1 collective-permute-done.12.refs_2_
  54.4 0.0 collective-permute-done.13.refs_3_
  54.4 0.6 %collective-permute-done.17.refs_4_ = bf16[64,1024]{1,0:T(8,128)(2,1)S(1)} collective-permute-done((bf16[64,1024]{1,0:T(8,128)(2,1)S(1)}, bf16[64,1024]{1,0:T(8,128)(2,1)S(1)}, u32[]{:S(2)}, u32[]{:S(2)}) %collective-permute-start.17) | collective-permute-done | bytes 131104 | tf_op jit(solution)/shard_map/ppermute | solution.py:429
  54.9 0.8 %shard_map.110 = f32[32,2,1024]{2,1,0:T(2,128)} custom-call(f32[64,1024]{1,0:T(8,128)S(1)} %get-tuple-element.35.refs_0_, bf16[64,1024]{1,0:T(8,128)(2,1)S(1)} %collective-permute-done.11.refs_1_, bf16[64,1024]{1,0:T(8,128)(2,1)S(1)} %collective-permute-done.12.refs_2_, bf16[64,1024]{1,0:T(8,128)(2,1)S(1)} %collective-permute-done.13.refs_3_, ...), custom_call_target="tpu_custom_call" | custom-call | bytes 1048576 | tf_op jit(solution)/shard_map/pallas_call | solution.py:49
  (16 shorter events, 0.0 us)
Async XLA Ops:
  0.6 1.2 %copy-start.3 = (bf16[1,2,512,512]{3,2,1,0:T(8,128)(2,1)S(1)}, bf16[1,2,512,512]{3,2,1,0:T(8,128)(2,1)}, u32[]{:S(2)}) copy-start(bf16[1,2,512,512]{3,2,1,0:T(8,128)(2,1)} %param.8) | copy-start | bytes 3145732
  1.9 7.6 %collective-permute-start.1 = (bf16[2,512,128]{2,1,0:T(8,128)(2,1)S(1)}, bf16[2,512,128]{2,1,0:T(8,128)(2,1)S(1)}, u32[]{:S(2)}, u32[]{:S(2)}) collective-permute-start(bf16[2,512,128]{2,1,0:T(8,128)(2,1)S(1)} %get-tuple-element.24), channel_id=1, source_target_pairs={{0,1},{1,0},{2,3},{3,2},{4,5},{5,4},{6,7},{7,6},{8,9},{9,8},{10,11... | collective-permute-start | bytes 786440 | tf_op jit(solution)/shard_map/ppermute | solution.py:368
  2.4 7.1 %collective-permute-start = (bf16[2,64,512]{2,1,0:T(8,128)(2,1)S(1)}, bf16[2,64,512]{2,1,0:T(8,128)(2,1)S(1)}, u32[]{:S(2)}, u32[]{:S(2)}) collective-permute-start(bf16[2,64,512]{2,1,0:T(8,128)(2,1)S(1)} %get-tuple-element.23), channel_id=1, source_target_pairs={{0,2},{2,0},{1,3},{3,1},{4,6},{6,4},{5,7},{7,5},{8,10},{10,8},{9,1... | collective-permute-start | bytes 393224 | tf_op jit(solution)/shard_map/ppermute | solution.py:366
  5.0 4.5 %collective-permute-start.2 = (bf16[2,64,128]{2,1,0:T(8,128)(2,1)S(1)}, bf16[2,64,128]{2,1,0:T(8,128)(2,1)S(1)}, u32[]{:S(2)}, u32[]{:S(2)}) collective-permute-start(bf16[2,64,128]{2,1,0:T(8,128)(2,1)S(1)} %get-tuple-element.25), channel_id=1, source_target_pairs={{0,3},{3,0},{1,2},{2,1},{4,7},{7,4},{5,6},{6,5},{8,11},{11,8},{9,1... | collective-permute-start | bytes 98312 | tf_op jit(solution)/shard_map/ppermute | solution.py:367
  9.6 1.2 %copy-start.4 = (bf16[1,2,512,512]{3,2,1,0:T(8,128)(2,1)S(1)}, bf16[1,2,512,512]{3,2,1,0:T(8,128)(2,1)}, u32[]{:S(2)}) copy-start(bf16[1,2,512,512]{3,2,1,0:T(8,128)(2,1)} %param.8) | copy-start | bytes 3145732
  10.8 1.2 %copy-start.6 = (f32[2,2,256,256]{3,2,1,0:T(8,128)S(1)}, f32[2,2,256,256]{3,2,1,0:T(8,128)}, u32[]{:S(2)}) copy-start(f32[2,2,256,256]{3,2,1,0:T(8,128)} %probe.1) | copy-start | bytes 3145732
  12.0 0.9 %copy-start.7 = (bf16[1,1,1,2,256,256]{5,4,3,2,1,0:T(8,128)(2,1)S(1)}, bf16[1,1,1,2,256,256]{5,4,3,2,1,0:T(8,128)(2,1)}, u32[]{:S(2)}) copy-start(bf16[1,1,1,2,256,256]{5,4,3,2,1,0:T(8,128)(2,1)} %param.10) | copy-start | bytes 786436
  13.0 0.7 %copy-start.8 = (s32[1,1,1,2,2]{4,3,2,1,0:T(2,128)S(1)}, s32[1,1,1,2,2]{4,3,2,1,0:T(2,128)}, u32[]{:S(2)}) copy-start(s32[1,1,1,2,2]{4,3,2,1,0:T(2,128)} %param.11) | copy-start | bytes 52
  13.7 10.9 %copy-start = (bf16[8,16,128,128]{3,2,1,0:T(8,128)(2,1)S(1)}, bf16[8,16,128,128]{3,2,1,0:T(8,128)(2,1)}, u32[]{:S(2)}) copy-start(bf16[8,16,128,128]{3,2,1,0:T(8,128)(2,1)} %values.1) | copy-start | bytes 12582916
  13.7 10.9 %copy-start.2 = (bf16[1024,1024]{1,0:T(8,128)(2,1)S(1)}, bf16[1024,1024]{1,0:T(8,128)(2,1)}, u32[]{:S(2)}) copy-start(bf16[1024,1024]{1,0:T(8,128)(2,1)} %constant.4.clone.ramp) | copy-start | bytes 6291460
  13.7 10.9 %copy-start.5 = (s32[8,16]{1,0:T(8,128)S(1)}, s32[8,16]{1,0:T(8,128)}, u32[]{:S(2)}) copy-start(s32[8,16]{1,0:T(8,128)} %index.1) | copy-start | bytes 1540
  20.7 2.2 %collective-permute-start.8 = (bf16[2,256,256]{2,1,0:T(8,128)(2,1)S(1)}, bf16[2,256,256]{2,1,0:T(8,128)(2,1)S(1)}, u32[]{:S(2)}, u32[]{:S(2)}) collective-permute-start(bf16[2,256,256]{2,1,0:T(8,128)(2,1)S(1)} %get-tuple-element.34), channel_id=1, source_target_pairs={{0,1},{1,0},{2,3},{3,2},{4,5},{5,4},{6,7},{7,6},{8,9},{9,8},{10,11... | collective-permute-start | bytes 786440 | tf_op jit(solution)/shard_map/ppermute | solution.py:408
  20.8 12.0 %collective-permute-start.3 = (bf16[2,256,640]{2,1,0:T(8,128)(2,1)S(1)}, bf16[2,256,640]{2,1,0:T(8,128)(2,1)S(1)}, u32[]{:S(2)}, u32[]{:S(2)}) collective-permute-start(bf16[2,256,640]{2,1,0:T(8,128)(2,1)S(1)} %get-tuple-element.27), channel_id=1, source_target_pairs={{0,1},{1,0},{2,3},{3,2},{4,5},{5,4},{6,7},{7,6},{8,9},{9,8},{10,11... | collective-permute-start | bytes 1966088 | tf_op jit(solution)/shard_map/ppermute | solution.py:404
  21.2 11.6 %collective-permute-start.5 = (bf16[2,32,640]{2,1,0:T(8,128)(2,1)S(1)}, bf16[2,32,640]{2,1,0:T(8,128)(2,1)S(1)}, u32[]{:S(2)}, u32[]{:S(2)}) collective-permute-start(bf16[2,32,640]{2,1,0:T(8,128)(2,1)S(1)} %get-tuple-element.29), channel_id=1, source_target_pairs={{0,2},{2,0},{1,3},{3,1},{4,6},{6,4},{5,7},{7,5},{8,10},{10,8},{9,1... | collective-permute-start | bytes 245768 | tf_op jit(solution)/shard_map/ppermute | solution.py:405
  22.9 9.9 %collective-permute-start.6 = (bf16[2,32,640]{2,1,0:T(8,128)(2,1)S(1)}, bf16[2,32,640]{2,1,0:T(8,128)(2,1)S(1)}, u32[]{:S(2)}, u32[]{:S(2)}) collective-permute-start(bf16[2,32,640]{2,1,0:T(8,128)(2,1)S(1)} %get-tuple-element.30), channel_id=1, source_target_pairs={{0,3},{3,0},{1,2},{2,1},{4,7},{7,4},{5,6},{6,5},{8,11},{11,8},{9,1... | collective-permute-start | bytes 245768 | tf_op jit(solution)/shard_map/ppermute | solution.py:406
  23.0 15.2 %collective-permute-start.9 = (bf16[2,256,256]{2,1,0:T(8,128)(2,1)S(1)}, bf16[2,256,256]{2,1,0:T(8,128)(2,1)S(1)}, u32[]{:S(2)}, u32[]{:S(2)}) collective-permute-start(bf16[2,256,256]{2,1,0:T(8,128)(2,1)S(1)} %add_convert_fusion.1), channel_id=1, source_target_pairs={{0,2},{2,0},{1,3},{3,1},{4,6},{6,4},{5,7},{7,5},{8,10},{10,8},{9,1... | collective-permute-start | bytes 786440 | tf_op jit(solution)/shard_map/ppermute | solution.py:410
  32.8 17.5 %copy-start.1 = (f32[2,512,512]{2,1,0:T(8,128)S(1)}, f32[2,512,512]{2,1,0:T(8,128)}, u32[]{:S(2)}) copy-start(f32[2,512,512]{2,1,0:T(8,128)} %get-tuple-element.26.grad) | copy-start | bytes 6291460
  34.6 7.3 %collective-permute-start.14 = (bf16[64,1024]{1,0:T(8,128)(2,1)S(1)}, bf16[64,1024]{1,0:T(8,128)(2,1)S(1)}, u32[]{:S(2)}, u32[]{:S(2)}) collective-permute-start(bf16[64,1024]{1,0:T(8,128)(2,1)S(1)} %get-tuple-element.40), channel_id=1, source_target_pairs={{0,12},{4,8},{8,4},{12,0},{16,28},{20,24},{24,20},{28,16},{1,13},{... | collective-permute-start | bytes 393224 | tf_op jit(solution)/shard_map/ppermute | solution.py:429
  37.2 7.0 %collective-permute-start.15 = (bf16[64,1024]{1,0:T(8,128)(2,1)S(1)}, bf16[64,1024]{1,0:T(8,128)(2,1)S(1)}, u32[]{:S(2)}, u32[]{:S(2)}) collective-permute-start(bf16[64,1024]{1,0:T(8,128)(2,1)S(1)} %get-tuple-element.41), channel_id=1, source_target_pairs={{0,8},{4,12},{8,0},{12,4},{16,24},{20,28},{24,16},{28,20},{1,9},{5... | collective-permute-start | bytes 393224 | tf_op jit(solution)/shard_map/ppermute | solution.py:429
  37.6 8.1 %collective-permute-start.16 = (bf16[64,1024]{1,0:T(8,128)(2,1)S(1)}, bf16[64,1024]{1,0:T(8,128)(2,1)S(1)}, u32[]{:S(2)}, u32[]{:S(2)}) collective-permute-start(bf16[64,1024]{1,0:T(8,128)(2,1)S(1)} %get-tuple-element.42), channel_id=1, source_target_pairs={{0,4},{4,0},{8,12},{12,8},{16,20},{20,16},{24,28},{28,24},{1,5},{5... | collective-permute-start | bytes 393224 | tf_op jit(solution)/shard_map/ppermute | solution.py:429
  38.2 13.8 %collective-permute-start.10 = (bf16[2,256,256]{2,1,0:T(8,128)(2,1)S(1)}, bf16[2,256,256]{2,1,0:T(8,128)(2,1)S(1)}, u32[]{:S(2)}, u32[]{:S(2)}) collective-permute-start(bf16[2,256,256]{2,1,0:T(8,128)(2,1)S(1)} %add_convert_fusion.mine), channel_id=1, source_target_pairs={{0,1},{1,0},{2,3},{3,2},{4,5},{5,4},{6,7},{7,6},{8,9},{9,8},{10,11... | collective-permute-start | bytes 786440 | tf_op jit(solution)/shard_map/ppermute | solution.py:412
  38.3 7.9 %collective-permute-start.4 = (bf16[2,256,128]{2,1,0:T(8,128)(2,1)S(1)}, bf16[2,256,128]{2,1,0:T(8,128)(2,1)S(1)}, u32[]{:S(2)}, u32[]{:S(2)}) collective-permute-start(bf16[2,256,128]{2,1,0:T(8,128)(2,1)S(1)} %get-tuple-element.28), channel_id=1, source_target_pairs={{0,1},{1,0},{2,3},{3,2},{4,5},{5,4},{6,7},{7,6},{8,9},{9,8},{10,11... | collective-permute-start | bytes 393224 | tf_op jit(solution)/shard_map/ppermute | solution.py:407
  41.9 5.9 %collective-permute-start.7 = (bf16[2,32,512]{2,1,0:T(8,128)(2,1)S(1)}, bf16[2,32,512]{2,1,0:T(8,128)(2,1)S(1)}, u32[]{:S(2)}, u32[]{:S(2)}) collective-permute-start(bf16[2,32,512]{2,1,0:T(8,128)(2,1)S(1)} %get-tuple-element.32), channel_id=1, source_target_pairs={{0,1},{1,0},{2,3},{3,2},{4,5},{5,4},{6,7},{7,6},{8,9},{9,8},{10,11... | collective-permute-start | bytes 196616 | tf_op jit(solution)/shard_map/ppermute | solution.py:438
  44.2 10.1 %collective-permute-start.11 = (bf16[64,1024]{1,0:T(8,128)(2,1)S(1)}, bf16[64,1024]{1,0:T(8,128)(2,1)S(1)}, u32[]{:S(2)}, u32[]{:S(2)}) collective-permute-start(bf16[64,1024]{1,0:T(8,128)(2,1)S(1)} %get-tuple-element.36), channel_id=1, source_target_pairs={{0,12},{4,8},{8,4},{12,0},{16,28},{20,24},{24,20},{28,16},{1,13},{... | collective-permute-start | bytes 393224 | tf_op jit(solution)/shard_map/ppermute | solution.py:429
  45.7 8.7 %collective-permute-start.12 = (bf16[64,1024]{1,0:T(8,128)(2,1)S(1)}, bf16[64,1024]{1,0:T(8,128)(2,1)S(1)}, u32[]{:S(2)}, u32[]{:S(2)}) collective-permute-start(bf16[64,1024]{1,0:T(8,128)(2,1)S(1)} %get-tuple-element.37), channel_id=1, source_target_pairs={{0,8},{4,12},{8,0},{12,4},{16,24},{20,28},{24,16},{28,20},{1,9},{5... | collective-permute-start | bytes 393224 | tf_op jit(solution)/shard_map/ppermute | solution.py:429
  46.2 8.2 %collective-permute-start.13 = (bf16[64,1024]{1,0:T(8,128)(2,1)S(1)}, bf16[64,1024]{1,0:T(8,128)(2,1)S(1)}, u32[]{:S(2)}, u32[]{:S(2)}) collective-permute-start(bf16[64,1024]{1,0:T(8,128)(2,1)S(1)} %get-tuple-element.38), channel_id=1, source_target_pairs={{0,4},{4,0},{8,12},{12,8},{16,20},{20,16},{24,28},{28,24},{1,5},{5... | collective-permute-start | bytes 393224 | tf_op jit(solution)/shard_map/ppermute | solution.py:429
  47.8 7.1 %collective-permute-start.17 = (bf16[64,1024]{1,0:T(8,128)(2,1)S(1)}, bf16[64,1024]{1,0:T(8,128)(2,1)S(1)}, u32[]{:S(2)}, u32[]{:S(2)}) collective-permute-start(bf16[64,1024]{1,0:T(8,128)(2,1)S(1)} %shard_map.109), channel_id=1, source_target_pairs={{0,16},{4,20},{8,24},{12,28},{16,0},{20,4},{24,8},{28,12},{1,17},{... | collective-permute-start | bytes 393224 | tf_op jit(solution)/shard_map/ppermute | solution.py:429

commit v2 on v1

--- a/solution.py
+++ b/solution.py
@@ -19,7 +19,8 @@
 
 VMEM = pl.BlockSpec(memory_space=pltpu.VMEM)
 SMEM = pl.BlockSpec(memory_space=pltpu.SMEM)
-HBM = pl.BlockSpec(memory_space=pl.ANY)
+ANY = pl.BlockSpec(memory_space=pl.ANY)
+HBM = pl.BlockSpec(memory_space=pltpu.HBM)
 
 
 def dft_blocks(length):
@@ -32,9 +33,8 @@
     return np.stack([forward, backward]).astype(np.float32).astype(ml_dtypes.bfloat16)
 
 
-def ramp_table(width):
-    ids = np.arange(width)
-    offsets = ids[None, :] - ids[:, None]
+def ramp_strip(width):
+    offsets = np.arange(2 * width - BLK)[None, :] - (width - BLK) - np.arange(BLK)[:, None]
     scaled = offsets.astype(np.float64) * math.pi
     values = np.where(offsets % 2 != 0, -1.0 / np.maximum(scaled * scaled, 1.0), 0.0)
     values = np.where(offsets == 0, 0.25, values)
@@ -45,7 +45,11 @@
     return jax.ShapeDtypeStruct(dims, dtype)
 
 
-def call(kernel, outs, ins, specs, scratch=(), limit=32, flops=0, moved=0):
+def call(kernel, outs, ins, specs, scratch=(), limit=16, flops=0, moved=0):
+    ins = [
+        pltpu.with_memory_space_constraint(x, pltpu.HBM) if spec is HBM else x
+        for x, spec in zip(ins, specs, strict=True)
+    ]
     return pl.pallas_call(
         kernel,
         out_shape=outs,
@@ -61,44 +65,72 @@
     return pl.multiple_of(value, step)
 
 
-def edge_kernel(obj, to_y, to_x, to_d):
+def edge_kernel(obj, to_y, to_x, to_d, sems):
     sy, sx = lax.axis_index("sy"), lax.axis_index("sx")
     rows, cols = obj.shape[1], obj.shape[2]
-    r = aligned((1 - sy) * (rows - RIM), RIM)
-    c = aligned((1 - sx) * (cols - BLK), BLK)
-    to_y[...] = obj[:, pl.ds(r, RIM), :]
-    to_x[...] = obj[:, :, pl.ds(c, BLK)]
-    to_d[...] = obj[:, pl.ds(r, RIM), pl.ds(c, BLK)]
-
-
-def weight_kernel(count, index, values, ramp, out, total, found):
+    r = pl.ds(aligned((1 - sy) * (rows - RIM), RIM), RIM)
+    c = pl.ds(aligned((1 - sx) * (cols - BLK), BLK), BLK)
+    copies = [
+        pltpu.make_async_copy(obj.at[:, r, :], to_y, sems.at[0]),
+        pltpu.make_async_copy(obj.at[:, r, c], to_d, sems.at[1]),
+        pltpu.make_async_copy(obj.at[:, :, c], to_x, sems.at[2]),
+    ]
+    for copy in copies:
+        copy.start()
+    for copy in copies:
+        copy.wait()
+
+
+def gather_kernel(count, index, values, out, blocks, sums, index_here, found, slots, sems):
     me = lax.axis_index("ang")
     lines, per = index.shape
-    total[...] = jnp.zeros_like(total)
-
-    def scan(e, n):
-        hit = index[e // per, e % per] // lines == me
-
-        @pl.when(hit & (n < count))
-        def _():
-            found[n] = e
-
-        return n + hit.astype(jnp.int32)
-
-    lax.fori_loop(0, lines * per, scan, jnp.int32(0))
-
-    def add(i, carry):
+    first = pltpu.make_async_copy(index, index_here, sems.at[count])
+    first.start()
+    out[...] = jnp.zeros_like(out)
+    for i in range(lines * lines):
+        slots[i] = jnp.int32(count)
+    first.wait()
+    low, high = me * lines, (me + 1) * lines
+    n = jnp.int32(0)
+    for b in range(lines):
+        for k in range(per):
+            g = index_here[b, k]
+            found[n] = jnp.int32(b * per + k)
+            n = jnp.minimum(n + ((g >= low) & (g < high)).astype(jnp.int32), count)
+    copies, places = [], []
+    for i in range(count):
         e = found[i]
-        b, k = e // per, e % per
-        col = aligned(index[b, k] % lines * BLK, BLK)
-        to = aligned(b * BLK, BLK)
-        total[:, pl.ds(to, BLK)] += jnp.dot(
-            ramp[:, pl.ds(col, BLK)], values[b, k], preferred_element_type=jnp.float32
-        )
-        return carry
-
-    lax.fori_loop(0, count, add, 0)
-    out[...] = total[...].astype(out.dtype)
+        b, k = lax.div(e, per), lax.rem(e, per)
+        copies.append(pltpu.make_async_copy(values.at[b, k], blocks.at[i], sems.at[i]))
+        copies[i].start()
+        places.append((index_here[b, k] - low, b))
+    for copy in copies:
+        copy.wait()
+    for i, (line, b) in enumerate(places):
+        place = line * lines + b
+        slot = jnp.minimum(slots[place], i)
+        value = blocks[i].astype(jnp.float32)
+        sums[slot] = jnp.where(slot < i, sums[slot] + value, value)
+        slots[place] = slot
+        row, col = pl.ds(aligned(line * BLK, BLK), BLK), pl.ds(aligned(b * BLK, BLK), BLK)
+        out[row, col] = sums[slot].astype(out.dtype)
+
+
+def weight_kernel(matrix, strip, *refs):
+    steps = (len(refs) - 2) // 2
+    sources, out, targets, sems = refs[:steps], refs[steps], refs[steps + 1 : -1], refs[-1]
+    moves = [
+        pltpu.make_async_copy(source, target, sems.at[i])
+        for i, (source, target) in enumerate(zip(sources, targets, strict=True))
+    ]
+    for move in moves:
+        move.start()
+    width = out.shape[0]
+    starts = range(width - BLK, -1, -BLK)
+    ramp = jnp.concatenate([strip[:, start : start + width] for start in starts], axis=0)
+    out[...] = jnp.dot(ramp, matrix[...], preferred_element_type=jnp.float32).astype(out.dtype)
+    for move in moves:
+        move.wait()
 
 
 def strip_select(half, rows, h, dtype):
@@ -151,10 +183,12 @@
 
 
 def patch_kernel(
-    h, pos, obj, from_y, from_x, from_d, probe, data, dft,
-    grad, own, to_x, rim_x, to_y, to_d, probe_keep, probe_send,
-    frame, total, stack, probe_total,
+    h, pos, ahead, obj, from_y, from_x, from_d, probe, data, dft,
+    grad, own, to_x, rim_x, to_y, to_d, probe_send,
+    frame, total, stack, probe_total, spots, sem,
 ):
+    fetch = pltpu.make_async_copy(pos, spots, sem)
+    fetch.start()
     sy, sx = lax.axis_index("sy"), lax.axis_index("sx")
     rows, cols = obj.shape[1], obj.shape[2]
     modes = probe.shape[0]
@@ -176,9 +210,10 @@
     total[...] = jnp.zeros_like(total)
     lane = lax.broadcasted_iota(jnp.int32, (PATCH, BLK), 1)
     spans = PATCH // BLK
+    fetch.wait()
 
     def place(p):
-        u, v = pos[p, 0], pos[p, 1] + (BLK - RIM)
+        u, v = spots[p, 0], spots[p, 1] + (BLK - RIM)
         start = aligned(v // BLK * BLK, BLK)
         top = aligned(u // 8 * 8, 8)
         return top, u - top, start, v - start
@@ -260,47 +295,70 @@
             wide[c, :, 0:cols] = pick_strips(total, c, row_in, RIM, inner, half, h)
             wide[c, :, cols:width] = pick_strips(total, c, row_in, RIM, out_block, half, h)
         rim_x[c] = own[c, :, cols:width]
-        probe_keep[c] = probe_total[sx, c]
-        probe_send[c] = probe_total[1 - sx, c].astype(bf16)
-
-
-def project_kernel(
-    h, group, own, from_x, from_y, from_d, weight, to_core, keep, *outs_and_scratch
-):
-    outs, (rows_all, chunks) = outs_and_scratch[:-2], outs_and_scratch[-2:]
-    sy, sx, me = lax.axis_index("sy"), lax.axis_index("sx"), lax.axis_index("ang")
+    probe_send[...] = probe_total[...].astype(bf16)
+
+
+def column_cuts(sx, cols):
+    low, high = aligned(sx * cols, BLK), aligned((1 - sx) * cols, BLK)
+    edge = cols - BLK
+    mine = pl.ds(aligned(sx * edge + (1 - sx) * cols, BLK), BLK)
+    other = pl.ds(aligned(sx * cols + (1 - sx) * edge, BLK), BLK)
+    return pl.ds(low, cols), pl.ds(high, cols), mine, other
+
+
+def project_kernel(h, own, from_x, weight, chunks, rows_all):
+    sx = lax.axis_index("sx")
     f32, bf16 = jnp.float32, jnp.bfloat16
-    rows = own.shape[1]
     cols = own.shape[2] - BLK
-    rims = from_y.shape[1]
-    count = rows // h
-    mine, other = pl.ds(aligned(sx * cols, BLK), cols), pl.ds(aligned((1 - sx) * cols, BLK), cols)
-    rim_mine = pl.ds(aligned(sx * (cols - BLK) + (1 - sx) * cols, BLK), BLK)
-    rim_other = pl.ds(aligned(sx * cols + (1 - sx) * (cols - BLK), BLK), BLK)
-    at = pl.ds(aligned((1 - sy) * (rows - rims), rims), rims)
-    edge = pl.ds(aligned(sx * (cols - BLK), BLK), BLK)
+    count = own.shape[1] // h
+    mine, other, rim_mine, rim_other = column_cuts(sx, cols)
     for c in range(2):
         rows_all[c, :, mine] = own[c, :, 0:cols].astype(f32)
         rows_all[c, :, other] = from_x[c, :, 0:cols].astype(f32)
         rows_all[c, :, rim_mine] += own[c, :, cols:].astype(f32)
         rows_all[c, :, rim_other] += from_x[c, :, cols:].astype(f32)
-        rows_all[c, at, mine] += from_y[c, :, 0:cols].astype(f32)
-        rows_all[c, at, other] += from_d[c, :, 0:cols].astype(f32)
-        rows_all[c, at, rim_mine] += from_y[c, :, cols:].astype(f32)
-        rows_all[c, at, rim_other] += from_d[c, :, cols:].astype(f32)
+        rows = rows_all[c].astype(bf16)
+        part = jnp.dot(rows, weight[...], preferred_element_type=f32)
+        for j in range(count):
+            chunks[j, c * h : (c + 1) * h, :] = part[j * h : (j + 1) * h]
+
+
+def rim_kernel(
+    h, group, from_y, from_d, weight, chunks, to_core, *outs_and_scratch
+):
+    outs, (rows_all, pieces) = outs_and_scratch[:-2], outs_and_scratch[-2:]
+    sy, sx, me = lax.axis_index("sy"), lax.axis_index("sx"), lax.axis_index("ang")
+    f32, bf16 = jnp.float32, jnp.bfloat16
+    cols = from_y.shape[2] - BLK
+    count = from_y.shape[1] // h
+    mine, other, rim_mine, rim_other = column_cuts(sx, cols)
+    edge = pl.ds(aligned(sx * (cols - BLK), BLK), BLK)
+    for c in range(2):
+        rows_all[c, :, mine] = from_y[c, :, 0:cols].astype(f32)
+        rows_all[c, :, other] = from_d[c, :, 0:cols].astype(f32)
+        rows_all[c, :, rim_mine] += from_y[c, :, cols:].astype(f32)
+        rows_all[c, :, rim_other] += from_d[c, :, cols:].astype(f32)
         to_core[c] = from_d[c, :, 0:cols]
         to_core[c, :, edge] = (from_d[c, :, edge].astype(f32) + from_y[c, :, cols:].astype(f32)).astype(bf16)
-        part = jnp.dot(rows_all[c].astype(bf16), weight[...], preferred_element_type=f32)
-        for j in range(count):
-            chunks[j, c * h : (c + 1) * h, :] = part[j * h : (j + 1) * h]
-    keep[...] = chunks[me]
-    for d in range(1, group):
-        outs[d - 1][...] = chunks[me ^ d].astype(bf16)
+    rows = rows_all[...].reshape(2 * count * h, 2 * cols).astype(bf16)
+    part = jnp.dot(rows, weight[...], preferred_element_type=f32)
+    for c in range(2):
+        for q in range(count):
+            row = (c * count + q) * h
+            pieces[q, c * h : (c + 1) * h, :] = part[row : row + h]
+    total = chunks.shape[0]
+    base = (1 - sy) * (total - count)
+
+    def piece(owner):
+        rel = owner - base
+        found = pieces[jnp.clip(rel, 0, count - 1)]
+        return chunks[owner] + jnp.where((rel >= 0) & (rel < count), found, jnp.zeros_like(found))
+
     for d in range(group):
-        for k in range(1, count // group):
-            piece = chunks[me ^ d ^ (k * group)]
-            ref = outs[group - 1 + d]
-            ref[(k - 1) * 2 * h : k * 2 * h, :] = piece.astype(ref.dtype)
+        outs[d][...] = piece(me ^ d).astype(outs[d].dtype)
+        far = outs[group + d]
+        for k in range(1, total // group):
+            far[(k - 1) * 2 * h : k * 2 * h, :] = piece(me ^ d ^ (k * group)).astype(far.dtype)
 
 
 def fold_kernel(h, grad, from_x, rim_x, from_y, from_d, from_core, out):
@@ -319,13 +377,16 @@
         add_strips(out, c, row, RIM, every, 1 - sx, h, from_core[c].astype(f32))
 
 
-def far_kernel(count, *refs):
+def far_kernel(*refs):
     out = refs[-1]
     total = refs[0][...]
     for ref in refs[1:-1]:
         total += ref[...].astype(jnp.float32)
-    total = total.astype(out.dtype)
-    out[...] = total
+    out[...] = total.astype(out.dtype)
+
+
+def probe_sum_kernel(kept, received, after, out):
+    out[...] = (kept[...].astype(jnp.float32) + received[...].astype(jnp.float32)).astype(out.dtype)
 
 
 def last_kernel(h, *refs):
@@ -338,9 +399,7 @@
 
 
 def probe_kernel(scale, mine, other, out):
-    sx = lax.axis_index("sx")
-    out[sx] = mine[...].astype(jnp.float32) * scale
-    out[1 - sx] = other[...].astype(jnp.float32) * scale
+    out[...] = (mine[...].astype(jnp.float32) + other[...].astype(jnp.float32)) * scale
 
 
 def body(objects, probe, data, positions, block_index, block_values):
@@ -361,24 +420,40 @@
     to_y, to_x, to_d = call(
         edge_kernel,
         (shape((2, RIM, cols)), shape((2, rows, BLK)), shape((2, RIM, BLK))),
-        (obj,), [VMEM], moved=2 * MIB,
+        (obj,), [HBM], [pltpu.SemaphoreType.DMA((3,))], moved=2 * MIB,
     )
     halo_y = lax.ppermute(to_y, "sy", SWAP)
     halo_d = lax.ppermute(to_d, ("sy", "sx"), CROSS)
     halo_x = lax.ppermute(to_x, "sx", SWAP)
 
     entries = block_index.size // n
-    weight = call(
-        partial(weight_kernel, entries),
+    matrix = call(
+        partial(gather_kernel, entries),
         shape((width, width)),
-        (block_index, block_values, jnp.asarray(ramp_table(width))),
-        [SMEM, VMEM, VMEM],
-        [pltpu.VMEM((width, width), f32), pltpu.SMEM((entries,), jnp.int32)],
-        flops=2 * entries * width * BLK * BLK * 4, moved=8 * MIB,
+        (block_index, block_values),
+        [HBM, HBM],
+        [
+            pltpu.VMEM((entries, BLK, BLK), bf16),
+            pltpu.VMEM((entries, BLK, BLK), f32),
+            pltpu.SMEM(block_index.shape, jnp.int32),
+            pltpu.SMEM((entries + 1,), jnp.int32),
+            pltpu.SMEM((lines * lines,), jnp.int32),
+            pltpu.SemaphoreType.DMA((entries + 1,)),
+        ],
+        flops=MIB, moved=4 * MIB,
+    )
+    carried = (obj, probe, measured, jnp.asarray(dft_blocks(PATCH)))
+    weight, obj, probe, measured, dft = call(
+        weight_kernel,
+        (shape((width, width)),) + tuple(shape(x.shape, x.dtype) for x in carried),
+        (matrix, jnp.asarray(ramp_strip(width))) + carried,
+        [VMEM, VMEM] + [HBM] * len(carried),
+        [pltpu.SemaphoreType.DMA((len(carried),))],
+        flops=2 * width**3, moved=6 * MIB,
     )
 
     wide = cols + BLK
-    grad, own, to_x, rim_x, to_y, to_d, probe_keep, probe_send = call(
+    grad, own, to_x, rim_x, to_y, to_d, probe_here = call(
         partial(patch_kernel, h),
         (
             shape((2, rows, cols), f32),
@@ -387,54 +462,64 @@
             shape((2, strip_rows, BLK)),
             shape((2, RIM // 2, wide)),
             shape((2, RIM // 2, wide)),
-            shape((2, PATCH, PATCH), f32),
-            shape((2, PATCH, PATCH)),
+            shape((modes, 2, PATCH, PATCH)),
         ),
-        (pos, obj, halo_y, halo_x, halo_d, probe, measured, jnp.asarray(dft_blocks(PATCH))),
-        [SMEM] + [VMEM] * 7,
+        (pos, weight, obj, halo_y, halo_x, halo_d, probe, measured, dft),
+        [HBM, ANY] + [VMEM] * 7,
         [
             pltpu.VMEM((2, rows + 2 * RIM + 8, cols + 2 * BLK), f32),
             pltpu.VMEM((2, rows + 2 * RIM + 8, cols + 2 * BLK), f32),
             pltpu.VMEM((2 * PATCH, patches * modes * PATCH), bf16),
             pltpu.VMEM((modes, 2, PATCH, PATCH), f32),
+            pltpu.SMEM(pos.shape, jnp.int32),
+            pltpu.SemaphoreType.DMA,
         ],
-        limit=48, flops=patches * modes * 32 * PATCH**3, moved=8 * MIB,
+        limit=24, flops=patches * modes * 32 * PATCH**3, moved=8 * MIB,
     )
 
     from_x = lax.ppermute(to_x, "sx", SWAP)
     from_y = lax.ppermute(to_y, "sy", SWAP)
     from_d = lax.ppermute(to_d, ("sy", "sx"), CROSS)
     from_rim = lax.ppermute(rim_x, "sx", SWAP)
-    probe_x = lax.ppermute(probe_send, "sx", SWAP)
-    probe_mine = (probe_keep + probe_x.astype(f32)).astype(bf16)
-    probe_y = lax.ppermute(probe_mine, "sy", SWAP)
-    probe_mine = (probe_mine.astype(f32) + probe_y.astype(f32)).astype(bf16)
-    probe_other = lax.ppermute(probe_mine, "sx", SWAP)
-
+    probe_x = lax.ppermute(probe_here, "sx", SWAP)
+
+    chunks = call(
+        partial(project_kernel, h),
+        shape((n, 2 * h, width), f32),
+        (own, from_x, weight),
+        [VMEM] * 3,
+        [pltpu.VMEM((2, strip_rows, width), f32)],
+        flops=4 * strip_rows * width * width, moved=8 * MIB,
+    )
     far = n // group - 1
     outs = call(
-        partial(project_kernel, h, group),
+        partial(rim_kernel, h, group),
         (shape((2, RIM // 2, cols)), shape((2 * h, width), f32))
         + (shape((2 * h, width)),) * (group - 1)
         + (shape((far * 2 * h, width), f32),)
         + (shape((far * 2 * h, width)),) * (group - 1),
-        (own, from_x, from_y, from_d, weight),
-        [VMEM] * 5,
-        [pltpu.VMEM((2, strip_rows, width), f32), pltpu.VMEM((n, 2 * h, width), f32)],
-        flops=4 * strip_rows * width * width, moved=8 * MIB,
-    )
-    to_core, keep, near, away = outs[0], outs[1], outs[2 : 1 + group], outs[1 + group :]
+        (from_y, from_d, weight, chunks),
+        [VMEM] * 4,
+        [pltpu.VMEM((2, RIM // 2, width), f32), pltpu.VMEM((RIM // (2 * h), 2 * h, width), f32)],
+        flops=2 * RIM * width * width, moved=4 * MIB,
+    )
+    to_core, near, away = outs[0], outs[1 : 1 + group], outs[1 + group :]
 
     def swap(array, d):
         return lax.ppermute(array, "ang", [(i, i ^ d) for i in range(n)])
 
     got = [swap(away[d], d) for d in range(group - 1, 0, -1)]
-    near_got = [swap(near[d - 1], d) for d in range(group - 1, 0, -1)]
+    near_got = [swap(near[d], d) for d in range(group - 1, 0, -1)]
     across = call(
-        partial(far_kernel, far), shape((far * 2 * h, width)), [away[0]] + got, [VMEM] * group,
-        moved=MIB,
+        far_kernel, shape((far * 2 * h, width)), [away[0]] + got, [VMEM] * group, moved=MIB,
     )
     across_got = [swap(across[(k - 1) * 2 * h : k * 2 * h], k * group) for k in range(1, far + 1)]
+
+    probe_here = call(
+        probe_sum_kernel, shape((modes, 2, PATCH, PATCH)), (probe_here, probe_x, to_core),
+        [VMEM, VMEM, ANY], moved=MIB,
+    )
+    probe_y = lax.ppermute(probe_here, "sy", SWAP)
     from_core = lax.ppermute(to_core, "sx", SWAP)
     object_grad = call(
         partial(fold_kernel, h),
@@ -445,13 +530,13 @@
     probe_grad = call(
         partial(probe_kernel, 1.0 / math.sqrt(patches * tiles)),
         shape((modes, 2, PATCH, PATCH), f32),
-        (probe_mine, probe_other),
+        (probe_here, probe_y),
         [VMEM] * 2, moved=2 * MIB,
     )
     vol = call(
         partial(last_kernel, h),
         shape((h, 2, width), f32),
-        [keep] + near_got + across_got,
+        [near[0]] + near_got + across_got,
         [VMEM] * (group + far), moved=MIB,
     )
     return (object_grad[None], probe_grad[None], vol[None])

time: 56 us -> 45.3 us (0.81)
  local copies, waits for them, and re-layouts: 5.31 us -> 0.01 us
  Pallas kernels: 20.7 us -> 16.3 us
  starting transfers between devices: 17.2 us -> 15.6 us
  waiting for transfers between devices: 11.7 us -> 12.5 us
    unnamed x18 -> x2, local copies, waits for them, and re-layouts: 5.31 us -> 0.01 us
    ppermute x1, waiting for transfers between devices: 4.46 us -> 0.01 us  [body(): halo_d = lax.ppermute(to_d, ('sy', 'sx'), CROSS)]
    pallas_call x8 -> x11, Pallas kernels: 20.7 us -> 16.3 us  [call(): pl.pallas_call(kernel, out_shape=outs, in_specs=specs, out_specs=jax.tree...]
    ppermute x1, starting transfers between devices: 0.07 us -> 2.64 us  [body(): halo_d = lax.ppermute(to_d, ('sy', 'sx'), CROSS)]
    ppermute x1, starting transfers between devices: 2.59 us -> 0.05 us  [body(): halo_y = lax.ppermute(to_y, 'sy', SWAP)]
    ppermute x1, waiting for transfers between devices: 0.01 us -> 1.79 us  [body(): from_d = lax.ppermute(to_d, ('sy', 'sx'), CROSS)]
    ppermute x7, waiting for transfers between devices: 7.23 us -> 8.83 us  [swap(): return lax.ppermute(array, 'ang', [(i, i ^ d) for i in range(n)])]
    ppermute x1, waiting for transfers between devices: 0.01 us -> 1.4 us  [body(): from_y = lax.ppermute(to_y, 'sy', SWAP)]
  transfers between devices with their start and end apart: 18 -> 17, of which waited for: 6 -> 8; matrix products, arithmetic and copies ran while one was open for 0% -> 0% of each run, Pallas kernels for 23% -> 22%
where the time goes in v2:
time: 45.3 us; the launch traced here: 45 us
  Pallas kernels  16.3 us (36%)
  starting transfers between devices  15.6 us (34%)
  waiting for transfers between devices  12.5 us (28%)
  between operations  0.74 us (2%)
    pallas_call x11, Pallas kernels, call(): pl.pallas_call(kernel, out_shape=outs, in_specs=specs, out_specs=jax.tree...  16.3 us
    ppermute x7, starting transfers between devices, swap(): return lax.ppermute(array, 'ang', [(i, i ^ d) for i in range(n)])  9.63 us
    ppermute x7, waiting for transfers between devices, swap(): return lax.ppermute(array, 'ang', [(i, i ^ d) for i in range(n)])  8.83 us
    ppermute x1, starting transfers between devices, body(): halo_d = lax.ppermute(to_d, ('sy', 'sx'), CROSS)  2.64 us
    ppermute x1, waiting for transfers between devices, body(): from_d = lax.ppermute(to_d, ('sy', 'sx'), CROSS)  1.79 us
    ppermute x1, starting transfers between devices, body(): from_y = lax.ppermute(to_y, 'sy', SWAP)  1.51 us
    ppermute x1, waiting for transfers between devices, body(): from_y = lax.ppermute(to_y, 'sy', SWAP)  1.4 us
  transfers between devices with their start and end apart: 17, of which 8 were waited for; matrix products, arithmetic and copies ran while one was open for 0% of the time, Pallas kernels for 22%

profile of v2, /device:TPU:0, one launch (start us, length us, event | category | flops | bytes accessed | tf_op | source)
XLA Modules:
  0.0 45.0 jit_solution(17265198559158297650)
XLA Ops:
  0.6 1.1 %shard_map.105 = (bf16[2,64,512]{2,1,0:T(8,128)(2,1)S(1)}, bf16[2,512,128]{2,1,0:T(8,128)(2,1)S(1)}, bf16[2,64,128]{2,1,0:T(8,128)(2,1)S(1)}) custom-call(bf16[2,512,512]{2,1,0:T(8,128)(2,1)} %bitcast.7), custom_call_target="tpu_custom_call" | custom-call | bytes 2097152 | tf_op jit(solution)/shard_map/pallas_call | solution.py:53
  1.8 0.5 %collective-permute-start.1 = (bf16[2,512,128]{2,1,0:T(8,128)(2,1)S(1)}, bf16[2,512,128]{2,1,0:T(8,128)(2,1)S(1)}, u32[]{:S(2)}, u32[]{:S(2)}) collective-permute-start(bf16[2,512,128]{2,1,0:T(8,128)(2,1)S(1)} %get-tuple-element.30), channel_id=1, source_target_pairs={{0,1},{1,0},{2,3},{3,2},{4,5},{5,4},{6,7},{7,6},{8,9},{9,8},{10,11... | collective-permute-start | bytes 786440 | tf_op jit(solution)/shard_map/ppermute | solution.py:427
  2.3 2.6 %collective-permute-start.2 = (bf16[2,64,128]{2,1,0:T(8,128)(2,1)S(1)}, bf16[2,64,128]{2,1,0:T(8,128)(2,1)S(1)}, u32[]{:S(2)}, u32[]{:S(2)}) collective-permute-start(bf16[2,64,128]{2,1,0:T(8,128)(2,1)S(1)} %get-tuple-element.31), channel_id=1, source_target_pairs={{0,3},{3,0},{1,2},{2,1},{4,7},{7,4},{5,6},{6,5},{8,11},{11,8},{9,1... | collective-permute-start | bytes 98312 | tf_op jit(solution)/shard_map/ppermute | solution.py:426
  4.9 0.0 copy-start
  4.9 0.1 collective-permute-start
  5.0 2.7 %shard_map.103.matrix = bf16[1024,1024]{1,0:T(8,128)(2,1)S(1)} custom-call(s32[8,16]{1,0:T(8,128)} %index.1, bf16[8,16,128,128]{3,2,1,0:T(8,128)(2,1)} %values.1), custom_call_target="tpu_custom_call" | custom-call | flops 1048576 | bytes 4194304 | tf_op jit(solution)/shard_map/pallas_call | solution.py:53
  7.7 0.0 copy-done
  7.7 2.4 %shard_map.104 = (bf16[1024,1024]{1,0:T(8,128)(2,1)S(1)}, bf16[2,512,512]{2,1,0:T(8,128)(2,1)S(1)}, f32[2,2,256,256]{3,2,1,0:T(8,128)S(1)}, bf16[2,256,256]{2,1,0:T(8,128)(2,1)S(1)}, bf16[2,512,512]{2,1,0:T(8,128)(2,1)S(1)}) custom-call(bf16[1024,1024]{1,0:T(8,128)(2,1)S(1)} %shard_map.103.matrix, bf16[128,1920]{1,0:T(8,128)(2,1)S(1)} %copy-done, ...), custom_call_target="tpu_custom_call" | custom-call | flops 2147483648 | bytes 6291456 | tf_op jit(solution)/shard_map/pallas_call | solution.py:53
  10.1 0.0 collective-permute-done.2.from_d
  10.1 0.3 collective-permute-done.from_y
  10.4 0.0 collective-permute-done.1.from_x
  10.4 4.2 %shard_map.106 = (f32[2,512,512]{2,1,0:T(8,128)S(1)}, bf16[2,256,640]{2,1,0:T(8,128)(2,1)S(1)}, bf16[2,256,640]{2,1,0:T(8,128)(2,1)S(1)}, bf16[2,256,128]{2,1,0:...) custom-call(s32[2,2]{1,0:T(2,128)} %bitcast.12, ...), custom_call_target="tpu_custom_call" | custom-call | flops 2147483648 | bytes 8388608 | tf_op jit(solution)/shard_map/pallas_call | solution.py:53
  14.6 0.1 collective-permute-start.3
  14.7 0.5 %collective-permute-start.8 = (bf16[2,2,256,256]{3,2,1,0:T(8,128)(2,1)S(1)}, bf16[2,2,256,256]{3,2,1,0:T(8,128)(2,1)S(1)}, u32[]{:S(2)}, u32[]{:S(2)}) collective-permute-start(bf16[2,2,256,256]{3,2,1,0:T(8,128)(2,1)S(1)} %get-tuple-element.42.kept), channel_id=1, source_target_pairs={{0,1},{1,0},{2,3},{3,2},{4,5},{5,4},{6,7},{7,6},{8,9},{9,8},{10,11... | collective-permute-start | bytes 1572872 | tf_op jit(solution)/shard_map/ppermute | solution.py:484
  15.2 1.5 %collective-permute-start.5 = (bf16[2,32,640]{2,1,0:T(8,128)(2,1)S(1)}, bf16[2,32,640]{2,1,0:T(8,128)(2,1)S(1)}, u32[]{:S(2)}, u32[]{:S(2)}) collective-permute-start(bf16[2,32,640]{2,1,0:T(8,128)(2,1)S(1)} %get-tuple-element.38), channel_id=1, source_target_pairs={{0,2},{2,0},{1,3},{3,1},{4,6},{6,4},{5,7},{7,5},{8,10},{10,8},{9,1... | collective-permute-start | bytes 245768 | tf_op jit(solution)/shard_map/ppermute | solution.py:481
  16.7 0.0 collective-permute-start.6
  16.7 0.1 collective-permute-done.3.from_x
  16.8 1.4 %shard_map.107.chunks = f32[8,64,1024]{2,1,0:T(8,128)S(1)} custom-call(bf16[2,256,640]{2,1,0:T(8,128)(2,1)S(1)} %get-tuple-element.40.own, bf16[2,256,640]{2,1,0:T(8,128)(2,1)S(1)} %collective-permute-done.3.from_x, bf16[1024,1024]{1,0:T(8,128)(2,1)S(1)} %get-tuple-element.27.ahead.weight), custom_call_target="tpu_custom_call" | custom-call | flops 1073741824 | bytes 8388608 | tf_op jit(solution)/shard_map/pallas_call | solution.py:53
  18.2 1.4 %collective-permute-done.5.from_y = bf16[2,32,640]{2,1,0:T(8,128)(2,1)S(1)} collective-permute-done((bf16[2,32,640]{2,1,0:T(8,128)(2,1)S(1)}, bf16[2,32,640]{2,1,0:T(8,128)(2,1)S(1)}, u32[]{:S(2)}, u32[]{:S(2)}) %collective-permute-start.5) | collective-permute-done | bytes 81952 | tf_op jit(solution)/shard_map/ppermute | solution.py:481
  19.6 1.8 %collective-permute-done.6.from_d = bf16[2,32,640]{2,1,0:T(8,128)(2,1)S(1)} collective-permute-done((bf16[2,32,640]{2,1,0:T(8,128)(2,1)S(1)}, bf16[2,32,640]{2,1,0:T(8,128)(2,1)S(1)}, u32[]{:S(2)}, u32[]{:S(2)}) %collective-permute-start.6) | collective-permute-done | bytes 81952 | tf_op jit(solution)/shard_map/ppermute | solution.py:482
  21.4 0.6 %shard_map.108 = (bf16[2,32,512]{2,1,0:T(8,128)(2,1)S(1)}, f32[64,1024]{1,0:T(8,128)S(1)}, bf16[64,1024]{1,0:T(8,128)(2,1)S(1)}, bf16[64,1024]{1,0:T(8,128)(2,1)...) custom-call(bf16[2,32,640]{2,1,0:T(8,128)(2,1)S(1)} %collective-perm, ...), custom_call_target="tpu_custom_call" | custom-call | flops 134217728 | bytes 4194304 | tf_op jit(solution)/shard_map/pallas_call | solution.py:53
  22.1 0.0 collective-permute-done.8.received
  22.1 0.1 shard_map.110.mine
  22.2 0.6 %collective-permute-start.9 = (bf16[2,2,256,256]{3,2,1,0:T(8,128)(2,1)S(1)}, bf16[2,2,256,256]{3,2,1,0:T(8,128)(2,1)S(1)}, u32[]{:S(2)}, u32[]{:S(2)}) collective-permute-start(bf16[2,2,256,256]{3,2,1,0:T(8,128)(2,1)S(1)} %shard_map.110.mine), channel_id=1, source_target_pairs={{0,2},{2,0},{1,3},{3,1},{4,6},{6,4},{5,7},{7,5},{8,10},{10,8},{9,1... | collective-permute-start | bytes 1572872 | tf_op jit(solution)/shard_map/ppermute | solution.py:522
  22.9 2.5 %collective-permute-start.13 = (bf16[64,1024]{1,0:T(8,128)(2,1)S(1)}, bf16[64,1024]{1,0:T(8,128)(2,1)S(1)}, u32[]{:S(2)}, u32[]{:S(2)}) collective-permute-start(bf16[64,1024]{1,0:T(8,128)(2,1)S(1)} %get-tuple-element.48), channel_id=1, source_target_pairs={{0,12},{4,8},{8,4},{12,0},{16,28},{20,24},{24,20},{28,16},{1,13},{... | collective-permute-start | bytes 393224 | tf_op jit(solution)/shard_map/ppermute | solution.py:509
  25.4 0.5 %collective-permute-start.14 = (bf16[64,1024]{1,0:T(8,128)(2,1)S(1)}, bf16[64,1024]{1,0:T(8,128)(2,1)S(1)}, u32[]{:S(2)}, u32[]{:S(2)}) collective-permute-start(bf16[64,1024]{1,0:T(8,128)(2,1)S(1)} %get-tuple-element.49), channel_id=1, source_target_pairs={{0,8},{4,12},{8,0},{12,4},{16,24},{20,28},{24,16},{28,20},{1,9},{5... | collective-permute-start | bytes 393224 | tf_op jit(solution)/shard_map/ppermute | solution.py:509
  25.9 0.5 %collective-permute-start.15 = (bf16[64,1024]{1,0:T(8,128)(2,1)S(1)}, bf16[64,1024]{1,0:T(8,128)(2,1)S(1)}, u32[]{:S(2)}, u32[]{:S(2)}) collective-permute-start(bf16[64,1024]{1,0:T(8,128)(2,1)S(1)} %get-tuple-element.50), channel_id=1, source_target_pairs={{0,4},{4,0},{8,12},{12,8},{16,20},{20,16},{24,28},{28,24},{1,5},{5... | collective-permute-start | bytes 393224 | tf_op jit(solution)/shard_map/ppermute | solution.py:509
  26.4 0.0 collective-permute-start.4
  26.4 3.7 %collective-permute-done.13.refs_1_ = bf16[64,1024]{1,0:T(8,128)(2,1)S(1)} collective-permute-done((bf16[64,1024]{1,0:T(8,128)(2,1)S(1)}, bf16[64,1024]{1,0:T(8,128)(2,1)S(1)}, u32[]{:S(2)}, u32[]{:S(2)}) %collective-permute-start.13) | collective-permute-done | bytes 131104 | tf_op jit(solution)/shard_map/ppermute | solution.py:509
  30.1 0.0 collective-permute-start.7
  30.1 2.4 %collective-permute-done.14.refs_2_ = bf16[64,1024]{1,0:T(8,128)(2,1)S(1)} collective-permute-done((bf16[64,1024]{1,0:T(8,128)(2,1)S(1)}, bf16[64,1024]{1,0:T(8,128)(2,1)S(1)}, u32[]{:S(2)}, u32[]{:S(2)}) %collective-permute-start.14) | collective-permute-done | bytes 131104 | tf_op jit(solution)/shard_map/ppermute | solution.py:509
  32.5 1.5 %collective-permute-start.10 = (bf16[64,1024]{1,0:T(8,128)(2,1)S(1)}, bf16[64,1024]{1,0:T(8,128)(2,1)S(1)}, u32[]{:S(2)}, u32[]{:S(2)}) collective-permute-start(bf16[64,1024]{1,0:T(8,128)(2,1)S(1)} %get-tuple-element.44), channel_id=1, source_target_pairs={{0,12},{4,8},{8,4},{12,0},{16,28},{20,24},{24,20},{28,16},{1,13},{... | collective-permute-start | bytes 393224 | tf_op jit(solution)/shard_map/ppermute | solution.py:509
  34.0 0.0 collective-permute-done.15.refs_3_
  34.0 0.4 collective-permute-start.11
  34.5 0.1 shard_map.112
  34.5 0.0 collective-permute-done.4.rim_x
  34.5 1.6 %collective-permute-start.12 = (bf16[64,1024]{1,0:T(8,128)(2,1)S(1)}, bf16[64,1024]{1,0:T(8,128)(2,1)S(1)}, u32[]{:S(2)}, u32[]{:S(2)}) collective-permute-start(bf16[64,1024]{1,0:T(8,128)(2,1)S(1)} %get-tuple-element.46), channel_id=1, source_target_pairs={{0,4},{4,0},{8,12},{12,8},{16,20},{20,16},{24,28},{28,24},{1,5},{5... | collective-permute-start | bytes 393224 | tf_op jit(solution)/shard_map/ppermute | solution.py:509
  36.2 0.0 collective-permute-done.7.from_core
  36.2 2.6 %collective-permute-start.16 = (bf16[64,1024]{1,0:T(8,128)(2,1)S(1)}, bf16[64,1024]{1,0:T(8,128)(2,1)S(1)}, u32[]{:S(2)}, u32[]{:S(2)}) collective-permute-start(bf16[64,1024]{1,0:T(8,128)(2,1)S(1)} %shard_map.112), channel_id=1, source_target_pairs={{0,16},{4,20},{8,24},{12,28},{16,0},{20,4},{24,8},{28,12},{1,17},{... | collective-permute-start | bytes 393224 | tf_op jit(solution)/shard_map/ppermute | solution.py:509
  38.7 1.7 %shard_map.109 = f32[2,512,512]{2,1,0:T(8,128)} custom-call(f32[2,512,512]{2,1,0:T(8,128)S(1)} %get-tuple-element.35.grad, bf16[2,256,640]{2,1,0:T(8,128)(2,1)S(1)} %collective-permute-done.3.from_x, bf16[2,256,128]{2,1,0:T(8,128)(2,1)S(1)} %collective-permute-done.4.rim_x, bf16[2,32,640]{2,1,0:T(8,128)(2,1)S(1)} %collective-permute-done.5.from_y, ...), custom_call_target="tpu_custom_call" | custom-call | bytes 6291456 | tf_op jit(solution)/shard_map/pallas_call | solution.py:53
  40.4 2.2 %collective-permute-done.10.refs_1_ = bf16[64,1024]{1,0:T(8,128)(2,1)S(1)} collective-permute-done((bf16[64,1024]{1,0:T(8,128)(2,1)S(1)}, bf16[64,1024]{1,0:T(8,128)(2,1)S(1)}, u32[]{:S(2)}, u32[]{:S(2)}) %collective-permute-start.10) | collective-permute-done | bytes 131104 | tf_op jit(solution)/shard_map/ppermute | solution.py:509
  42.6 0.4 collective-permute-done.11.refs_2_
  43.1 0.0 collective-permute-done.12.refs_3_
  43.1 0.0 collective-permute-done.16.refs_4_
  43.1 0.8 %shard_map.113 = f32[32,2,1024]{2,1,0:T(2,128)} custom-call(f32[64,1024]{1,0:T(8,128)S(1)} %get-tuple-element.43.refs_0_, bf16[64,1024]{1,0:T(8,128)(2,1)S(1)} %collective-permute-done.10.refs_1_, bf16[64,1024]{1,0:T(8,128)(2,1)S(1)} %collective-permute-done.11.refs_2_, bf16[64,1024]{1,0:T(8,128)(2,1)S(1)} %collective-permute-done.12.refs_3_, ...), custom_call_target="tpu_custom_call" | custom-call | bytes 1048576 | tf_op jit(solution)/shard_map/pallas_call | solution.py:53
  43.9 0.0 collective-permute-done.9.other
  43.9 1.1 %shard_map.111 = f32[2,2,256,256]{3,2,1,0:T(8,128)} custom-call(bf16[2,2,256,256]{3,2,1,0:T(8,128)(2,1)S(1)} %shard_map.110.mine, bf16[2,2,256,256]{3,2,1,0:T(8,128)(2,1)S(1)} %collective-permute-done.9.other), custom_call_target="tpu_custom_call" | custom-call | bytes 2097152 | tf_op jit(solution)/shard_map/pallas_call | solution.py:53
Async XLA Ops:
  1.8 8.6 %collective-permute-start.1 = (bf16[2,512,128]{2,1,0:T(8,128)(2,1)S(1)}, bf16[2,512,128]{2,1,0:T(8,128)(2,1)S(1)}, u32[]{:S(2)}, u32[]{:S(2)}) collective-permute-start(bf16[2,512,128]{2,1,0:T(8,128)(2,1)S(1)} %get-tuple-element.30), channel_id=1, source_target_pairs={{0,1},{1,0},{2,3},{3,2},{4,5},{5,4},{6,7},{7,6},{8,9},{9,8},{10,11... | collective-permute-start | bytes 786440 | tf_op jit(solution)/shard_map/ppermute | solution.py:427
  2.3 7.8 %collective-permute-start.2 = (bf16[2,64,128]{2,1,0:T(8,128)(2,1)S(1)}, bf16[2,64,128]{2,1,0:T(8,128)(2,1)S(1)}, u32[]{:S(2)}, u32[]{:S(2)}) collective-permute-start(bf16[2,64,128]{2,1,0:T(8,128)(2,1)S(1)} %get-tuple-element.31), channel_id=1, source_target_pairs={{0,3},{3,0},{1,2},{2,1},{4,7},{7,4},{5,6},{6,5},{8,11},{11,8},{9,1... | collective-permute-start | bytes 98312 | tf_op jit(solution)/shard_map/ppermute | solution.py:426
  4.9 2.7 %copy-start = (bf16[128,1920]{1,0:T(8,128)(2,1)S(1)}, bf16[128,1920]{1,0:T(8,128)(2,1)}, u32[]{:S(2)}) copy-start(bf16[128,1920]{1,0:T(8,128)(2,1)} %constant.5.clone.strip) | copy-start | bytes 1474564
  4.9 5.5 %collective-permute-start = (bf16[2,64,512]{2,1,0:T(8,128)(2,1)S(1)}, bf16[2,64,512]{2,1,0:T(8,128)(2,1)S(1)}, u32[]{:S(2)}, u32[]{:S(2)}) collective-permute-start(bf16[2,64,512]{2,1,0:T(8,128)(2,1)S(1)} %get-tuple-element.29), channel_id=1, source_target_pairs={{0,2},{2,0},{1,3},{3,1},{4,6},{6,4},{5,7},{7,5},{8,10},{10,8},{9,1... | collective-permute-start | bytes 393224 | tf_op jit(solution)/shard_map/ppermute | solution.py:425
  14.6 2.2 %collective-permute-start.3 = (bf16[2,256,640]{2,1,0:T(8,128)(2,1)S(1)}, bf16[2,256,640]{2,1,0:T(8,128)(2,1)S(1)}, u32[]{:S(2)}, u32[]{:S(2)}) collective-permute-start(bf16[2,256,640]{2,1,0:T(8,128)(2,1)S(1)} %get-tuple-element.36), channel_id=1, source_target_pairs={{0,1},{1,0},{2,3},{3,2},{4,5},{5,4},{6,7},{7,6},{8,9},{9,8},{10,11... | collective-permute-start | bytes 1966088 | tf_op jit(solution)/shard_map/ppermute | solution.py:480
  14.7 7.4 %collective-permute-start.8 = (bf16[2,2,256,256]{3,2,1,0:T(8,128)(2,1)S(1)}, bf16[2,2,256,256]{3,2,1,0:T(8,128)(2,1)S(1)}, u32[]{:S(2)}, u32[]{:S(2)}) collective-permute-start(bf16[2,2,256,256]{3,2,1,0:T(8,128)(2,1)S(1)} %get-tuple-element.42.kept), channel_id=1, source_target_pairs={{0,1},{1,0},{2,3},{3,2},{4,5},{5,4},{6,7},{7,6},{8,9},{9,8},{10,11... | collective-permute-start | bytes 1572872 | tf_op jit(solution)/shard_map/ppermute | solution.py:484
  15.2 4.4 %collective-permute-start.5 = (bf16[2,32,640]{2,1,0:T(8,128)(2,1)S(1)}, bf16[2,32,640]{2,1,0:T(8,128)(2,1)S(1)}, u32[]{:S(2)}, u32[]{:S(2)}) collective-permute-start(bf16[2,32,640]{2,1,0:T(8,128)(2,1)S(1)} %get-tuple-element.38), channel_id=1, source_target_pairs={{0,2},{2,0},{1,3},{3,1},{4,6},{6,4},{5,7},{7,5},{8,10},{10,8},{9,1... | collective-permute-start | bytes 245768 | tf_op jit(solution)/shard_map/ppermute | solution.py:481
  16.7 4.7 %collective-permute-start.6 = (bf16[2,32,640]{2,1,0:T(8,128)(2,1)S(1)}, bf16[2,32,640]{2,1,0:T(8,128)(2,1)S(1)}, u32[]{:S(2)}, u32[]{:S(2)}) collective-permute-start(bf16[2,32,640]{2,1,0:T(8,128)(2,1)S(1)} %get-tuple-element.39), channel_id=1, source_target_pairs={{0,3},{3,0},{1,2},{2,1},{4,7},{7,4},{5,6},{6,5},{8,11},{11,8},{9,1... | collective-permute-start | bytes 245768 | tf_op jit(solution)/shard_map/ppermute | solution.py:482
  22.2 21.7 %collective-permute-start.9 = (bf16[2,2,256,256]{3,2,1,0:T(8,128)(2,1)S(1)}, bf16[2,2,256,256]{3,2,1,0:T(8,128)(2,1)S(1)}, u32[]{:S(2)}, u32[]{:S(2)}) collective-permute-start(bf16[2,2,256,256]{3,2,1,0:T(8,128)(2,1)S(1)} %shard_map.110.mine), channel_id=1, source_target_pairs={{0,2},{2,0},{1,3},{3,1},{4,6},{6,4},{5,7},{7,5},{8,10},{10,8},{9,1... | collective-permute-start | bytes 1572872 | tf_op jit(solution)/shard_map/ppermute | solution.py:522
  22.9 7.2 %collective-permute-start.13 = (bf16[64,1024]{1,0:T(8,128)(2,1)S(1)}, bf16[64,1024]{1,0:T(8,128)(2,1)S(1)}, u32[]{:S(2)}, u32[]{:S(2)}) collective-permute-start(bf16[64,1024]{1,0:T(8,128)(2,1)S(1)} %get-tuple-element.48), channel_id=1, source_target_pairs={{0,12},{4,8},{8,4},{12,0},{16,28},{20,24},{24,20},{28,16},{1,13},{... | collective-permute-start | bytes 393224 | tf_op jit(solution)/shard_map/ppermute | solution.py:509
  25.4 7.1 %collective-permute-start.14 = (bf16[64,1024]{1,0:T(8,128)(2,1)S(1)}, bf16[64,1024]{1,0:T(8,128)(2,1)S(1)}, u32[]{:S(2)}, u32[]{:S(2)}) collective-permute-start(bf16[64,1024]{1,0:T(8,128)(2,1)S(1)} %get-tuple-element.49), channel_id=1, source_target_pairs={{0,8},{4,12},{8,0},{12,4},{16,24},{20,28},{24,16},{28,20},{1,9},{5... | collective-permute-start | bytes 393224 | tf_op jit(solution)/shard_map/ppermute | solution.py:509
  25.9 8.1 %collective-permute-start.15 = (bf16[64,1024]{1,0:T(8,128)(2,1)S(1)}, bf16[64,1024]{1,0:T(8,128)(2,1)S(1)}, u32[]{:S(2)}, u32[]{:S(2)}) collective-permute-start(bf16[64,1024]{1,0:T(8,128)(2,1)S(1)} %get-tuple-element.50), channel_id=1, source_target_pairs={{0,4},{4,0},{8,12},{12,8},{16,20},{20,16},{24,28},{28,24},{1,5},{5... | collective-permute-start | bytes 393224 | tf_op jit(solution)/shard_map/ppermute | solution.py:509
  26.4 8.2 %collective-permute-start.4 = (bf16[2,256,128]{2,1,0:T(8,128)(2,1)S(1)}, bf16[2,256,128]{2,1,0:T(8,128)(2,1)S(1)}, u32[]{:S(2)}, u32[]{:S(2)}) collective-permute-start(bf16[2,256,128]{2,1,0:T(8,128)(2,1)S(1)} %get-tuple-element.37), channel_id=1, source_target_pairs={{0,1},{1,0},{2,3},{3,2},{4,5},{5,4},{6,7},{7,6},{8,9},{9,8},{10,11... | collective-permute-start | bytes 393224 | tf_op jit(solution)/shard_map/ppermute | solution.py:483
  30.1 6.1 %collective-permute-start.7 = (bf16[2,32,512]{2,1,0:T(8,128)(2,1)S(1)}, bf16[2,32,512]{2,1,0:T(8,128)(2,1)S(1)}, u32[]{:S(2)}, u32[]{:S(2)}) collective-permute-start(bf16[2,32,512]{2,1,0:T(8,128)(2,1)S(1)} %get-tuple-element.41.after), channel_id=1, source_target_pairs={{0,1},{1,0},{2,3},{3,2},{4,5},{5,4},{6,7},{7,6},{8,9},{9,8},{10,11... | collective-permute-start | bytes 196616 | tf_op jit(solution)/shard_map/ppermute | solution.py:523
  32.5 10.1 %collective-permute-start.10 = (bf16[64,1024]{1,0:T(8,128)(2,1)S(1)}, bf16[64,1024]{1,0:T(8,128)(2,1)S(1)}, u32[]{:S(2)}, u32[]{:S(2)}) collective-permute-start(bf16[64,1024]{1,0:T(8,128)(2,1)S(1)} %get-tuple-element.44), channel_id=1, source_target_pairs={{0,12},{4,8},{8,4},{12,0},{16,28},{20,24},{24,20},{28,16},{1,13},{... | collective-permute-start | bytes 393224 | tf_op jit(solution)/shard_map/ppermute | solution.py:509
  34.0 9.1 %collective-permute-start.11 = (bf16[64,1024]{1,0:T(8,128)(2,1)S(1)}, bf16[64,1024]{1,0:T(8,128)(2,1)S(1)}, u32[]{:S(2)}, u32[]{:S(2)}) collective-permute-start(bf16[64,1024]{1,0:T(8,128)(2,1)S(1)} %get-tuple-element.45), channel_id=1, source_target_pairs={{0,8},{4,12},{8,0},{12,4},{16,24},{20,28},{24,16},{28,20},{1,9},{5... | collective-permute-start | bytes 393224 | tf_op jit(solution)/shard_map/ppermute | solution.py:509
  34.5 8.5 %collective-permute-start.12 = (bf16[64,1024]{1,0:T(8,128)(2,1)S(1)}, bf16[64,1024]{1,0:T(8,128)(2,1)S(1)}, u32[]{:S(2)}, u32[]{:S(2)}) collective-permute-start(bf16[64,1024]{1,0:T(8,128)(2,1)S(1)} %get-tuple-element.46), channel_id=1, source_target_pairs={{0,4},{4,0},{8,12},{12,8},{16,20},{20,16},{24,28},{28,24},{1,5},{5... | collective-permute-start | bytes 393224 | tf_op jit(solution)/shard_map/ppermute | solution.py:509
  36.2 6.9 %collective-permute-start.16 = (bf16[64,1024]{1,0:T(8,128)(2,1)S(1)}, bf16[64,1024]{1,0:T(8,128)(2,1)S(1)}, u32[]{:S(2)}, u32[]{:S(2)}) collective-permute-start(bf16[64,1024]{1,0:T(8,128)(2,1)S(1)} %shard_map.112), channel_id=1, source_target_pairs={{0,16},{4,20},{8,24},{12,28},{16,0},{20,4},{24,8},{28,12},{1,17},{... | collective-permute-start | bytes 393224 | tf_op jit(solution)/shard_map/ppermute | solution.py:509

commit v3 on v2

--- a/solution.py
+++ b/solution.py
@@ -184,7 +184,7 @@
 
 def patch_kernel(
     h, pos, ahead, obj, from_y, from_x, from_d, probe, data, dft,
-    grad, own, to_x, rim_x, to_y, to_d, probe_send,
+    grad, own, to_x, to_y, to_d, probe_here,
     frame, total, stack, probe_total, spots, sem,
 ):
     fetch = pltpu.make_async_copy(pos, spots, sem)
@@ -294,8 +294,8 @@
         for half, wide in ((sx, to_y), (1 - sx, to_d)):
             wide[c, :, 0:cols] = pick_strips(total, c, row_in, RIM, inner, half, h)
             wide[c, :, cols:width] = pick_strips(total, c, row_in, RIM, out_block, half, h)
-        rim_x[c] = own[c, :, cols:width]
-    probe_send[...] = probe_total[...].astype(bf16)
+        to_x[c, :, width : width + BLK] = own[c, :, cols:width]
+    probe_here[...] = probe_total[...].astype(bf16)
 
 
 def column_cuts(sx, cols):
@@ -306,7 +306,17 @@
     return pl.ds(low, cols), pl.ds(high, cols), mine, other
 
 
-def project_kernel(h, own, from_x, weight, chunks, rows_all):
+def at_home(group, total, count):
+    return lax.axis_index("ang") // group == (1 - lax.axis_index("sy")) * (total - count) // group
+
+
+def owner_of(first, group, d, k):
+    me = lax.axis_index("ang")
+    return jnp.where(first, me ^ d ^ (k * group), me ^ d)
+
+
+def project_kernel(h, group, rims, own, from_x, weight, chunks, *outs_and_scratch):
+    outs, rows_all = outs_and_scratch[:-1], outs_and_scratch[-1]
     sx = lax.axis_index("sx")
     f32, bf16 = jnp.float32, jnp.bfloat16
     cols = own.shape[2] - BLK
@@ -316,30 +326,32 @@
         rows_all[c, :, mine] = own[c, :, 0:cols].astype(f32)
         rows_all[c, :, other] = from_x[c, :, 0:cols].astype(f32)
         rows_all[c, :, rim_mine] += own[c, :, cols:].astype(f32)
-        rows_all[c, :, rim_other] += from_x[c, :, cols:].astype(f32)
+        rows_all[c, :, rim_other] += from_x[c, :, cols : cols + BLK].astype(f32)
         rows = rows_all[c].astype(bf16)
         part = jnp.dot(rows, weight[...], preferred_element_type=f32)
         for j in range(count):
             chunks[j, c * h : (c + 1) * h, :] = part[j * h : (j + 1) * h]
+    home = at_home(group, count, rims)
+    for d, ref in enumerate(outs):
+        for k in range(1, count // group):
+            part = chunks[owner_of(home, group, d, k)]
+            ref[(k - 1) * 2 * h : k * 2 * h, :] = part.astype(ref.dtype)
 
 
 def rim_kernel(
-    h, group, from_y, from_d, weight, chunks, to_core, *outs_and_scratch
+    h, group, after, from_y, from_d, weight, chunks, *outs_and_scratch
 ):
     outs, (rows_all, pieces) = outs_and_scratch[:-2], outs_and_scratch[-2:]
-    sy, sx, me = lax.axis_index("sy"), lax.axis_index("sx"), lax.axis_index("ang")
+    sy, sx = lax.axis_index("sy"), lax.axis_index("sx")
     f32, bf16 = jnp.float32, jnp.bfloat16
     cols = from_y.shape[2] - BLK
     count = from_y.shape[1] // h
     mine, other, rim_mine, rim_other = column_cuts(sx, cols)
-    edge = pl.ds(aligned(sx * (cols - BLK), BLK), BLK)
     for c in range(2):
         rows_all[c, :, mine] = from_y[c, :, 0:cols].astype(f32)
         rows_all[c, :, other] = from_d[c, :, 0:cols].astype(f32)
         rows_all[c, :, rim_mine] += from_y[c, :, cols:].astype(f32)
         rows_all[c, :, rim_other] += from_d[c, :, cols:].astype(f32)
-        to_core[c] = from_d[c, :, 0:cols]
-        to_core[c, :, edge] = (from_d[c, :, edge].astype(f32) + from_y[c, :, cols:].astype(f32)).astype(bf16)
     rows = rows_all[...].reshape(2 * count * h, 2 * cols).astype(bf16)
     part = jnp.dot(rows, weight[...], preferred_element_type=f32)
     for c in range(2):
@@ -348,20 +360,17 @@
             pieces[q, c * h : (c + 1) * h, :] = part[row : row + h]
     total = chunks.shape[0]
     base = (1 - sy) * (total - count)
-
-    def piece(owner):
-        rel = owner - base
-        found = pieces[jnp.clip(rel, 0, count - 1)]
-        return chunks[owner] + jnp.where((rel >= 0) & (rel < count), found, jnp.zeros_like(found))
-
-    for d in range(group):
-        outs[d][...] = piece(me ^ d).astype(outs[d].dtype)
-        far = outs[group + d]
+    away = jnp.logical_not(at_home(group, total, count))
+    for d, ref in enumerate(outs):
         for k in range(1, total // group):
-            far[(k - 1) * 2 * h : k * 2 * h, :] = piece(me ^ d ^ (k * group)).astype(far.dtype)
-
-
-def fold_kernel(h, grad, from_x, rim_x, from_y, from_d, from_core, out):
+            owner = owner_of(away, group, d, k)
+            rel = owner - base
+            found = pieces[jnp.clip(rel, 0, count - 1)]
+            part = chunks[owner] + jnp.where((rel >= 0) & (rel < count), found, jnp.zeros_like(found))
+            ref[(k - 1) * 2 * h : k * 2 * h, :] = part.astype(ref.dtype)
+
+
+def fold_kernel(h, grad, from_x, from_y, from_d, from_core, out):
     sy, sx = lax.axis_index("sy"), lax.axis_index("sx")
     f32 = jnp.float32
     rows, cols = grad.shape[1], grad.shape[2]
@@ -370,26 +379,42 @@
     every = pl.ds(0, cols)
     for c in range(2):
         out[c] = grad[c]
-        add_strips(out, c, 0, rows, edge, sx, h, from_x[c, :, cols:].astype(f32))
-        add_strips(out, c, 0, rows, edge, 1 - sx, h, rim_x[c].astype(f32))
+        add_strips(out, c, 0, rows, edge, sx, h, from_x[c, :, cols : cols + BLK].astype(f32))
+        add_strips(out, c, 0, rows, edge, 1 - sx, h, from_x[c, :, cols + BLK : cols + 2 * BLK].astype(f32))
         add_strips(out, c, row, RIM, every, sx, h, from_y[c, :, 0:cols].astype(f32))
         add_strips(out, c, row, RIM, edge, sx, h, from_d[c, :, cols:].astype(f32))
         add_strips(out, c, row, RIM, every, 1 - sx, h, from_core[c].astype(f32))
 
 
-def far_kernel(*refs):
-    out = refs[-1]
+def add(refs):
     total = refs[0][...]
-    for ref in refs[1:-1]:
+    for ref in refs[1:]:
         total += ref[...].astype(jnp.float32)
-    out[...] = total.astype(out.dtype)
-
-
-def probe_sum_kernel(kept, received, after, out):
+    return total
+
+
+def early_kernel(*refs):
+    refs[-1][...] = add(refs[:-1])
+
+
+def group_kernel(group, total, rims, from_y, from_d, early, *refs):
+    late, (across, near, to_core) = refs[:group], refs[group:]
+    first, second = early[...], add(late)
+    home = at_home(group, total, rims)
+    across[...] = jnp.where(home, first, second).astype(across.dtype)
+    near[...] = jnp.where(home, second, first)[: near.shape[0]]
+    cols = to_core.shape[2]
+    edge = pl.ds(aligned(lax.axis_index("sx") * (cols - BLK), BLK), BLK)
+    to_core[...] = from_d[:, :, 0:cols]
+    at_edge = from_d[:, :, edge].astype(jnp.float32) + from_y[:, :, cols:].astype(jnp.float32)
+    to_core[:, :, edge] = at_edge.astype(to_core.dtype)
+
+
+def probe_sum_kernel(after, kept, received, out):
     out[...] = (kept[...].astype(jnp.float32) + received[...].astype(jnp.float32)).astype(out.dtype)
 
 
-def last_kernel(h, *refs):
+def last_kernel(h, after, *refs):
     out = refs[-1]
     total = refs[0][...]
     for ref in refs[1:-1]:
@@ -453,13 +478,12 @@
     )
 
     wide = cols + BLK
-    grad, own, to_x, rim_x, to_y, to_d, probe_here = call(
+    grad, own, to_x, to_y, to_d, probe_here = call(
         partial(patch_kernel, h),
         (
             shape((2, rows, cols), f32),
             shape((2, strip_rows, wide)),
-            shape((2, strip_rows, wide)),
-            shape((2, strip_rows, BLK)),
+            shape((2, strip_rows, wide + BLK)),
             shape((2, RIM // 2, wide)),
             shape((2, RIM // 2, wide)),
             shape((modes, 2, PATCH, PATCH)),
@@ -478,54 +502,56 @@
     )
 
     from_x = lax.ppermute(to_x, "sx", SWAP)
+    probe_x = lax.ppermute(probe_here, "sx", SWAP)
     from_y = lax.ppermute(to_y, "sy", SWAP)
     from_d = lax.ppermute(to_d, ("sy", "sx"), CROSS)
-    from_rim = lax.ppermute(rim_x, "sx", SWAP)
-    probe_x = lax.ppermute(probe_here, "sx", SWAP)
-
-    chunks = call(
-        partial(project_kernel, h),
-        shape((n, 2 * h, width), f32),
+
+    far = n // group - 1
+    rims = RIM // (2 * h)
+    parts = (shape((far * 2 * h, width), f32),) + (shape((far * 2 * h, width)),) * (group - 1)
+    chunks, *early = call(
+        partial(project_kernel, h, group, rims),
+        (shape((n, 2 * h, width), f32),) + parts,
         (own, from_x, weight),
         [VMEM] * 3,
         [pltpu.VMEM((2, strip_rows, width), f32)],
         flops=4 * strip_rows * width * width, moved=8 * MIB,
     )
-    far = n // group - 1
-    outs = call(
+    probe_here = call(
+        probe_sum_kernel, shape((modes, 2, PATCH, PATCH)), (chunks, probe_here, probe_x),
+        [ANY, VMEM, VMEM], moved=MIB,
+    )
+    late = call(
         partial(rim_kernel, h, group),
-        (shape((2, RIM // 2, cols)), shape((2 * h, width), f32))
-        + (shape((2 * h, width)),) * (group - 1)
-        + (shape((far * 2 * h, width), f32),)
-        + (shape((far * 2 * h, width)),) * (group - 1),
-        (from_y, from_d, weight, chunks),
-        [VMEM] * 4,
-        [pltpu.VMEM((2, RIM // 2, width), f32), pltpu.VMEM((RIM // (2 * h), 2 * h, width), f32)],
-        flops=2 * RIM * width * width, moved=4 * MIB,
-    )
-    to_core, near, away = outs[0], outs[1 : 1 + group], outs[1 + group :]
+        parts,
+        (probe_here, from_y, from_d, weight, chunks),
+        [ANY] + [VMEM] * 4,
+        [pltpu.VMEM((2, RIM // 2, width), f32), pltpu.VMEM((rims, 2 * h, width), f32)],
+        flops=12 * width**3, moved=4 * MIB,
+    )
 
     def swap(array, d):
         return lax.ppermute(array, "ang", [(i, i ^ d) for i in range(n)])
 
-    got = [swap(away[d], d) for d in range(group - 1, 0, -1)]
-    near_got = [swap(near[d], d) for d in range(group - 1, 0, -1)]
-    across = call(
-        far_kernel, shape((far * 2 * h, width)), [away[0]] + got, [VMEM] * group, moved=MIB,
+    order = range(1, group)
+    late_here, late = late[0], list(late)
+    early[1:] = [swap(early[d], d) for d in order]
+    late[1:] = [swap(late[d], d) for d in order]
+    early = call(early_kernel, parts[0], early, [VMEM] * group, flops=16 * width**3 // 4, moved=MIB)
+    across, near, to_core = call(
+        partial(group_kernel, group, n, rims),
+        (shape((far * 2 * h, width)), shape((2 * h, width), f32), shape((2, RIM // 2, cols))),
+        [from_y, from_d, early] + late, [VMEM] * (3 + group), moved=MIB,
     )
     across_got = [swap(across[(k - 1) * 2 * h : k * 2 * h], k * group) for k in range(1, far + 1)]
 
-    probe_here = call(
-        probe_sum_kernel, shape((modes, 2, PATCH, PATCH)), (probe_here, probe_x, to_core),
-        [VMEM, VMEM, ANY], moved=MIB,
-    )
     probe_y = lax.ppermute(probe_here, "sy", SWAP)
     from_core = lax.ppermute(to_core, "sx", SWAP)
     object_grad = call(
         partial(fold_kernel, h),
         shape((2, rows, cols), f32),
-        (grad, from_x, from_rim, from_y, from_d, from_core),
-        [VMEM] * 6, moved=6 * MIB,
+        (grad, from_x, from_y, from_d, from_core),
+        [VMEM] * 5, moved=6 * MIB,
     )
     probe_grad = call(
         partial(probe_kernel, 1.0 / math.sqrt(patches * tiles)),
@@ -536,8 +562,8 @@
     vol = call(
         partial(last_kernel, h),
         shape((h, 2, width), f32),
-        [near[0]] + near_got + across_got,
-        [VMEM] * (group + far), moved=MIB,
+        [probe_grad, near] + across_got,
+        [HBM] + [VMEM] * (1 + far), moved=MIB,
     )
     return (object_grad[None], probe_grad[None], vol[None])
 

time: 45.3 us -> 43.2 us (0.954)
  waiting for transfers between devices: 12.5 us -> 9.19 us
  starting transfers between devices: 15.6 us -> 16.8 us
    ppermute x1, waiting for transfers between devices: 1.79 us -> 0.01 us  [body(): from_d = lax.ppermute(to_d, ('sy', 'sx'), CROSS)]
    ppermute x7, waiting for transfers between devices: 8.83 us -> 7.35 us  [swap(): return lax.ppermute(array, 'ang', [(i, i ^ d) for i in range(n)])]
    ppermute x1, waiting for transfers between devices: 1.4 us -> 0.01 us  [body(): from_y = lax.ppermute(to_y, 'sy', SWAP)]
    ppermute x1, waiting for transfers between devices: 0.01 us -> 1.25 us  [body(): from_core = lax.ppermute(to_core, 'sx', SWAP)]
    ppermute x1, starting transfers between devices: 0.65 us -> 1.61 us  [body(): probe_y = lax.ppermute(probe_here, 'sy', SWAP)]
    pallas_call x11 -> x12, Pallas kernels: 16.3 us -> 16.2 us  [call(): pl.pallas_call(kernel, out_shape=outs, in_specs=specs, out_specs=jax.tree...]
  transfers between devices with their start and end apart: 17 -> 16, of which waited for: 8 -> 7; matrix products, arithmetic and copies ran while one was open for 0% -> 0% of each run, Pallas kernels for 22% -> 24%
where the time goes in v3:
time: 43.2 us; the launch traced here: 42.9 us
  starting transfers between devices  16.8 us (39%)
  Pallas kernels  16.2 us (38%)
  waiting for transfers between devices  9.19 us (21%)
  between operations  0.73 us (2%)
    pallas_call x12, Pallas kernels, call(): pl.pallas_call(kernel, out_shape=outs, in_specs=specs, out_specs=jax.tree...  16.2 us
    ppermute x7, starting transfers between devices, swap(): return lax.ppermute(array, 'ang', [(i, i ^ d) for i in range(n)])  9.83 us
    ppermute x7, waiting for transfers between devices, swap(): return lax.ppermute(array, 'ang', [(i, i ^ d) for i in range(n)])  7.35 us
    ppermute x1, starting transfers between devices, body(): halo_d = lax.ppermute(to_d, ('sy', 'sx'), CROSS)  2.64 us
    ppermute x1, starting transfers between devices, body(): probe_y = lax.ppermute(probe_here, 'sy', SWAP)  1.61 us
    ppermute x1, starting transfers between devices, body(): from_y = lax.ppermute(to_y, 'sy', SWAP)  1.54 us
    ppermute x1, waiting for transfers between devices, body(): from_core = lax.ppermute(to_core, 'sx', SWAP)  1.25 us
  transfers between devices with their start and end apart: 16, of which 7 were waited for; matrix products, arithmetic and copies ran while one was open for 0% of the time, Pallas kernels for 24%

profile of v3, /device:TPU:0, one launch (start us, length us, event | category | flops | bytes accessed | tf_op | source)
XLA Modules:
  0.0 42.9 jit_solution(17655904845577596720)
XLA Ops:
  0.6 1.1 %shard_map.105 = (bf16[2,64,512]{2,1,0:T(8,128)(2,1)S(1)}, bf16[2,512,128]{2,1,0:T(8,128)(2,1)S(1)}, bf16[2,64,128]{2,1,0:T(8,128)(2,1)S(1)}) custom-call(bf16[2,512,512]{2,1,0:T(8,128)(2,1)} %bitcast.8), custom_call_target="tpu_custom_call" | custom-call | bytes 2097152 | tf_op jit(solution)/shard_map/pallas_call | solution.py:53
  1.8 0.5 %collective-permute-start.1 = (bf16[2,512,128]{2,1,0:T(8,128)(2,1)S(1)}, bf16[2,512,128]{2,1,0:T(8,128)(2,1)S(1)}, u32[]{:S(2)}, u32[]{:S(2)}) collective-permute-start(bf16[2,512,128]{2,1,0:T(8,128)(2,1)S(1)} %get-tuple-element.32), channel_id=1, source_target_pairs={{0,1},{1,0},{2,3},{3,2},{4,5},{5,4},{6,7},{7,6},{8,9},{9,8},{10,11... | collective-permute-start | bytes 786440 | tf_op jit(solution)/shard_map/ppermute | solution.py:452
  2.3 2.6 %collective-permute-start.2 = (bf16[2,64,128]{2,1,0:T(8,128)(2,1)S(1)}, bf16[2,64,128]{2,1,0:T(8,128)(2,1)S(1)}, u32[]{:S(2)}, u32[]{:S(2)}) collective-permute-start(bf16[2,64,128]{2,1,0:T(8,128)(2,1)S(1)} %get-tuple-element.33), channel_id=1, source_target_pairs={{0,3},{3,0},{1,2},{2,1},{4,7},{7,4},{5,6},{6,5},{8,11},{11,8},{9,1... | collective-permute-start | bytes 98312 | tf_op jit(solution)/shard_map/ppermute | solution.py:451
  4.9 0.0 copy-start
  4.9 0.1 collective-permute-start
  5.0 2.7 %shard_map.103.matrix = bf16[1024,1024]{1,0:T(8,128)(2,1)S(1)} custom-call(s32[8,16]{1,0:T(8,128)} %index.1, bf16[8,16,128,128]{3,2,1,0:T(8,128)(2,1)} %values.1), custom_call_target="tpu_custom_call" | custom-call | flops 1048576 | bytes 4194304 | tf_op jit(solution)/shard_map/pallas_call | solution.py:53
  7.7 0.0 copy-done
  7.7 2.4 %shard_map.104 = (bf16[1024,1024]{1,0:T(8,128)(2,1)S(1)}, bf16[2,512,512]{2,1,0:T(8,128)(2,1)S(1)}, f32[2,2,256,256]{3,2,1,0:T(8,128)S(1)}, bf16[2,256,256]{2,1,0:T(8,128)(2,1)S(1)}, bf16[2,512,512]{2,1,0:T(8,128)(2,1)S(1)}) custom-call(bf16[1024,1024]{1,0:T(8,128)(2,1)S(1)} %shard_map.103.matrix, bf16[128,1920]{1,0:T(8,128)(2,1)S(1)} %copy-done, ...), custom_call_target="tpu_custom_call" | custom-call | flops 2147483648 | bytes 6291456 | tf_op jit(solution)/shard_map/pallas_call | solution.py:53
  10.1 0.0 collective-permute-done.2.from_d
  10.1 0.3 collective-permute-done.from_y
  10.4 0.0 collective-permute-done.1.from_x
  10.4 4.2 %shard_map.106 = (f32[2,512,512]{2,1,0:T(8,128)S(1)}, bf16[2,256,640]{2,1,0:T(8,128)(2,1)S(1)}, bf16[2,256,768]{2,1,0:T(8,128)(2,1)S(1)}, bf16[2,32,640]{2,1,0:T...) custom-call(s32[2,2]{1,0:T(2,128)} %bitcast.12, ...), custom_call_target="tpu_custom_call" | custom-call | flops 2147483648 | bytes 8388608 | tf_op jit(solution)/shard_map/pallas_call | solution.py:53
  14.6 0.1 collective-permute-start.3
  14.7 0.5 %collective-permute-start.9 = (bf16[2,2,256,256]{3,2,1,0:T(8,128)(2,1)S(1)}, bf16[2,2,256,256]{3,2,1,0:T(8,128)(2,1)S(1)}, u32[]{:S(2)}, u32[]{:S(2)}) collective-permute-start(bf16[2,2,256,256]{3,2,1,0:T(8,128)(2,1)S(1)} %get-tuple-element.47.kept), channel_id=1, source_target_pairs={{0,1},{1,0},{2,3},{3,2},{4,5},{5,4},{6,7},{7,6},{8,9},{9,8},{10,11... | collective-permute-start | bytes 1572872 | tf_op jit(solution)/shard_map/ppermute | solution.py:505
  15.2 1.5 %collective-permute-start.4 = (bf16[2,32,640]{2,1,0:T(8,128)(2,1)S(1)}, bf16[2,32,640]{2,1,0:T(8,128)(2,1)S(1)}, u32[]{:S(2)}, u32[]{:S(2)}) collective-permute-start(bf16[2,32,640]{2,1,0:T(8,128)(2,1)S(1)} %get-tuple-element.39), channel_id=1, source_target_pairs={{0,2},{2,0},{1,3},{3,1},{4,6},{6,4},{5,7},{7,5},{8,10},{10,8},{9,1... | collective-permute-start | bytes 245768 | tf_op jit(solution)/shard_map/ppermute | solution.py:506
  16.8 0.0 collective-permute-start.5
  16.8 0.2 collective-permute-done.3.from_x
  17.0 1.5 %shard_map.107 = (f32[8,64,1024]{2,1,0:T(8,128)S(1)}, f32[64,1024]{1,0:T(8,128)S(1)}, bf16[64,1024]{1,0:T(8,128)(2,1)S(1)}, bf16[64,1024]{1,0:T(8,128)(2,1)S(1)}, bf16[64,1024]{1,0:T(8,128)(2,1)S(1)}) custom-call(bf16[2,256,640]{2,1,0:T(8,128)(2,1)S(1)} %get-tuple-element.41.own, bf16[2,256,768]{2,1,0:T(8,128)(2,1)S(1)} %collective-permute-done.3.from_x, ...), custom_call_target="tpu_custom_call" | custom-call | flops 1073741824 | bytes 8388608 | tf_op jit(solution)/shard_map/pallas_call | solution.py:53
  18.5 1.6 %collective-permute-start.6 = (bf16[64,1024]{1,0:T(8,128)(2,1)S(1)}, bf16[64,1024]{1,0:T(8,128)(2,1)S(1)}, u32[]{:S(2)}, u32[]{:S(2)}) collective-permute-start(bf16[64,1024]{1,0:T(8,128)(2,1)S(1)} %get-tuple-element.43), channel_id=1, source_target_pairs={{0,4},{4,0},{8,12},{12,8},{16,20},{20,16},{24,28},{28,24},{1,5},{5... | collective-permute-start | bytes 393224 | tf_op jit(solution)/shard_map/ppermute | solution.py:534
  20.1 1.6 %collective-permute-start.7 = (bf16[64,1024]{1,0:T(8,128)(2,1)S(1)}, bf16[64,1024]{1,0:T(8,128)(2,1)S(1)}, u32[]{:S(2)}, u32[]{:S(2)}) collective-permute-start(bf16[64,1024]{1,0:T(8,128)(2,1)S(1)} %get-tuple-element.44), channel_id=1, source_target_pairs={{0,8},{4,12},{8,0},{12,4},{16,24},{20,28},{24,16},{28,20},{1,9},{5... | collective-permute-start | bytes 393224 | tf_op jit(solution)/shard_map/ppermute | solution.py:534
  21.6 0.0 collective-permute-done.9.received
  21.6 0.4 collective-permute-start.8
  22.1 0.1 shard_map.109.after.mine
  22.2 0.0 collective-permute-done.4.from_y
  22.2 1.6 %collective-permute-start.14 = (bf16[2,2,256,256]{3,2,1,0:T(8,128)(2,1)S(1)}, bf16[2,2,256,256]{3,2,1,0:T(8,128)(2,1)S(1)}, u32[]{:S(2)}, u32[]{:S(2)}) collective-permute-start(bf16[2,2,256,256]{3,2,1,0:T(8,128)(2,1)S(1)} %shard_map.109.after.mine), channel_id=1, source_target_pairs={{0,2},{2,0},{1,3},{3,1},{4,6},{6,4},{5,7},{7,5},{8,10},{10,8},{9,1... | collective-permute-start | bytes 1572872 | tf_op jit(solution)/shard_map/ppermute | solution.py:548
  23.8 0.0 collective-permute-done.5.from_d
  23.8 0.5 %shard_map.110 = (f32[64,1024]{1,0:T(8,128)S(1)}, bf16[64,1024]{1,0:T(8,128)(2,1)S(1)}, bf16[64,1024]{1,0:T(8,128)(2,1)S(1)}, bf16[64,1024]{1,0:T(8,128)(2,1)S(1)}) custom-call(bf16[2,2,256,256]{3,2,1,0:T(8,128)(2,1)S(1)} %shard_map.109.after.mine, bf16[2,32,640]{2,1,0:T(8,128)(2,1)S(1)} %collective-permute-done.4.from_y, ...), custom_call_target="tpu_custom_call" | custom-call | flops 12884901888 | bytes 4194304 | tf_op jit(solution)/shard_map/pallas_call | solution.py:53
  24.4 1.5 %collective-permute-start.10 = (bf16[64,1024]{1,0:T(8,128)(2,1)S(1)}, bf16[64,1024]{1,0:T(8,128)(2,1)S(1)}, u32[]{:S(2)}, u32[]{:S(2)}) collective-permute-start(bf16[64,1024]{1,0:T(8,128)(2,1)S(1)} %get-tuple-element.49), channel_id=1, source_target_pairs={{0,4},{4,0},{8,12},{12,8},{16,20},{20,16},{24,28},{28,24},{1,5},{5... | collective-permute-start | bytes 393224 | tf_op jit(solution)/shard_map/ppermute | solution.py:534
  25.9 0.0 collective-permute-done.6.refs_1_
  25.9 1.6 %collective-permute-start.11 = (bf16[64,1024]{1,0:T(8,128)(2,1)S(1)}, bf16[64,1024]{1,0:T(8,128)(2,1)S(1)}, u32[]{:S(2)}, u32[]{:S(2)}) collective-permute-start(bf16[64,1024]{1,0:T(8,128)(2,1)S(1)} %get-tuple-element.50), channel_id=1, source_target_pairs={{0,8},{4,12},{8,0},{12,4},{16,24},{20,28},{24,16},{28,20},{1,9},{5... | collective-permute-start | bytes 393224 | tf_op jit(solution)/shard_map/ppermute | solution.py:534
  27.5 0.0 collective-permute-done.7.refs_2_
  27.5 0.5 %collective-permute-start.12 = (bf16[64,1024]{1,0:T(8,128)(2,1)S(1)}, bf16[64,1024]{1,0:T(8,128)(2,1)S(1)}, u32[]{:S(2)}, u32[]{:S(2)}) collective-permute-start(bf16[64,1024]{1,0:T(8,128)(2,1)S(1)} %get-tuple-element.51), channel_id=1, source_target_pairs={{0,12},{4,8},{8,4},{12,0},{16,28},{20,24},{24,20},{28,16},{1,13},{... | collective-permute-start | bytes 393224 | tf_op jit(solution)/shard_map/ppermute | solution.py:534
  28.0 1.0 %collective-permute-done.8.refs_3_ = bf16[64,1024]{1,0:T(8,128)(2,1)S(1)} collective-permute-done((bf16[64,1024]{1,0:T(8,128)(2,1)S(1)}, bf16[64,1024]{1,0:T(8,128)(2,1)S(1)}, u32[]{:S(2)}, u32[]{:S(2)}) %collective-permute-start.8) | collective-permute-done | bytes 131104 | tf_op jit(solution)/shard_map/ppermute | solution.py:534
  28.9 0.1 shard_map.108.early
  29.0 3.3 %collective-permute-done.10.refs_1_ = bf16[64,1024]{1,0:T(8,128)(2,1)S(1)} collective-permute-done((bf16[64,1024]{1,0:T(8,128)(2,1)S(1)}, bf16[64,1024]{1,0:T(8,128)(2,1)S(1)}, u32[]{:S(2)}, u32[]{:S(2)}) %collective-permute-start.10) | collective-permute-done | bytes 131104 | tf_op jit(solution)/shard_map/ppermute | solution.py:534
  32.3 0.0 collective-permute-done.11.refs_2_
  32.3 1.6 %collective-permute-done.12.refs_3_ = bf16[64,1024]{1,0:T(8,128)(2,1)S(1)} collective-permute-done((bf16[64,1024]{1,0:T(8,128)(2,1)S(1)}, bf16[64,1024]{1,0:T(8,128)(2,1)S(1)}, u32[]{:S(2)}, u32[]{:S(2)}) %collective-permute-start.12) | collective-permute-done | bytes 131104 | tf_op jit(solution)/shard_map/ppermute | solution.py:534
  34.0 0.1 shard_map.111
  34.0 2.7 %collective-permute-start.15 = (bf16[64,1024]{1,0:T(8,128)(2,1)S(1)}, bf16[64,1024]{1,0:T(8,128)(2,1)S(1)}, u32[]{:S(2)}, u32[]{:S(2)}) collective-permute-start(bf16[64,1024]{1,0:T(8,128)(2,1)S(1)} %get-tuple-element.54), channel_id=1, source_target_pairs={{0,16},{4,20},{8,24},{12,28},{16,0},{20,4},{24,8},{28,12},{1,17},{... | collective-permute-start | bytes 393224 | tf_op jit(solution)/shard_map/ppermute | solution.py:534
  36.7 0.0 collective-permute-start.13
  36.7 1.3 %collective-permute-done.13.from_core = bf16[2,32,512]{2,1,0:T(8,128)(2,1)S(1)} collective-permute-done((bf16[2,32,512]{2,1,0:T(8,128)(2,1)S(1)}, bf16[2,32,512]{2,1,0:T(8,128)(2,1)S(1)}, u32[]{:S(2)}, u32[]{:S(2)}) %collective-permute-start.13) | collective-permute-done | bytes 65568 | tf_op jit(solution)/shard_map/ppermute | solution.py:549
  38.0 1.7 %shard_map.112 = f32[2,512,512]{2,1,0:T(8,128)} custom-call(f32[2,512,512]{2,1,0:T(8,128)S(1)} %get-tuple-element.37.grad, bf16[2,256,768]{2,1,0:T(8,128)(2,1)S(1)} %collective-permute-done.3.from_x, bf16[2,32,640]{2,1,0:T(8,128)(2,1)S(1)} %collective-permute-done.4.from_y, bf16[2,32,640]{2,1,0:T(8,128)(2,1)S(1)} %collective-permute-done.5.from_d, ...), custom_call_target="tpu_custom_call" | custom-call | bytes 6291456 | tf_op jit(solution)/shard_map/pallas_call | solution.py:53
  39.6 0.0 collective-permute-done.14.other
  39.6 1.1 %shard_map.113.after = f32[2,2,256,256]{3,2,1,0:T(8,128)} custom-call(bf16[2,2,256,256]{3,2,1,0:T(8,128)(2,1)S(1)} %shard_map.109.after.mine, bf16[2,2,256,256]{3,2,1,0:T(8,128)(2,1)S(1)} %collective-permute-done.14.other), custom_call_target="tpu_custom_call" | custom-call | bytes 2097152 | tf_op jit(solution)/shard_map/pallas_call | solution.py:53
  40.8 1.4 %collective-permute-done.15.refs_1_ = bf16[64,1024]{1,0:T(8,128)(2,1)S(1)} collective-permute-done((bf16[64,1024]{1,0:T(8,128)(2,1)S(1)}, bf16[64,1024]{1,0:T(8,128)(2,1)S(1)}, u32[]{:S(2)}, u32[]{:S(2)}) %collective-permute-start.15) | collective-permute-done | bytes 131104 | tf_op jit(solution)/shard_map/ppermute | solution.py:534
  42.2 0.8 %shard_map.114 = f32[32,2,1024]{2,1,0:T(2,128)} custom-call(f32[2,2,256,256]{3,2,1,0:T(8,128)} %shard_map.113.after, f32[64,1024]{1,0:T(8,128)S(1)} %get-tuple-element.53.refs_0_, bf16[64,1024]{1,0:T(8,128)(2,1)S(1)} %collective-permute-done.15.refs_1_), custom_call_target="tpu_custom_call" | custom-call | bytes 1048576 | tf_op jit(solution)/shard_map/pallas_call | solution.py:53
Async XLA Ops:
  1.8 8.6 %collective-permute-start.1 = (bf16[2,512,128]{2,1,0:T(8,128)(2,1)S(1)}, bf16[2,512,128]{2,1,0:T(8,128)(2,1)S(1)}, u32[]{:S(2)}, u32[]{:S(2)}) collective-permute-start(bf16[2,512,128]{2,1,0:T(8,128)(2,1)S(1)} %get-tuple-element.32), channel_id=1, source_target_pairs={{0,1},{1,0},{2,3},{3,2},{4,5},{5,4},{6,7},{7,6},{8,9},{9,8},{10,11... | collective-permute-start | bytes 786440 | tf_op jit(solution)/shard_map/ppermute | solution.py:452
  2.3 7.8 %collective-permute-start.2 = (bf16[2,64,128]{2,1,0:T(8,128)(2,1)S(1)}, bf16[2,64,128]{2,1,0:T(8,128)(2,1)S(1)}, u32[]{:S(2)}, u32[]{:S(2)}) collective-permute-start(bf16[2,64,128]{2,1,0:T(8,128)(2,1)S(1)} %get-tuple-element.33), channel_id=1, source_target_pairs={{0,3},{3,0},{1,2},{2,1},{4,7},{7,4},{5,6},{6,5},{8,11},{11,8},{9,1... | collective-permute-start | bytes 98312 | tf_op jit(solution)/shard_map/ppermute | solution.py:451
  4.9 2.7 %copy-start = (bf16[128,1920]{1,0:T(8,128)(2,1)S(1)}, bf16[128,1920]{1,0:T(8,128)(2,1)}, u32[]{:S(2)}) copy-start(bf16[128,1920]{1,0:T(8,128)(2,1)} %constant.5.clone.strip) | copy-start | bytes 1474564
  4.9 5.5 %collective-permute-start = (bf16[2,64,512]{2,1,0:T(8,128)(2,1)S(1)}, bf16[2,64,512]{2,1,0:T(8,128)(2,1)S(1)}, u32[]{:S(2)}, u32[]{:S(2)}) collective-permute-start(bf16[2,64,512]{2,1,0:T(8,128)(2,1)S(1)} %get-tuple-element.31), channel_id=1, source_target_pairs={{0,2},{2,0},{1,3},{3,1},{4,6},{6,4},{5,7},{7,5},{8,10},{10,8},{9,1... | collective-permute-start | bytes 393224 | tf_op jit(solution)/shard_map/ppermute | solution.py:450
  14.6 2.4 %collective-permute-start.3 = (bf16[2,256,768]{2,1,0:T(8,128)(2,1)S(1)}, bf16[2,256,768]{2,1,0:T(8,128)(2,1)S(1)}, u32[]{:S(2)}, u32[]{:S(2)}) collective-permute-start(bf16[2,256,768]{2,1,0:T(8,128)(2,1)S(1)} %get-tuple-element.38), channel_id=1, source_target_pairs={{0,1},{1,0},{2,3},{3,2},{4,5},{5,4},{6,7},{7,6},{8,9},{9,8},{10,11... | collective-permute-start | bytes 2359304 | tf_op jit(solution)/shard_map/ppermute | solution.py:504
  14.7 6.9 %collective-permute-start.9 = (bf16[2,2,256,256]{3,2,1,0:T(8,128)(2,1)S(1)}, bf16[2,2,256,256]{3,2,1,0:T(8,128)(2,1)S(1)}, u32[]{:S(2)}, u32[]{:S(2)}) collective-permute-start(bf16[2,2,256,256]{3,2,1,0:T(8,128)(2,1)S(1)} %get-tuple-element.47.kept), channel_id=1, source_target_pairs={{0,1},{1,0},{2,3},{3,2},{4,5},{5,4},{6,7},{7,6},{8,9},{9,8},{10,11... | collective-permute-start | bytes 1572872 | tf_op jit(solution)/shard_map/ppermute | solution.py:505
  15.2 7.0 %collective-permute-start.4 = (bf16[2,32,640]{2,1,0:T(8,128)(2,1)S(1)}, bf16[2,32,640]{2,1,0:T(8,128)(2,1)S(1)}, u32[]{:S(2)}, u32[]{:S(2)}) collective-permute-start(bf16[2,32,640]{2,1,0:T(8,128)(2,1)S(1)} %get-tuple-element.39), channel_id=1, source_target_pairs={{0,2},{2,0},{1,3},{3,1},{4,6},{6,4},{5,7},{7,5},{8,10},{10,8},{9,1... | collective-permute-start | bytes 245768 | tf_op jit(solution)/shard_map/ppermute | solution.py:506
  16.8 7.1 %collective-permute-start.5 = (bf16[2,32,640]{2,1,0:T(8,128)(2,1)S(1)}, bf16[2,32,640]{2,1,0:T(8,128)(2,1)S(1)}, u32[]{:S(2)}, u32[]{:S(2)}) collective-permute-start(bf16[2,32,640]{2,1,0:T(8,128)(2,1)S(1)} %get-tuple-element.40), channel_id=1, source_target_pairs={{0,3},{3,0},{1,2},{2,1},{4,7},{7,4},{5,6},{6,5},{8,11},{11,8},{9,1... | collective-permute-start | bytes 245768 | tf_op jit(solution)/shard_map/ppermute | solution.py:507
  18.5 7.4 %collective-permute-start.6 = (bf16[64,1024]{1,0:T(8,128)(2,1)S(1)}, bf16[64,1024]{1,0:T(8,128)(2,1)S(1)}, u32[]{:S(2)}, u32[]{:S(2)}) collective-permute-start(bf16[64,1024]{1,0:T(8,128)(2,1)S(1)} %get-tuple-element.43), channel_id=1, source_target_pairs={{0,4},{4,0},{8,12},{12,8},{16,20},{20,16},{24,28},{28,24},{1,5},{5... | collective-permute-start | bytes 393224 | tf_op jit(solution)/shard_map/ppermute | solution.py:534
  20.1 7.4 %collective-permute-start.7 = (bf16[64,1024]{1,0:T(8,128)(2,1)S(1)}, bf16[64,1024]{1,0:T(8,128)(2,1)S(1)}, u32[]{:S(2)}, u32[]{:S(2)}) collective-permute-start(bf16[64,1024]{1,0:T(8,128)(2,1)S(1)} %get-tuple-element.44), channel_id=1, source_target_pairs={{0,8},{4,12},{8,0},{12,4},{16,24},{20,28},{24,16},{28,20},{1,9},{5... | collective-permute-start | bytes 393224 | tf_op jit(solution)/shard_map/ppermute | solution.py:534
  21.6 7.3 %collective-permute-start.8 = (bf16[64,1024]{1,0:T(8,128)(2,1)S(1)}, bf16[64,1024]{1,0:T(8,128)(2,1)S(1)}, u32[]{:S(2)}, u32[]{:S(2)}) collective-permute-start(bf16[64,1024]{1,0:T(8,128)(2,1)S(1)} %get-tuple-element.45), channel_id=1, source_target_pairs={{0,12},{4,8},{8,4},{12,0},{16,28},{20,24},{24,20},{28,16},{1,13},{... | collective-permute-start | bytes 393224 | tf_op jit(solution)/shard_map/ppermute | solution.py:534
  22.2 17.4 %collective-permute-start.14 = (bf16[2,2,256,256]{3,2,1,0:T(8,128)(2,1)S(1)}, bf16[2,2,256,256]{3,2,1,0:T(8,128)(2,1)S(1)}, u32[]{:S(2)}, u32[]{:S(2)}) collective-permute-start(bf16[2,2,256,256]{3,2,1,0:T(8,128)(2,1)S(1)} %shard_map.109.after.mine), channel_id=1, source_target_pairs={{0,2},{2,0},{1,3},{3,1},{4,6},{6,4},{5,7},{7,5},{8,10},{10,8},{9,1... | collective-permute-start | bytes 1572872 | tf_op jit(solution)/shard_map/ppermute | solution.py:548
  24.4 8.0 %collective-permute-start.10 = (bf16[64,1024]{1,0:T(8,128)(2,1)S(1)}, bf16[64,1024]{1,0:T(8,128)(2,1)S(1)}, u32[]{:S(2)}, u32[]{:S(2)}) collective-permute-start(bf16[64,1024]{1,0:T(8,128)(2,1)S(1)} %get-tuple-element.49), channel_id=1, source_target_pairs={{0,4},{4,0},{8,12},{12,8},{16,20},{20,16},{24,28},{28,24},{1,5},{5... | collective-permute-start | bytes 393224 | tf_op jit(solution)/shard_map/ppermute | solution.py:534
  25.9 6.5 %collective-permute-start.11 = (bf16[64,1024]{1,0:T(8,128)(2,1)S(1)}, bf16[64,1024]{1,0:T(8,128)(2,1)S(1)}, u32[]{:S(2)}, u32[]{:S(2)}) collective-permute-start(bf16[64,1024]{1,0:T(8,128)(2,1)S(1)} %get-tuple-element.50), channel_id=1, source_target_pairs={{0,8},{4,12},{8,0},{12,4},{16,24},{20,28},{24,16},{28,20},{1,9},{5... | collective-permute-start | bytes 393224 | tf_op jit(solution)/shard_map/ppermute | solution.py:534
  27.5 6.5 %collective-permute-start.12 = (bf16[64,1024]{1,0:T(8,128)(2,1)S(1)}, bf16[64,1024]{1,0:T(8,128)(2,1)S(1)}, u32[]{:S(2)}, u32[]{:S(2)}) collective-permute-start(bf16[64,1024]{1,0:T(8,128)(2,1)S(1)} %get-tuple-element.51), channel_id=1, source_target_pairs={{0,12},{4,8},{8,4},{12,0},{16,28},{20,24},{24,20},{28,16},{1,13},{... | collective-permute-start | bytes 393224 | tf_op jit(solution)/shard_map/ppermute | solution.py:534
  34.0 8.1 %collective-permute-start.15 = (bf16[64,1024]{1,0:T(8,128)(2,1)S(1)}, bf16[64,1024]{1,0:T(8,128)(2,1)S(1)}, u32[]{:S(2)}, u32[]{:S(2)}) collective-permute-start(bf16[64,1024]{1,0:T(8,128)(2,1)S(1)} %get-tuple-element.54), channel_id=1, source_target_pairs={{0,16},{4,20},{8,24},{12,28},{16,0},{20,4},{24,8},{28,12},{1,17},{... | collective-permute-start | bytes 393224 | tf_op jit(solution)/shard_map/ppermute | solution.py:534
  36.7 1.3 %collective-permute-start.13 = (bf16[2,32,512]{2,1,0:T(8,128)(2,1)S(1)}, bf16[2,32,512]{2,1,0:T(8,128)(2,1)S(1)}, u32[]{:S(2)}, u32[]{:S(2)}) collective-permute-start(bf16[2,32,512]{2,1,0:T(8,128)(2,1)S(1)} %get-tuple-element.52), channel_id=1, source_target_pairs={{0,1},{1,0},{2,3},{3,2},{4,5},{5,4},{6,7},{7,6},{8,9},{9,8},{10,11... | collective-permute-start | bytes 196616 | tf_op jit(solution)/shard_map/ppermute | solution.py:549

commit v4 on v3

--- a/solution.py
+++ b/solution.py
@@ -315,31 +315,38 @@
     return jnp.where(first, me ^ d ^ (k * group), me ^ d)
 
 
-def project_kernel(h, group, rims, own, from_x, weight, chunks, *outs_and_scratch):
+def project_kernel(h, group, rims, half, after, own, from_x, weight, chunks, *outs_and_scratch):
     outs, rows_all = outs_and_scratch[:-1], outs_and_scratch[-1]
-    sx = lax.axis_index("sx")
+    sx, me = lax.axis_index("sx"), lax.axis_index("ang")
     f32, bf16 = jnp.float32, jnp.bfloat16
     cols = own.shape[2] - BLK
-    count = own.shape[1] // h
+    total = own.shape[1] // h
+    home = at_home(group, total, rims)
+    rows = rows_all.shape[1]
+    served = 0
+    if half is not None:
+        served = (me // group) ^ jnp.where(home, 1 - half, half)
+    at = pl.ds(aligned(served * rows, rows), rows)
     mine, other, rim_mine, rim_other = column_cuts(sx, cols)
     for c in range(2):
-        rows_all[c, :, mine] = own[c, :, 0:cols].astype(f32)
-        rows_all[c, :, other] = from_x[c, :, 0:cols].astype(f32)
-        rows_all[c, :, rim_mine] += own[c, :, cols:].astype(f32)
-        rows_all[c, :, rim_other] += from_x[c, :, cols : cols + BLK].astype(f32)
-        rows = rows_all[c].astype(bf16)
-        part = jnp.dot(rows, weight[...], preferred_element_type=f32)
-        for j in range(count):
-            chunks[j, c * h : (c + 1) * h, :] = part[j * h : (j + 1) * h]
-    home = at_home(group, count, rims)
+        rows_all[c, :, mine] = own[c, at, 0:cols].astype(f32)
+        rows_all[c, :, other] = from_x[c, at, 0:cols].astype(f32)
+        rows_all[c, :, rim_mine] += own[c, at, cols:].astype(f32)
+        rows_all[c, :, rim_other] += from_x[c, at, cols : cols + BLK].astype(f32)
+    stacked = rows_all[...].reshape(2 * rows, 2 * cols).astype(bf16)
+    part = jnp.dot(stacked, weight[...], preferred_element_type=f32)
+    for c in range(2):
+        for j in range(rows // h):
+            row = c * rows + j * h
+            chunks[j, c * h : (c + 1) * h, :] = part[row : row + h]
     for d, ref in enumerate(outs):
-        for k in range(1, count // group):
-            part = chunks[owner_of(home, group, d, k)]
-            ref[(k - 1) * 2 * h : k * 2 * h, :] = part.astype(ref.dtype)
+        for k in range(1, total // group):
+            owner = owner_of(home, group, d, k) - served * (rows // h)
+            ref[(k - 1) * 2 * h : k * 2 * h, :] = chunks[owner].astype(ref.dtype)
 
 
 def rim_kernel(
-    h, group, after, from_y, from_d, weight, chunks, *outs_and_scratch
+    h, group, total, after, from_y, from_d, weight, chunks, *outs_and_scratch
 ):
     outs, (rows_all, pieces) = outs_and_scratch[:-2], outs_and_scratch[-2:]
     sy, sx = lax.axis_index("sy"), lax.axis_index("sx")
@@ -358,7 +365,7 @@
         for q in range(count):
             row = (c * count + q) * h
             pieces[q, c * h : (c + 1) * h, :] = part[row : row + h]
-    total = chunks.shape[0]
+    held = chunks.shape[0]
     base = (1 - sy) * (total - count)
     away = jnp.logical_not(at_home(group, total, count))
     for d, ref in enumerate(outs):
@@ -366,7 +373,7 @@
             owner = owner_of(away, group, d, k)
             rel = owner - base
             found = pieces[jnp.clip(rel, 0, count - 1)]
-            part = chunks[owner] + jnp.where((rel >= 0) & (rel < count), found, jnp.zeros_like(found))
+            part = chunks[owner % held] + jnp.where((rel >= 0) & (rel < count), found, jnp.zeros_like(found))
             ref[(k - 1) * 2 * h : k * 2 * h, :] = part.astype(ref.dtype)
 
 
@@ -509,20 +516,28 @@
     far = n // group - 1
     rims = RIM // (2 * h)
     parts = (shape((far * 2 * h, width), f32),) + (shape((far * 2 * h, width)),) * (group - 1)
-    chunks, *early = call(
-        partial(project_kernel, h, group, rims),
-        (shape((n, 2 * h, width), f32),) + parts,
-        (own, from_x, weight),
-        [VMEM] * 3,
-        [pltpu.VMEM((2, strip_rows, width), f32)],
-        flops=4 * strip_rows * width * width, moved=8 * MIB,
-    )
+    split = far == 1
+
+    def project(half, after, sent):
+        rows = strip_rows // 2 if split else strip_rows
+        return call(
+            partial(project_kernel, h, group, rims, half),
+            (shape((rows // h, 2 * h, width), f32),) + sent,
+            (after, own, from_x, weight),
+            [ANY] + [VMEM] * 3,
+            [pltpu.VMEM((2, rows, width), f32)],
+            flops=4 * rows * width * width, moved=8 * MIB,
+        )
+
+    chunks, *early = project(0 if split else None, weight, parts)
+    if split:
+        (chunks,) = project(1, chunks, ())
     probe_here = call(
-        probe_sum_kernel, shape((modes, 2, PATCH, PATCH)), (chunks, probe_here, probe_x),
+        probe_sum_kernel, shape((modes, 2, PATCH, PATCH)), (early[0], probe_here, probe_x),
         [ANY, VMEM, VMEM], moved=MIB,
     )
     late = call(
-        partial(rim_kernel, h, group),
+        partial(rim_kernel, h, group, n),
         parts,
         (probe_here, from_y, from_d, weight, chunks),
         [ANY] + [VMEM] * 4,

time: 43.2 us -> 42.8 us (level)
  waiting for transfers between devices: 9.19 us -> 8.72 us
    ppermute x7, waiting for transfers between devices: 7.35 us -> 6.89 us  [swap(): return lax.ppermute(array, 'ang', [(i, i ^ d) for i in range(n)])]
    pallas_call x12 -> x13, Pallas kernels: 16.2 us -> 16.4 us  [call(): pl.pallas_call(kernel, out_shape=outs, in_specs=specs, out_specs=jax.tree...]
where the time goes in v4:
time: 42.8 us; the launch traced here: 42.6 us
  starting transfers between devices  16.7 us (39%)
  Pallas kernels  16.4 us (38%)
  waiting for transfers between devices  8.72 us (20%)
  between operations  0.74 us (2%)
    pallas_call x13, Pallas kernels, call(): pl.pallas_call(kernel, out_shape=outs, in_specs=specs, out_specs=jax.tree...  16.4 us
    ppermute x7, starting transfers between devices, swap(): return lax.ppermute(array, 'ang', [(i, i ^ d) for i in range(n)])  9.74 us
    ppermute x7, waiting for transfers between devices, swap(): return lax.ppermute(array, 'ang', [(i, i ^ d) for i in range(n)])  6.89 us
    ppermute x1, starting transfers between devices, body(): halo_d = lax.ppermute(to_d, ('sy', 'sx'), CROSS)  2.64 us
    ppermute x1, starting transfers between devices, body(): probe_y = lax.ppermute(probe_here, 'sy', SWAP)  1.61 us
    ppermute x1, starting transfers between devices, body(): from_y = lax.ppermute(to_y, 'sy', SWAP)  1.55 us
    ppermute x1, waiting for transfers between devices, body(): from_core = lax.ppermute(to_core, 'sx', SWAP)  1.25 us
  transfers between devices with their start and end apart: 16, of which 7 were waited for; matrix products, arithmetic and copies ran while one was open for 0% of the time, Pallas kernels for 24%

profile of v4, /device:TPU:0, one launch (start us, length us, event | category | flops | bytes accessed | tf_op | source)
XLA Modules:
  0.0 42.6 jit_solution(11035524721733141139)
XLA Ops:
  0.6 1.1 %shard_map.105 = (bf16[2,64,512]{2,1,0:T(8,128)(2,1)S(1)}, bf16[2,512,128]{2,1,0:T(8,128)(2,1)S(1)}, bf16[2,64,128]{2,1,0:T(8,128)(2,1)S(1)}) custom-call(bf16[2,512,512]{2,1,0:T(8,128)(2,1)} %bitcast.8), custom_call_target="tpu_custom_call" | custom-call | bytes 2097152 | tf_op jit(solution)/shard_map/pallas_call | solution.py:53
  1.8 0.5 %collective-permute-start.1 = (bf16[2,512,128]{2,1,0:T(8,128)(2,1)S(1)}, bf16[2,512,128]{2,1,0:T(8,128)(2,1)S(1)}, u32[]{:S(2)}, u32[]{:S(2)}) collective-permute-start(bf16[2,512,128]{2,1,0:T(8,128)(2,1)S(1)} %get-tuple-element.32), channel_id=1, source_target_pairs={{0,1},{1,0},{2,3},{3,2},{4,5},{5,4},{6,7},{7,6},{8,9},{9,8},{10,11... | collective-permute-start | bytes 786440 | tf_op jit(solution)/shard_map/ppermute | solution.py:459
  2.3 2.6 %collective-permute-start.2 = (bf16[2,64,128]{2,1,0:T(8,128)(2,1)S(1)}, bf16[2,64,128]{2,1,0:T(8,128)(2,1)S(1)}, u32[]{:S(2)}, u32[]{:S(2)}) collective-permute-start(bf16[2,64,128]{2,1,0:T(8,128)(2,1)S(1)} %get-tuple-element.33), channel_id=1, source_target_pairs={{0,3},{3,0},{1,2},{2,1},{4,7},{7,4},{5,6},{6,5},{8,11},{11,8},{9,1... | collective-permute-start | bytes 98312 | tf_op jit(solution)/shard_map/ppermute | solution.py:458
  4.9 0.0 copy-start
  4.9 0.1 collective-permute-start
  5.0 2.7 %shard_map.103.matrix = bf16[1024,1024]{1,0:T(8,128)(2,1)S(1)} custom-call(s32[8,16]{1,0:T(8,128)} %index.1, bf16[8,16,128,128]{3,2,1,0:T(8,128)(2,1)} %values.1), custom_call_target="tpu_custom_call" | custom-call | flops 1048576 | bytes 4194304 | tf_op jit(solution)/shard_map/pallas_call | solution.py:53
  7.7 0.0 copy-done
  7.7 2.4 %shard_map.104 = (bf16[1024,1024]{1,0:T(8,128)(2,1)S(1)}, bf16[2,512,512]{2,1,0:T(8,128)(2,1)S(1)}, f32[2,2,256,256]{3,2,1,0:T(8,128)S(1)}, bf16[2,256,256]{2,1,0:T(8,128)(2,1)S(1)}, bf16[2,512,512]{2,1,0:T(8,128)(2,1)S(1)}) custom-call(bf16[1024,1024]{1,0:T(8,128)(2,1)S(1)} %shard_map.103.matrix, bf16[128,1920]{1,0:T(8,128)(2,1)S(1)} %copy-done, ...), custom_call_target="tpu_custom_call" | custom-call | flops 2147483648 | bytes 6291456 | tf_op jit(solution)/shard_map/pallas_call | solution.py:53
  10.1 0.0 collective-permute-done.2.from_d
  10.1 0.3 collective-permute-done.from_y
  10.4 0.0 collective-permute-done.1.from_x
  10.4 4.2 %shard_map.106 = (f32[2,512,512]{2,1,0:T(8,128)S(1)}, bf16[2,256,640]{2,1,0:T(8,128)(2,1)S(1)}, bf16[2,256,768]{2,1,0:T(8,128)(2,1)S(1)}, bf16[2,32,640]{2,1,0:T...) custom-call(s32[2,2]{1,0:T(2,128)} %bitcast.12, ...), custom_call_target="tpu_custom_call" | custom-call | flops 2147483648 | bytes 8388608 | tf_op jit(solution)/shard_map/pallas_call | solution.py:53
  14.6 0.1 collective-permute-start.3
  14.7 0.5 %collective-permute-start.9 = (bf16[2,2,256,256]{3,2,1,0:T(8,128)(2,1)S(1)}, bf16[2,2,256,256]{3,2,1,0:T(8,128)(2,1)S(1)}, u32[]{:S(2)}, u32[]{:S(2)}) collective-permute-start(bf16[2,2,256,256]{3,2,1,0:T(8,128)(2,1)S(1)} %get-tuple-element.46.kept), channel_id=1, source_target_pairs={{0,1},{1,0},{2,3},{3,2},{4,5},{5,4},{6,7},{7,6},{8,9},{9,8},{10,11... | collective-permute-start | bytes 1572872 | tf_op jit(solution)/shard_map/ppermute | solution.py:512
  15.2 1.5 %collective-permute-start.4 = (bf16[2,32,640]{2,1,0:T(8,128)(2,1)S(1)}, bf16[2,32,640]{2,1,0:T(8,128)(2,1)S(1)}, u32[]{:S(2)}, u32[]{:S(2)}) collective-permute-start(bf16[2,32,640]{2,1,0:T(8,128)(2,1)S(1)} %get-tuple-element.39), channel_id=1, source_target_pairs={{0,2},{2,0},{1,3},{3,1},{4,6},{6,4},{5,7},{7,5},{8,10},{10,8},{9,1... | collective-permute-start | bytes 245768 | tf_op jit(solution)/shard_map/ppermute | solution.py:513
  16.8 0.0 collective-permute-start.5
  16.8 0.2 collective-permute-done.3.from_x
  17.0 0.9 %shard_map.107 = (f32[4,64,1024]{2,1,0:T(8,128)S(1)}, f32[64,1024]{1,0:T(8,128)S(1)}, bf16[64,1024]{1,0:T(8,128)(2,1)S(1)}, bf16[64,1024]{1,0:T(8,128)(2,1)S(1)}, bf16[64,1024]{1,0:T(8,128)(2,1)S(1)}) custom-call(bf16[1024,1024]{1,0:T(8,128)(2,1)S(1)} %get-tuple-element.29.ahead.after.weight, bf16[2,256,640]{2,1,0:T(8,128)(2,1)S(1)} %get-tuple-element.41.own, ...), custom_call_target="tpu_custom_call" | custom-call | flops 536870912 | bytes 8388608 | tf_op jit(solution)/shard_map/pallas_call | solution.py:53
  17.9 1.6 %collective-permute-start.6 = (bf16[64,1024]{1,0:T(8,128)(2,1)S(1)}, bf16[64,1024]{1,0:T(8,128)(2,1)S(1)}, u32[]{:S(2)}, u32[]{:S(2)}) collective-permute-start(bf16[64,1024]{1,0:T(8,128)(2,1)S(1)} %get-tuple-element.43), channel_id=1, source_target_pairs={{0,4},{4,0},{8,12},{12,8},{16,20},{20,16},{24,28},{28,24},{1,5},{5... | collective-permute-start | bytes 393224 | tf_op jit(solution)/shard_map/ppermute | solution.py:549
  19.5 1.6 %collective-permute-start.7 = (bf16[64,1024]{1,0:T(8,128)(2,1)S(1)}, bf16[64,1024]{1,0:T(8,128)(2,1)S(1)}, u32[]{:S(2)}, u32[]{:S(2)}) collective-permute-start(bf16[64,1024]{1,0:T(8,128)(2,1)S(1)} %get-tuple-element.44), channel_id=1, source_target_pairs={{0,8},{4,12},{8,0},{12,4},{16,24},{20,28},{24,16},{28,20},{1,9},{5... | collective-permute-start | bytes 393224 | tf_op jit(solution)/shard_map/ppermute | solution.py:549
  21.0 0.0 collective-permute-done.9.received
  21.0 0.4 collective-permute-start.8
  21.4 0.1 shard_map.109.after.mine
  21.6 0.8 %shard_map.110.chunks = f32[4,64,1024]{2,1,0:T(8,128)S(1)} custom-call(f32[4,64,1024]{2,1,0:T(8,128)S(1)} %get-tuple-element.47.after, bf16[2,256,640]{2,1,0:T(8,128)(2,1)S(1)} %get-tuple-element.41.own, bf16[2,256,768]{2,1,0:T(8,128)(2,1)S(1)} %collective-permute-done.3.from_x, bf16[1024,1024]{1,0:T(8,128)(2,1)S(1)} %get-tuple-element.29.ahead.after.weight), custom_call_target="tpu_custom_call" | custom-call | flops 536870912 | bytes 8388608 | tf_op jit(solution)/shard_map/pallas_call | solution.py:53
  22.4 0.0 collective-permute-done.4.from_y
  22.4 1.6 %collective-permute-start.14 = (bf16[2,2,256,256]{3,2,1,0:T(8,128)(2,1)S(1)}, bf16[2,2,256,256]{3,2,1,0:T(8,128)(2,1)S(1)}, u32[]{:S(2)}, u32[]{:S(2)}) collective-permute-start(bf16[2,2,256,256]{3,2,1,0:T(8,128)(2,1)S(1)} %shard_map.109.after.mine), channel_id=1, source_target_pairs={{0,2},{2,0},{1,3},{3,1},{4,6},{6,4},{5,7},{7,5},{8,10},{10,8},{9,1... | collective-permute-start | bytes 1572872 | tf_op jit(solution)/shard_map/ppermute | solution.py:563
  24.0 0.0 collective-permute-done.5.from_d
  24.0 0.5 %shard_map.111 = (f32[64,1024]{1,0:T(8,128)S(1)}, bf16[64,1024]{1,0:T(8,128)(2,1)S(1)}, bf16[64,1024]{1,0:T(8,128)(2,1)S(1)}, bf16[64,1024]{1,0:T(8,128)(2,1)S(1)}) custom-call(bf16[2,2,256,256]{3,2,1,0:T(8,128)(2,1)S(1)} %shard_map.109.after.mine, bf16[2,32,640]{2,1,0:T(8,128)(2,1)S(1)} %collective-permute-done.4.from_y, ...), custom_call_target="tpu_custom_call" | custom-call | flops 12884901888 | bytes 4194304 | tf_op jit(solution)/shard_map/pallas_call | solution.py:53
  24.6 1.5 %collective-permute-start.10 = (bf16[64,1024]{1,0:T(8,128)(2,1)S(1)}, bf16[64,1024]{1,0:T(8,128)(2,1)S(1)}, u32[]{:S(2)}, u32[]{:S(2)}) collective-permute-start(bf16[64,1024]{1,0:T(8,128)(2,1)S(1)} %get-tuple-element.49), channel_id=1, source_target_pairs={{0,4},{4,0},{8,12},{12,8},{16,20},{20,16},{24,28},{28,24},{1,5},{5... | collective-permute-start | bytes 393224 | tf_op jit(solution)/shard_map/ppermute | solution.py:549
  26.1 0.0 collective-permute-done.6.refs_1_
  26.1 1.6 %collective-permute-start.11 = (bf16[64,1024]{1,0:T(8,128)(2,1)S(1)}, bf16[64,1024]{1,0:T(8,128)(2,1)S(1)}, u32[]{:S(2)}, u32[]{:S(2)}) collective-permute-start(bf16[64,1024]{1,0:T(8,128)(2,1)S(1)} %get-tuple-element.50), channel_id=1, source_target_pairs={{0,8},{4,12},{8,0},{12,4},{16,24},{20,28},{24,16},{28,20},{1,9},{5... | collective-permute-start | bytes 393224 | tf_op jit(solution)/shard_map/ppermute | solution.py:549
  27.7 0.0 collective-permute-done.7.refs_2_
  27.7 0.4 %collective-permute-start.12 = (bf16[64,1024]{1,0:T(8,128)(2,1)S(1)}, bf16[64,1024]{1,0:T(8,128)(2,1)S(1)}, u32[]{:S(2)}, u32[]{:S(2)}) collective-permute-start(bf16[64,1024]{1,0:T(8,128)(2,1)S(1)} %get-tuple-element.51), channel_id=1, source_target_pairs={{0,12},{4,8},{8,4},{12,0},{16,28},{20,24},{24,20},{28,16},{1,13},{... | collective-permute-start | bytes 393224 | tf_op jit(solution)/shard_map/ppermute | solution.py:549
  28.1 0.0 collective-permute-done.8.refs_3_
  28.1 0.1 shard_map.108.early
  28.2 3.0 %collective-permute-done.10.refs_1_ = bf16[64,1024]{1,0:T(8,128)(2,1)S(1)} collective-permute-done((bf16[64,1024]{1,0:T(8,128)(2,1)S(1)}, bf16[64,1024]{1,0:T(8,128)(2,1)S(1)}, u32[]{:S(2)}, u32[]{:S(2)}) %collective-permute-start.10) | collective-permute-done | bytes 131104 | tf_op jit(solution)/shard_map/ppermute | solution.py:549
  31.2 0.8 %collective-permute-done.11.refs_2_ = bf16[64,1024]{1,0:T(8,128)(2,1)S(1)} collective-permute-done((bf16[64,1024]{1,0:T(8,128)(2,1)S(1)}, bf16[64,1024]{1,0:T(8,128)(2,1)S(1)}, u32[]{:S(2)}, u32[]{:S(2)}) %collective-permute-start.11) | collective-permute-done | bytes 131104 | tf_op jit(solution)/shard_map/ppermute | solution.py:549
  32.0 1.9 %collective-permute-done.12.refs_3_ = bf16[64,1024]{1,0:T(8,128)(2,1)S(1)} collective-permute-done((bf16[64,1024]{1,0:T(8,128)(2,1)S(1)}, bf16[64,1024]{1,0:T(8,128)(2,1)S(1)}, u32[]{:S(2)}, u32[]{:S(2)}) %collective-permute-start.12) | collective-permute-done | bytes 131104 | tf_op jit(solution)/shard_map/ppermute | solution.py:549
  33.9 0.1 shard_map.112
  34.0 2.6 %collective-permute-start.15 = (bf16[64,1024]{1,0:T(8,128)(2,1)S(1)}, bf16[64,1024]{1,0:T(8,128)(2,1)S(1)}, u32[]{:S(2)}, u32[]{:S(2)}) collective-permute-start(bf16[64,1024]{1,0:T(8,128)(2,1)S(1)} %get-tuple-element.54), channel_id=1, source_target_pairs={{0,16},{4,20},{8,24},{12,28},{16,0},{20,4},{24,8},{28,12},{1,17},{... | collective-permute-start | bytes 393224 | tf_op jit(solution)/shard_map/ppermute | solution.py:549
  36.6 0.0 collective-permute-start.13
  36.6 1.3 %collective-permute-done.13.from_core = bf16[2,32,512]{2,1,0:T(8,128)(2,1)S(1)} collective-permute-done((bf16[2,32,512]{2,1,0:T(8,128)(2,1)S(1)}, bf16[2,32,512]{2,1,0:T(8,128)(2,1)S(1)}, u32[]{:S(2)}, u32[]{:S(2)}) %collective-permute-start.13) | collective-permute-done | bytes 65568 | tf_op jit(solution)/shard_map/ppermute | solution.py:564
  37.8 1.7 %shard_map.113 = f32[2,512,512]{2,1,0:T(8,128)} custom-call(f32[2,512,512]{2,1,0:T(8,128)S(1)} %get-tuple-element.37.grad, bf16[2,256,768]{2,1,0:T(8,128)(2,1)S(1)} %collective-permute-done.3.from_x, bf16[2,32,640]{2,1,0:T(8,128)(2,1)S(1)} %collective-permute-done.4.from_y, bf16[2,32,640]{2,1,0:T(8,128)(2,1)S(1)} %collective-permute-done.5.from_d, ...), custom_call_target="tpu_custom_call" | custom-call | bytes 6291456 | tf_op jit(solution)/shard_map/pallas_call | solution.py:53
  39.5 0.0 collective-permute-done.14.other
  39.5 1.1 %shard_map.114.after = f32[2,2,256,256]{3,2,1,0:T(8,128)} custom-call(bf16[2,2,256,256]{3,2,1,0:T(8,128)(2,1)S(1)} %shard_map.109.after.mine, bf16[2,2,256,256]{3,2,1,0:T(8,128)(2,1)S(1)} %collective-permute-done.14.other), custom_call_target="tpu_custom_call" | custom-call | bytes 2097152 | tf_op jit(solution)/shard_map/pallas_call | solution.py:53
  40.6 1.2 %collective-permute-done.15.refs_1_ = bf16[64,1024]{1,0:T(8,128)(2,1)S(1)} collective-permute-done((bf16[64,1024]{1,0:T(8,128)(2,1)S(1)}, bf16[64,1024]{1,0:T(8,128)(2,1)S(1)}, u32[]{:S(2)}, u32[]{:S(2)}) %collective-permute-start.15) | collective-permute-done | bytes 131104 | tf_op jit(solution)/shard_map/ppermute | solution.py:549
  41.8 0.8 %shard_map.115 = f32[32,2,1024]{2,1,0:T(2,128)} custom-call(f32[2,2,256,256]{3,2,1,0:T(8,128)} %shard_map.114.after, f32[64,1024]{1,0:T(8,128)S(1)} %get-tuple-element.53.refs_0_, bf16[64,1024]{1,0:T(8,128)(2,1)S(1)} %collective-permute-done.15.refs_1_), custom_call_target="tpu_custom_call" | custom-call | bytes 1048576 | tf_op jit(solution)/shard_map/pallas_call | solution.py:53
Async XLA Ops:
  1.8 8.6 %collective-permute-start.1 = (bf16[2,512,128]{2,1,0:T(8,128)(2,1)S(1)}, bf16[2,512,128]{2,1,0:T(8,128)(2,1)S(1)}, u32[]{:S(2)}, u32[]{:S(2)}) collective-permute-start(bf16[2,512,128]{2,1,0:T(8,128)(2,1)S(1)} %get-tuple-element.32), channel_id=1, source_target_pairs={{0,1},{1,0},{2,3},{3,2},{4,5},{5,4},{6,7},{7,6},{8,9},{9,8},{10,11... | collective-permute-start | bytes 786440 | tf_op jit(solution)/shard_map/ppermute | solution.py:459
  2.3 7.8 %collective-permute-start.2 = (bf16[2,64,128]{2,1,0:T(8,128)(2,1)S(1)}, bf16[2,64,128]{2,1,0:T(8,128)(2,1)S(1)}, u32[]{:S(2)}, u32[]{:S(2)}) collective-permute-start(bf16[2,64,128]{2,1,0:T(8,128)(2,1)S(1)} %get-tuple-element.33), channel_id=1, source_target_pairs={{0,3},{3,0},{1,2},{2,1},{4,7},{7,4},{5,6},{6,5},{8,11},{11,8},{9,1... | collective-permute-start | bytes 98312 | tf_op jit(solution)/shard_map/ppermute | solution.py:458
  4.9 2.7 %copy-start = (bf16[128,1920]{1,0:T(8,128)(2,1)S(1)}, bf16[128,1920]{1,0:T(8,128)(2,1)}, u32[]{:S(2)}) copy-start(bf16[128,1920]{1,0:T(8,128)(2,1)} %constant.5.clone.strip) | copy-start | bytes 1474564
  4.9 5.5 %collective-permute-start = (bf16[2,64,512]{2,1,0:T(8,128)(2,1)S(1)}, bf16[2,64,512]{2,1,0:T(8,128)(2,1)S(1)}, u32[]{:S(2)}, u32[]{:S(2)}) collective-permute-start(bf16[2,64,512]{2,1,0:T(8,128)(2,1)S(1)} %get-tuple-element.31), channel_id=1, source_target_pairs={{0,2},{2,0},{1,3},{3,1},{4,6},{6,4},{5,7},{7,5},{8,10},{10,8},{9,1... | collective-permute-start | bytes 393224 | tf_op jit(solution)/shard_map/ppermute | solution.py:457
  14.6 2.4 %collective-permute-start.3 = (bf16[2,256,768]{2,1,0:T(8,128)(2,1)S(1)}, bf16[2,256,768]{2,1,0:T(8,128)(2,1)S(1)}, u32[]{:S(2)}, u32[]{:S(2)}) collective-permute-start(bf16[2,256,768]{2,1,0:T(8,128)(2,1)S(1)} %get-tuple-element.38), channel_id=1, source_target_pairs={{0,1},{1,0},{2,3},{3,2},{4,5},{5,4},{6,7},{7,6},{8,9},{9,8},{10,11... | collective-permute-start | bytes 2359304 | tf_op jit(solution)/shard_map/ppermute | solution.py:511
  14.7 6.3 %collective-permute-start.9 = (bf16[2,2,256,256]{3,2,1,0:T(8,128)(2,1)S(1)}, bf16[2,2,256,256]{3,2,1,0:T(8,128)(2,1)S(1)}, u32[]{:S(2)}, u32[]{:S(2)}) collective-permute-start(bf16[2,2,256,256]{3,2,1,0:T(8,128)(2,1)S(1)} %get-tuple-element.46.kept), channel_id=1, source_target_pairs={{0,1},{1,0},{2,3},{3,2},{4,5},{5,4},{6,7},{7,6},{8,9},{9,8},{10,11... | collective-permute-start | bytes 1572872 | tf_op jit(solution)/shard_map/ppermute | solution.py:512
  15.2 7.2 %collective-permute-start.4 = (bf16[2,32,640]{2,1,0:T(8,128)(2,1)S(1)}, bf16[2,32,640]{2,1,0:T(8,128)(2,1)S(1)}, u32[]{:S(2)}, u32[]{:S(2)}) collective-permute-start(bf16[2,32,640]{2,1,0:T(8,128)(2,1)S(1)} %get-tuple-element.39), channel_id=1, source_target_pairs={{0,2},{2,0},{1,3},{3,1},{4,6},{6,4},{5,7},{7,5},{8,10},{10,8},{9,1... | collective-permute-start | bytes 245768 | tf_op jit(solution)/shard_map/ppermute | solution.py:513
  16.8 7.3 %collective-permute-start.5 = (bf16[2,32,640]{2,1,0:T(8,128)(2,1)S(1)}, bf16[2,32,640]{2,1,0:T(8,128)(2,1)S(1)}, u32[]{:S(2)}, u32[]{:S(2)}) collective-permute-start(bf16[2,32,640]{2,1,0:T(8,128)(2,1)S(1)} %get-tuple-element.40), channel_id=1, source_target_pairs={{0,3},{3,0},{1,2},{2,1},{4,7},{7,4},{5,6},{6,5},{8,11},{11,8},{9,1... | collective-permute-start | bytes 245768 | tf_op jit(solution)/shard_map/ppermute | solution.py:514
  17.9 8.2 %collective-permute-start.6 = (bf16[64,1024]{1,0:T(8,128)(2,1)S(1)}, bf16[64,1024]{1,0:T(8,128)(2,1)S(1)}, u32[]{:S(2)}, u32[]{:S(2)}) collective-permute-start(bf16[64,1024]{1,0:T(8,128)(2,1)S(1)} %get-tuple-element.43), channel_id=1, source_target_pairs={{0,4},{4,0},{8,12},{12,8},{16,20},{20,16},{24,28},{28,24},{1,5},{5... | collective-permute-start | bytes 393224 | tf_op jit(solution)/shard_map/ppermute | solution.py:549
  19.5 8.2 %collective-permute-start.7 = (bf16[64,1024]{1,0:T(8,128)(2,1)S(1)}, bf16[64,1024]{1,0:T(8,128)(2,1)S(1)}, u32[]{:S(2)}, u32[]{:S(2)}) collective-permute-start(bf16[64,1024]{1,0:T(8,128)(2,1)S(1)} %get-tuple-element.44), channel_id=1, source_target_pairs={{0,8},{4,12},{8,0},{12,4},{16,24},{20,28},{24,16},{28,20},{1,9},{5... | collective-permute-start | bytes 393224 | tf_op jit(solution)/shard_map/ppermute | solution.py:549
  21.0 7.1 %collective-permute-start.8 = (bf16[64,1024]{1,0:T(8,128)(2,1)S(1)}, bf16[64,1024]{1,0:T(8,128)(2,1)S(1)}, u32[]{:S(2)}, u32[]{:S(2)}) collective-permute-start(bf16[64,1024]{1,0:T(8,128)(2,1)S(1)} %get-tuple-element.45), channel_id=1, source_target_pairs={{0,12},{4,8},{8,4},{12,0},{16,28},{20,24},{24,20},{28,16},{1,13},{... | collective-permute-start | bytes 393224 | tf_op jit(solution)/shard_map/ppermute | solution.py:549
  22.4 17.1 %collective-permute-start.14 = (bf16[2,2,256,256]{3,2,1,0:T(8,128)(2,1)S(1)}, bf16[2,2,256,256]{3,2,1,0:T(8,128)(2,1)S(1)}, u32[]{:S(2)}, u32[]{:S(2)}) collective-permute-start(bf16[2,2,256,256]{3,2,1,0:T(8,128)(2,1)S(1)} %shard_map.109.after.mine), channel_id=1, source_target_pairs={{0,2},{2,0},{1,3},{3,1},{4,6},{6,4},{5,7},{7,5},{8,10},{10,8},{9,1... | collective-permute-start | bytes 1572872 | tf_op jit(solution)/shard_map/ppermute | solution.py:563
  24.6 6.6 %collective-permute-start.10 = (bf16[64,1024]{1,0:T(8,128)(2,1)S(1)}, bf16[64,1024]{1,0:T(8,128)(2,1)S(1)}, u32[]{:S(2)}, u32[]{:S(2)}) collective-permute-start(bf16[64,1024]{1,0:T(8,128)(2,1)S(1)} %get-tuple-element.49), channel_id=1, source_target_pairs={{0,4},{4,0},{8,12},{12,8},{16,20},{20,16},{24,28},{28,24},{1,5},{5... | collective-permute-start | bytes 393224 | tf_op jit(solution)/shard_map/ppermute | solution.py:549
  26.1 5.9 %collective-permute-start.11 = (bf16[64,1024]{1,0:T(8,128)(2,1)S(1)}, bf16[64,1024]{1,0:T(8,128)(2,1)S(1)}, u32[]{:S(2)}, u32[]{:S(2)}) collective-permute-start(bf16[64,1024]{1,0:T(8,128)(2,1)S(1)} %get-tuple-element.50), channel_id=1, source_target_pairs={{0,8},{4,12},{8,0},{12,4},{16,24},{20,28},{24,16},{28,20},{1,9},{5... | collective-permute-start | bytes 393224 | tf_op jit(solution)/shard_map/ppermute | solution.py:549
  27.7 6.2 %collective-permute-start.12 = (bf16[64,1024]{1,0:T(8,128)(2,1)S(1)}, bf16[64,1024]{1,0:T(8,128)(2,1)S(1)}, u32[]{:S(2)}, u32[]{:S(2)}) collective-permute-start(bf16[64,1024]{1,0:T(8,128)(2,1)S(1)} %get-tuple-element.51), channel_id=1, source_target_pairs={{0,12},{4,8},{8,4},{12,0},{16,28},{20,24},{24,20},{28,16},{1,13},{... | collective-permute-start | bytes 393224 | tf_op jit(solution)/shard_map/ppermute | solution.py:549
  34.0 7.9 %collective-permute-start.15 = (bf16[64,1024]{1,0:T(8,128)(2,1)S(1)}, bf16[64,1024]{1,0:T(8,128)(2,1)S(1)}, u32[]{:S(2)}, u32[]{:S(2)}) collective-permute-start(bf16[64,1024]{1,0:T(8,128)(2,1)S(1)} %get-tuple-element.54), channel_id=1, source_target_pairs={{0,16},{4,20},{8,24},{12,28},{16,0},{20,4},{24,8},{28,12},{1,17},{... | collective-permute-start | bytes 393224 | tf_op jit(solution)/shard_map/ppermute | solution.py:549
  36.6 1.3 %collective-permute-start.13 = (bf16[2,32,512]{2,1,0:T(8,128)(2,1)S(1)}, bf16[2,32,512]{2,1,0:T(8,128)(2,1)S(1)}, u32[]{:S(2)}, u32[]{:S(2)}) collective-permute-start(bf16[2,32,512]{2,1,0:T(8,128)(2,1)S(1)} %get-tuple-element.52), channel_id=1, source_target_pairs={{0,1},{1,0},{2,3},{3,2},{4,5},{5,4},{6,7},{7,6},{8,9},{9,8},{10,11... | collective-permute-start | bytes 196616 | tf_op jit(solution)/shard_map/ppermute | solution.py:564

commit v5 on v4

--- a/solution.py
+++ b/solution.py
@@ -184,8 +184,8 @@
 
 def patch_kernel(
     h, pos, ahead, obj, from_y, from_x, from_d, probe, data, dft,
-    grad, own, to_x, to_y, to_d, probe_here,
-    frame, total, stack, probe_total, spots, sem,
+    total, own, to_x, to_y, to_d, probe_here,
+    frame, stack, probe_total, spots, sem,
 ):
     fetch = pltpu.make_async_copy(pos, spots, sem)
     fetch.start()
@@ -268,11 +268,12 @@
             g_re += p_re * c_re + p_im * c_im
             g_im += p_re * c_im - p_im * c_re
             q_re, q_im = o_re * c_re + o_im * c_im, o_re * c_im - o_im * c_re
-            if p == 0:
-                probe_total[m, 0], probe_total[m, 1] = q_re, q_im
-            else:
-                probe_total[m, 0] += q_re
-                probe_total[m, 1] += q_im
+            for c, q in enumerate((q_re, q_im)):
+                q = q + probe_total[m, c] if p else q
+                if p < patches - 1:
+                    probe_total[m, c] = q
+                else:
+                    probe_here[m, c] = q.astype(bf16)
         top, down, start, shift = place(p)
         for c, g in enumerate((g_re, g_im)):
             turned = [pltpu.roll(g[:, k * BLK : (k + 1) * BLK], shift, 1) for k in range(spans)]
@@ -287,7 +288,6 @@
     out_block = pl.ds(col_in, BLK)
     width = cols + BLK
     for c in range(2):
-        grad[c] = total[c, RIM:last, BLK : BLK + cols]
         for half, wide in ((sx, own), (1 - sx, to_x)):
             wide[c, :, 0:cols] = pick_strips(total, c, RIM, rows, inner, half, h)
             wide[c, :, cols:width] = pick_strips(total, c, RIM, rows, out_block, half, h)
@@ -295,7 +295,6 @@
             wide[c, :, 0:cols] = pick_strips(total, c, row_in, RIM, inner, half, h)
             wide[c, :, cols:width] = pick_strips(total, c, row_in, RIM, out_block, half, h)
         to_x[c, :, width : width + BLK] = own[c, :, cols:width]
-    probe_here[...] = probe_total[...].astype(bf16)
 
 
 def column_cuts(sx, cols):
@@ -380,12 +379,12 @@
 def fold_kernel(h, grad, from_x, from_y, from_d, from_core, out):
     sy, sx = lax.axis_index("sy"), lax.axis_index("sx")
     f32 = jnp.float32
-    rows, cols = grad.shape[1], grad.shape[2]
+    rows, cols = out.shape[1], out.shape[2]
     edge = pl.ds(aligned((1 - sx) * (cols - BLK), BLK), BLK)
     row = aligned((1 - sy) * (rows - RIM), RIM)
     every = pl.ds(0, cols)
     for c in range(2):
-        out[c] = grad[c]
+        out[c] = grad[c, RIM : RIM + rows, BLK : BLK + cols]
         add_strips(out, c, 0, rows, edge, sx, h, from_x[c, :, cols : cols + BLK].astype(f32))
         add_strips(out, c, 0, rows, edge, 1 - sx, h, from_x[c, :, cols + BLK : cols + 2 * BLK].astype(f32))
         add_strips(out, c, row, RIM, every, sx, h, from_y[c, :, 0:cols].astype(f32))
@@ -488,7 +487,7 @@
     grad, own, to_x, to_y, to_d, probe_here = call(
         partial(patch_kernel, h),
         (
-            shape((2, rows, cols), f32),
+            shape((2, rows + 2 * RIM + 8, cols + 2 * BLK), f32),
             shape((2, strip_rows, wide)),
             shape((2, strip_rows, wide + BLK)),
             shape((2, RIM // 2, wide)),
@@ -499,7 +498,6 @@
         [HBM, ANY] + [VMEM] * 7,
         [
             pltpu.VMEM((2, rows + 2 * RIM + 8, cols + 2 * BLK), f32),
-            pltpu.VMEM((2, rows + 2 * RIM + 8, cols + 2 * BLK), f32),
             pltpu.VMEM((2 * PATCH, patches * modes * PATCH), bf16),
             pltpu.VMEM((modes, 2, PATCH, PATCH), f32),
             pltpu.SMEM(pos.shape, jnp.int32),

time: 42.8 us -> 42.7 us (level)
  no operation moved by 1% of the time
where the time goes in v5:
time: 42.7 us; the launch traced here: 42.4 us
  starting transfers between devices  16.7 us (39%)
  Pallas kernels  16.3 us (38%)
  waiting for transfers between devices  8.72 us (20%)
  between operations  0.74 us (2%)
    pallas_call x13, Pallas kernels, call(): pl.pallas_call(kernel, out_shape=outs, in_specs=specs, out_specs=jax.tree...  16.3 us
    ppermute x7, starting transfers between devices, swap(): return lax.ppermute(array, 'ang', [(i, i ^ d) for i in range(n)])  9.78 us
    ppermute x7, waiting for transfers between devices, swap(): return lax.ppermute(array, 'ang', [(i, i ^ d) for i in range(n)])  6.85 us
    ppermute x1, starting transfers between devices, body(): halo_d = lax.ppermute(to_d, ('sy', 'sx'), CROSS)  2.64 us
    ppermute x1, starting transfers between devices, body(): probe_y = lax.ppermute(probe_here, 'sy', SWAP)  1.59 us
    ppermute x1, starting transfers between devices, body(): from_y = lax.ppermute(to_y, 'sy', SWAP)  1.52 us
    ppermute x1, waiting for transfers between devices, body(): from_core = lax.ppermute(to_core, 'sx', SWAP)  1.25 us
  transfers between devices with their start and end apart: 16, of which 7 were waited for; matrix products, arithmetic and copies ran while one was open for 0% of the time, Pallas kernels for 24%

profile of v5, /device:TPU:0, one launch (start us, length us, event | category | flops | bytes accessed | tf_op | source)
XLA Modules:
  0.0 42.4 jit_solution(15184423016615727810)
XLA Ops:
  0.6 1.1 %shard_map.105 = (bf16[2,64,512]{2,1,0:T(8,128)(2,1)S(1)}, bf16[2,512,128]{2,1,0:T(8,128)(2,1)S(1)}, bf16[2,64,128]{2,1,0:T(8,128)(2,1)S(1)}) custom-call(bf16[2,512,512]{2,1,0:T(8,128)(2,1)} %bitcast.8), custom_call_target="tpu_custom_call" | custom-call | bytes 2097152 | tf_op jit(solution)/shard_map/pallas_call | solution.py:53
  1.8 0.5 %collective-permute-start.1 = (bf16[2,512,128]{2,1,0:T(8,128)(2,1)S(1)}, bf16[2,512,128]{2,1,0:T(8,128)(2,1)S(1)}, u32[]{:S(2)}, u32[]{:S(2)}) collective-permute-start(bf16[2,512,128]{2,1,0:T(8,128)(2,1)S(1)} %get-tuple-element.32), channel_id=1, source_target_pairs={{0,1},{1,0},{2,3},{3,2},{4,5},{5,4},{6,7},{7,6},{8,9},{9,8},{10,11... | collective-permute-start | bytes 786440 | tf_op jit(solution)/shard_map/ppermute | solution.py:458
  2.3 2.6 %collective-permute-start.2 = (bf16[2,64,128]{2,1,0:T(8,128)(2,1)S(1)}, bf16[2,64,128]{2,1,0:T(8,128)(2,1)S(1)}, u32[]{:S(2)}, u32[]{:S(2)}) collective-permute-start(bf16[2,64,128]{2,1,0:T(8,128)(2,1)S(1)} %get-tuple-element.33), channel_id=1, source_target_pairs={{0,3},{3,0},{1,2},{2,1},{4,7},{7,4},{5,6},{6,5},{8,11},{11,8},{9,1... | collective-permute-start | bytes 98312 | tf_op jit(solution)/shard_map/ppermute | solution.py:457
  4.9 0.0 copy-start
  4.9 0.1 collective-permute-start
  5.0 2.7 %shard_map.103.matrix = bf16[1024,1024]{1,0:T(8,128)(2,1)S(1)} custom-call(s32[8,16]{1,0:T(8,128)} %index.1, bf16[8,16,128,128]{3,2,1,0:T(8,128)(2,1)} %values.1), custom_call_target="tpu_custom_call" | custom-call | flops 1048576 | bytes 4194304 | tf_op jit(solution)/shard_map/pallas_call | solution.py:53
  7.7 0.0 copy-done
  7.7 2.4 %shard_map.104 = (bf16[1024,1024]{1,0:T(8,128)(2,1)S(1)}, bf16[2,512,512]{2,1,0:T(8,128)(2,1)S(1)}, f32[2,2,256,256]{3,2,1,0:T(8,128)S(1)}, bf16[2,256,256]{2,1,0:T(8,128)(2,1)S(1)}, bf16[2,512,512]{2,1,0:T(8,128)(2,1)S(1)}) custom-call(bf16[1024,1024]{1,0:T(8,128)(2,1)S(1)} %shard_map.103.matrix, bf16[128,1920]{1,0:T(8,128)(2,1)S(1)} %copy-done, ...), custom_call_target="tpu_custom_call" | custom-call | flops 2147483648 | bytes 6291456 | tf_op jit(solution)/shard_map/pallas_call | solution.py:53
  10.1 0.0 collective-permute-done.2.from_d
  10.1 0.3 collective-permute-done.from_y
  10.4 0.0 collective-permute-done.1.from_x
  10.4 4.1 %shard_map.106 = (f32[2,648,768]{2,1,0:T(8,128)S(1)}, bf16[2,256,640]{2,1,0:T(8,128)(2,1)S(1)}, bf16[2,256,768]{2,1,0:T(8,128)(2,1)S(1)}, bf16[2,32,640]{2,1,0:T...) custom-call(s32[2,2]{1,0:T(2,128)} %bitcast.12, ...), custom_call_target="tpu_custom_call" | custom-call | flops 2147483648 | bytes 8388608 | tf_op jit(solution)/shard_map/pallas_call | solution.py:53
  14.5 0.1 collective-permute-start.3
  14.6 0.5 %collective-permute-start.9 = (bf16[2,2,256,256]{3,2,1,0:T(8,128)(2,1)S(1)}, bf16[2,2,256,256]{3,2,1,0:T(8,128)(2,1)S(1)}, u32[]{:S(2)}, u32[]{:S(2)}) collective-permute-start(bf16[2,2,256,256]{3,2,1,0:T(8,128)(2,1)S(1)} %get-tuple-element.46.kept), channel_id=1, source_target_pairs={{0,1},{1,0},{2,3},{3,2},{4,5},{5,4},{6,7},{7,6},{8,9},{9,8},{10,11... | collective-permute-start | bytes 1572872 | tf_op jit(solution)/shard_map/ppermute | solution.py:510
  15.1 1.5 %collective-permute-start.4 = (bf16[2,32,640]{2,1,0:T(8,128)(2,1)S(1)}, bf16[2,32,640]{2,1,0:T(8,128)(2,1)S(1)}, u32[]{:S(2)}, u32[]{:S(2)}) collective-permute-start(bf16[2,32,640]{2,1,0:T(8,128)(2,1)S(1)} %get-tuple-element.39), channel_id=1, source_target_pairs={{0,2},{2,0},{1,3},{3,1},{4,6},{6,4},{5,7},{7,5},{8,10},{10,8},{9,1... | collective-permute-start | bytes 245768 | tf_op jit(solution)/shard_map/ppermute | solution.py:511
  16.6 0.0 collective-permute-start.5
  16.6 0.3 collective-permute-done.3.from_x
  16.8 0.9 %shard_map.107 = (f32[4,64,1024]{2,1,0:T(8,128)S(1)}, f32[64,1024]{1,0:T(8,128)S(1)}, bf16[64,1024]{1,0:T(8,128)(2,1)S(1)}, bf16[64,1024]{1,0:T(8,128)(2,1)S(1)}, bf16[64,1024]{1,0:T(8,128)(2,1)S(1)}) custom-call(bf16[1024,1024]{1,0:T(8,128)(2,1)S(1)} %get-tuple-element.29.ahead.after.weight, bf16[2,256,640]{2,1,0:T(8,128)(2,1)S(1)} %get-tuple-element.41.own, ...), custom_call_target="tpu_custom_call" | custom-call | flops 536870912 | bytes 8388608 | tf_op jit(solution)/shard_map/pallas_call | solution.py:53
  17.7 1.6 %collective-permute-start.6 = (bf16[64,1024]{1,0:T(8,128)(2,1)S(1)}, bf16[64,1024]{1,0:T(8,128)(2,1)S(1)}, u32[]{:S(2)}, u32[]{:S(2)}) collective-permute-start(bf16[64,1024]{1,0:T(8,128)(2,1)S(1)} %get-tuple-element.43), channel_id=1, source_target_pairs={{0,4},{4,0},{8,12},{12,8},{16,20},{20,16},{24,28},{28,24},{1,5},{5... | collective-permute-start | bytes 393224 | tf_op jit(solution)/shard_map/ppermute | solution.py:547
  19.3 1.6 %collective-permute-start.7 = (bf16[64,1024]{1,0:T(8,128)(2,1)S(1)}, bf16[64,1024]{1,0:T(8,128)(2,1)S(1)}, u32[]{:S(2)}, u32[]{:S(2)}) collective-permute-start(bf16[64,1024]{1,0:T(8,128)(2,1)S(1)} %get-tuple-element.44), channel_id=1, source_target_pairs={{0,8},{4,12},{8,0},{12,4},{16,24},{20,28},{24,16},{28,20},{1,9},{5... | collective-permute-start | bytes 393224 | tf_op jit(solution)/shard_map/ppermute | solution.py:547
  20.9 0.0 collective-permute-done.9.received
  20.9 0.4 %collective-permute-start.8 = (bf16[64,1024]{1,0:T(8,128)(2,1)S(1)}, bf16[64,1024]{1,0:T(8,128)(2,1)S(1)}, u32[]{:S(2)}, u32[]{:S(2)}) collective-permute-start(bf16[64,1024]{1,0:T(8,128)(2,1)S(1)} %get-tuple-element.45), channel_id=1, source_target_pairs={{0,12},{4,8},{8,4},{12,0},{16,28},{20,24},{24,20},{28,16},{1,13},{... | collective-permute-start | bytes 393224 | tf_op jit(solution)/shard_map/ppermute | solution.py:547
  21.3 0.1 shard_map.109.after.mine
  21.4 0.8 %shard_map.110.chunks = f32[4,64,1024]{2,1,0:T(8,128)S(1)} custom-call(f32[4,64,1024]{2,1,0:T(8,128)S(1)} %get-tuple-element.47.after, bf16[2,256,640]{2,1,0:T(8,128)(2,1)S(1)} %get-tuple-element.41.own, bf16[2,256,768]{2,1,0:T(8,128)(2,1)S(1)} %collective-permute-done.3.from_x, bf16[1024,1024]{1,0:T(8,128)(2,1)S(1)} %get-tuple-element.29.ahead.after.weight), custom_call_target="tpu_custom_call" | custom-call | flops 536870912 | bytes 8388608 | tf_op jit(solution)/shard_map/pallas_call | solution.py:53
  22.3 0.0 collective-permute-done.4.from_y
  22.3 1.6 %collective-permute-start.14 = (bf16[2,2,256,256]{3,2,1,0:T(8,128)(2,1)S(1)}, bf16[2,2,256,256]{3,2,1,0:T(8,128)(2,1)S(1)}, u32[]{:S(2)}, u32[]{:S(2)}) collective-permute-start(bf16[2,2,256,256]{3,2,1,0:T(8,128)(2,1)S(1)} %shard_map.109.after.mine), channel_id=1, source_target_pairs={{0,2},{2,0},{1,3},{3,1},{4,6},{6,4},{5,7},{7,5},{8,10},{10,8},{9,1... | collective-permute-start | bytes 1572872 | tf_op jit(solution)/shard_map/ppermute | solution.py:561
  23.9 0.0 collective-permute-done.5.from_d
  23.9 0.5 %shard_map.111 = (f32[64,1024]{1,0:T(8,128)S(1)}, bf16[64,1024]{1,0:T(8,128)(2,1)S(1)}, bf16[64,1024]{1,0:T(8,128)(2,1)S(1)}, bf16[64,1024]{1,0:T(8,128)(2,1)S(1)}) custom-call(bf16[2,2,256,256]{3,2,1,0:T(8,128)(2,1)S(1)} %shard_map.109.after.mine, bf16[2,32,640]{2,1,0:T(8,128)(2,1)S(1)} %collective-permute-done.4.from_y, ...), custom_call_target="tpu_custom_call" | custom-call | flops 12884901888 | bytes 4194304 | tf_op jit(solution)/shard_map/pallas_call | solution.py:53
  24.4 1.5 %collective-permute-start.10 = (bf16[64,1024]{1,0:T(8,128)(2,1)S(1)}, bf16[64,1024]{1,0:T(8,128)(2,1)S(1)}, u32[]{:S(2)}, u32[]{:S(2)}) collective-permute-start(bf16[64,1024]{1,0:T(8,128)(2,1)S(1)} %get-tuple-element.49), channel_id=1, source_target_pairs={{0,4},{4,0},{8,12},{12,8},{16,20},{20,16},{24,28},{28,24},{1,5},{5... | collective-permute-start | bytes 393224 | tf_op jit(solution)/shard_map/ppermute | solution.py:547
  26.0 0.0 collective-permute-done.6.refs_1_
  26.0 1.6 %collective-permute-start.11 = (bf16[64,1024]{1,0:T(8,128)(2,1)S(1)}, bf16[64,1024]{1,0:T(8,128)(2,1)S(1)}, u32[]{:S(2)}, u32[]{:S(2)}) collective-permute-start(bf16[64,1024]{1,0:T(8,128)(2,1)S(1)} %get-tuple-element.50), channel_id=1, source_target_pairs={{0,8},{4,12},{8,0},{12,4},{16,24},{20,28},{24,16},{28,20},{1,9},{5... | collective-permute-start | bytes 393224 | tf_op jit(solution)/shard_map/ppermute | solution.py:547
  27.5 0.0 collective-permute-done.7.refs_2_
  27.5 0.4 %collective-permute-start.12 = (bf16[64,1024]{1,0:T(8,128)(2,1)S(1)}, bf16[64,1024]{1,0:T(8,128)(2,1)S(1)}, u32[]{:S(2)}, u32[]{:S(2)}) collective-permute-start(bf16[64,1024]{1,0:T(8,128)(2,1)S(1)} %get-tuple-element.51), channel_id=1, source_target_pairs={{0,12},{4,8},{8,4},{12,0},{16,28},{20,24},{24,20},{28,16},{1,13},{... | collective-permute-start | bytes 393224 | tf_op jit(solution)/shard_map/ppermute | solution.py:547
  28.0 0.0 collective-permute-done.8.refs_3_
  28.0 0.1 shard_map.108.early
  28.0 3.0 %collective-permute-done.10.refs_1_ = bf16[64,1024]{1,0:T(8,128)(2,1)S(1)} collective-permute-done((bf16[64,1024]{1,0:T(8,128)(2,1)S(1)}, bf16[64,1024]{1,0:T(8,128)(2,1)S(1)}, u32[]{:S(2)}, u32[]{:S(2)}) %collective-permute-start.10) | collective-permute-done | bytes 131104 | tf_op jit(solution)/shard_map/ppermute | solution.py:547
  31.0 0.8 %collective-permute-done.11.refs_2_ = bf16[64,1024]{1,0:T(8,128)(2,1)S(1)} collective-permute-done((bf16[64,1024]{1,0:T(8,128)(2,1)S(1)}, bf16[64,1024]{1,0:T(8,128)(2,1)S(1)}, u32[]{:S(2)}, u32[]{:S(2)}) %collective-permute-start.11) | collective-permute-done | bytes 131104 | tf_op jit(solution)/shard_map/ppermute | solution.py:547
  31.8 1.9 %collective-permute-done.12.refs_3_ = bf16[64,1024]{1,0:T(8,128)(2,1)S(1)} collective-permute-done((bf16[64,1024]{1,0:T(8,128)(2,1)S(1)}, bf16[64,1024]{1,0:T(8,128)(2,1)S(1)}, u32[]{:S(2)}, u32[]{:S(2)}) %collective-permute-start.12) | collective-permute-done | bytes 131104 | tf_op jit(solution)/shard_map/ppermute | solution.py:547
  33.7 0.1 shard_map.112
  33.8 2.7 %collective-permute-start.15 = (bf16[64,1024]{1,0:T(8,128)(2,1)S(1)}, bf16[64,1024]{1,0:T(8,128)(2,1)S(1)}, u32[]{:S(2)}, u32[]{:S(2)}) collective-permute-start(bf16[64,1024]{1,0:T(8,128)(2,1)S(1)} %get-tuple-element.54), channel_id=1, source_target_pairs={{0,16},{4,20},{8,24},{12,28},{16,0},{20,4},{24,8},{28,12},{1,17},{... | collective-permute-start | bytes 393224 | tf_op jit(solution)/shard_map/ppermute | solution.py:547
  36.5 0.0 collective-permute-start.13
  36.5 1.3 %collective-permute-done.13.from_core = bf16[2,32,512]{2,1,0:T(8,128)(2,1)S(1)} collective-permute-done((bf16[2,32,512]{2,1,0:T(8,128)(2,1)S(1)}, bf16[2,32,512]{2,1,0:T(8,128)(2,1)S(1)}, u32[]{:S(2)}, u32[]{:S(2)}) %collective-permute-start.13) | collective-permute-done | bytes 65568 | tf_op jit(solution)/shard_map/ppermute | solution.py:562
  37.7 1.7 %shard_map.113 = f32[2,512,512]{2,1,0:T(8,128)} custom-call(f32[2,648,768]{2,1,0:T(8,128)S(1)} %get-tuple-element.37.grad, bf16[2,256,768]{2,1,0:T(8,128)(2,1)S(1)} %collective-permute-done.3.from_x, bf16[2,32,640]{2,1,0:T(8,128)(2,1)S(1)} %collective-permute-done.4.from_y, bf16[2,32,640]{2,1,0:T(8,128)(2,1)S(1)} %collective-permute-done.5.from_d, ...), custom_call_target="tpu_custom_call" | custom-call | bytes 6291456 | tf_op jit(solution)/shard_map/pallas_call | solution.py:53
  39.4 0.0 collective-permute-done.14.other
  39.4 1.1 %shard_map.114.after = f32[2,2,256,256]{3,2,1,0:T(8,128)} custom-call(bf16[2,2,256,256]{3,2,1,0:T(8,128)(2,1)S(1)} %shard_map.109.after.mine, bf16[2,2,256,256]{3,2,1,0:T(8,128)(2,1)S(1)} %collective-permute-done.14.other), custom_call_target="tpu_custom_call" | custom-call | bytes 2097152 | tf_op jit(solution)/shard_map/pallas_call | solution.py:53
  40.5 1.2 %collective-permute-done.15.refs_1_ = bf16[64,1024]{1,0:T(8,128)(2,1)S(1)} collective-permute-done((bf16[64,1024]{1,0:T(8,128)(2,1)S(1)}, bf16[64,1024]{1,0:T(8,128)(2,1)S(1)}, u32[]{:S(2)}, u32[]{:S(2)}) %collective-permute-start.15) | collective-permute-done | bytes 131104 | tf_op jit(solution)/shard_map/ppermute | solution.py:547
  41.7 0.8 %shard_map.115 = f32[32,2,1024]{2,1,0:T(2,128)} custom-call(f32[2,2,256,256]{3,2,1,0:T(8,128)} %shard_map.114.after, f32[64,1024]{1,0:T(8,128)S(1)} %get-tuple-element.53.refs_0_, bf16[64,1024]{1,0:T(8,128)(2,1)S(1)} %collective-permute-done.15.refs_1_), custom_call_target="tpu_custom_call" | custom-call | bytes 1048576 | tf_op jit(solution)/shard_map/pallas_call | solution.py:53
Async XLA Ops:
  1.8 8.6 %collective-permute-start.1 = (bf16[2,512,128]{2,1,0:T(8,128)(2,1)S(1)}, bf16[2,512,128]{2,1,0:T(8,128)(2,1)S(1)}, u32[]{:S(2)}, u32[]{:S(2)}) collective-permute-start(bf16[2,512,128]{2,1,0:T(8,128)(2,1)S(1)} %get-tuple-element.32), channel_id=1, source_target_pairs={{0,1},{1,0},{2,3},{3,2},{4,5},{5,4},{6,7},{7,6},{8,9},{9,8},{10,11... | collective-permute-start | bytes 786440 | tf_op jit(solution)/shard_map/ppermute | solution.py:458
  2.3 7.8 %collective-permute-start.2 = (bf16[2,64,128]{2,1,0:T(8,128)(2,1)S(1)}, bf16[2,64,128]{2,1,0:T(8,128)(2,1)S(1)}, u32[]{:S(2)}, u32[]{:S(2)}) collective-permute-start(bf16[2,64,128]{2,1,0:T(8,128)(2,1)S(1)} %get-tuple-element.33), channel_id=1, source_target_pairs={{0,3},{3,0},{1,2},{2,1},{4,7},{7,4},{5,6},{6,5},{8,11},{11,8},{9,1... | collective-permute-start | bytes 98312 | tf_op jit(solution)/shard_map/ppermute | solution.py:457
  4.9 2.7 %copy-start = (bf16[128,1920]{1,0:T(8,128)(2,1)S(1)}, bf16[128,1920]{1,0:T(8,128)(2,1)}, u32[]{:S(2)}) copy-start(bf16[128,1920]{1,0:T(8,128)(2,1)} %constant.5.clone.strip) | copy-start | bytes 1474564
  4.9 5.5 %collective-permute-start = (bf16[2,64,512]{2,1,0:T(8,128)(2,1)S(1)}, bf16[2,64,512]{2,1,0:T(8,128)(2,1)S(1)}, u32[]{:S(2)}, u32[]{:S(2)}) collective-permute-start(bf16[2,64,512]{2,1,0:T(8,128)(2,1)S(1)} %get-tuple-element.31), channel_id=1, source_target_pairs={{0,2},{2,0},{1,3},{3,1},{4,6},{6,4},{5,7},{7,5},{8,10},{10,8},{9,1... | collective-permute-start | bytes 393224 | tf_op jit(solution)/shard_map/ppermute | solution.py:456
  14.5 2.4 %collective-permute-start.3 = (bf16[2,256,768]{2,1,0:T(8,128)(2,1)S(1)}, bf16[2,256,768]{2,1,0:T(8,128)(2,1)S(1)}, u32[]{:S(2)}, u32[]{:S(2)}) collective-permute-start(bf16[2,256,768]{2,1,0:T(8,128)(2,1)S(1)} %get-tuple-element.38), channel_id=1, source_target_pairs={{0,1},{1,0},{2,3},{3,2},{4,5},{5,4},{6,7},{7,6},{8,9},{9,8},{10,11... | collective-permute-start | bytes 2359304 | tf_op jit(solution)/shard_map/ppermute | solution.py:509
  14.6 6.3 %collective-permute-start.9 = (bf16[2,2,256,256]{3,2,1,0:T(8,128)(2,1)S(1)}, bf16[2,2,256,256]{3,2,1,0:T(8,128)(2,1)S(1)}, u32[]{:S(2)}, u32[]{:S(2)}) collective-permute-start(bf16[2,2,256,256]{3,2,1,0:T(8,128)(2,1)S(1)} %get-tuple-element.46.kept), channel_id=1, source_target_pairs={{0,1},{1,0},{2,3},{3,2},{4,5},{5,4},{6,7},{7,6},{8,9},{9,8},{10,11... | collective-permute-start | bytes 1572872 | tf_op jit(solution)/shard_map/ppermute | solution.py:510
  15.1 7.2 %collective-permute-start.4 = (bf16[2,32,640]{2,1,0:T(8,128)(2,1)S(1)}, bf16[2,32,640]{2,1,0:T(8,128)(2,1)S(1)}, u32[]{:S(2)}, u32[]{:S(2)}) collective-permute-start(bf16[2,32,640]{2,1,0:T(8,128)(2,1)S(1)} %get-tuple-element.39), channel_id=1, source_target_pairs={{0,2},{2,0},{1,3},{3,1},{4,6},{6,4},{5,7},{7,5},{8,10},{10,8},{9,1... | collective-permute-start | bytes 245768 | tf_op jit(solution)/shard_map/ppermute | solution.py:511
  16.6 7.3 %collective-permute-start.5 = (bf16[2,32,640]{2,1,0:T(8,128)(2,1)S(1)}, bf16[2,32,640]{2,1,0:T(8,128)(2,1)S(1)}, u32[]{:S(2)}, u32[]{:S(2)}) collective-permute-start(bf16[2,32,640]{2,1,0:T(8,128)(2,1)S(1)} %get-tuple-element.40), channel_id=1, source_target_pairs={{0,3},{3,0},{1,2},{2,1},{4,7},{7,4},{5,6},{6,5},{8,11},{11,8},{9,1... | collective-permute-start | bytes 245768 | tf_op jit(solution)/shard_map/ppermute | solution.py:512
  17.7 8.2 %collective-permute-start.6 = (bf16[64,1024]{1,0:T(8,128)(2,1)S(1)}, bf16[64,1024]{1,0:T(8,128)(2,1)S(1)}, u32[]{:S(2)}, u32[]{:S(2)}) collective-permute-start(bf16[64,1024]{1,0:T(8,128)(2,1)S(1)} %get-tuple-element.43), channel_id=1, source_target_pairs={{0,4},{4,0},{8,12},{12,8},{16,20},{20,16},{24,28},{28,24},{1,5},{5... | collective-permute-start | bytes 393224 | tf_op jit(solution)/shard_map/ppermute | solution.py:547
  19.3 8.2 %collective-permute-start.7 = (bf16[64,1024]{1,0:T(8,128)(2,1)S(1)}, bf16[64,1024]{1,0:T(8,128)(2,1)S(1)}, u32[]{:S(2)}, u32[]{:S(2)}) collective-permute-start(bf16[64,1024]{1,0:T(8,128)(2,1)S(1)} %get-tuple-element.44), channel_id=1, source_target_pairs={{0,8},{4,12},{8,0},{12,4},{16,24},{20,28},{24,16},{28,20},{1,9},{5... | collective-permute-start | bytes 393224 | tf_op jit(solution)/shard_map/ppermute | solution.py:547
  20.9 7.1 %collective-permute-start.8 = (bf16[64,1024]{1,0:T(8,128)(2,1)S(1)}, bf16[64,1024]{1,0:T(8,128)(2,1)S(1)}, u32[]{:S(2)}, u32[]{:S(2)}) collective-permute-start(bf16[64,1024]{1,0:T(8,128)(2,1)S(1)} %get-tuple-element.45), channel_id=1, source_target_pairs={{0,12},{4,8},{8,4},{12,0},{16,28},{20,24},{24,20},{28,16},{1,13},{... | collective-permute-start | bytes 393224 | tf_op jit(solution)/shard_map/ppermute | solution.py:547
  22.3 17.1 %collective-permute-start.14 = (bf16[2,2,256,256]{3,2,1,0:T(8,128)(2,1)S(1)}, bf16[2,2,256,256]{3,2,1,0:T(8,128)(2,1)S(1)}, u32[]{:S(2)}, u32[]{:S(2)}) collective-permute-start(bf16[2,2,256,256]{3,2,1,0:T(8,128)(2,1)S(1)} %shard_map.109.after.mine), channel_id=1, source_target_pairs={{0,2},{2,0},{1,3},{3,1},{4,6},{6,4},{5,7},{7,5},{8,10},{10,8},{9,1... | collective-permute-start | bytes 1572872 | tf_op jit(solution)/shard_map/ppermute | solution.py:561
  24.4 6.6 %collective-permute-start.10 = (bf16[64,1024]{1,0:T(8,128)(2,1)S(1)}, bf16[64,1024]{1,0:T(8,128)(2,1)S(1)}, u32[]{:S(2)}, u32[]{:S(2)}) collective-permute-start(bf16[64,1024]{1,0:T(8,128)(2,1)S(1)} %get-tuple-element.49), channel_id=1, source_target_pairs={{0,4},{4,0},{8,12},{12,8},{16,20},{20,16},{24,28},{28,24},{1,5},{5... | collective-permute-start | bytes 393224 | tf_op jit(solution)/shard_map/ppermute | solution.py:547
  26.0 5.9 %collective-permute-start.11 = (bf16[64,1024]{1,0:T(8,128)(2,1)S(1)}, bf16[64,1024]{1,0:T(8,128)(2,1)S(1)}, u32[]{:S(2)}, u32[]{:S(2)}) collective-permute-start(bf16[64,1024]{1,0:T(8,128)(2,1)S(1)} %get-tuple-element.50), channel_id=1, source_target_pairs={{0,8},{4,12},{8,0},{12,4},{16,24},{20,28},{24,16},{28,20},{1,9},{5... | collective-permute-start | bytes 393224 | tf_op jit(solution)/shard_map/ppermute | solution.py:547
  27.5 6.2 %collective-permute-start.12 = (bf16[64,1024]{1,0:T(8,128)(2,1)S(1)}, bf16[64,1024]{1,0:T(8,128)(2,1)S(1)}, u32[]{:S(2)}, u32[]{:S(2)}) collective-permute-start(bf16[64,1024]{1,0:T(8,128)(2,1)S(1)} %get-tuple-element.51), channel_id=1, source_target_pairs={{0,12},{4,8},{8,4},{12,0},{16,28},{20,24},{24,20},{28,16},{1,13},{... | collective-permute-start | bytes 393224 | tf_op jit(solution)/shard_map/ppermute | solution.py:547
  33.8 7.9 %collective-permute-start.15 = (bf16[64,1024]{1,0:T(8,128)(2,1)S(1)}, bf16[64,1024]{1,0:T(8,128)(2,1)S(1)}, u32[]{:S(2)}, u32[]{:S(2)}) collective-permute-start(bf16[64,1024]{1,0:T(8,128)(2,1)S(1)} %get-tuple-element.54), channel_id=1, source_target_pairs={{0,16},{4,20},{8,24},{12,28},{16,0},{20,4},{24,8},{28,12},{1,17},{... | collective-permute-start | bytes 393224 | tf_op jit(solution)/shard_map/ppermute | solution.py:547
  36.5 1.3 %collective-permute-start.13 = (bf16[2,32,512]{2,1,0:T(8,128)(2,1)S(1)}, bf16[2,32,512]{2,1,0:T(8,128)(2,1)S(1)}, u32[]{:S(2)}, u32[]{:S(2)}) collective-permute-start(bf16[2,32,512]{2,1,0:T(8,128)(2,1)S(1)} %get-tuple-element.52), channel_id=1, source_target_pairs={{0,1},{1,0},{2,3},{3,2},{4,5},{5,4},{6,7},{7,6},{8,9},{9,8},{10,11... | collective-permute-start | bytes 196616 | tf_op jit(solution)/shard_map/ppermute | solution.py:562

commit v6 on v5

--- a/solution.py
+++ b/solution.py
@@ -273,7 +273,7 @@
                 if p < patches - 1:
                     probe_total[m, c] = q
                 else:
-                    probe_here[m, c] = q.astype(bf16)
+                    probe_here[c, :, m * PATCH : (m + 1) * PATCH] = q.astype(bf16)
         top, down, start, shift = place(p)
         for c, g in enumerate((g_re, g_im)):
             turned = [pltpu.roll(g[:, k * BLK : (k + 1) * BLK], shift, 1) for k in range(spans)]
@@ -294,7 +294,7 @@
         for half, wide in ((sx, to_y), (1 - sx, to_d)):
             wide[c, :, 0:cols] = pick_strips(total, c, row_in, RIM, inner, half, h)
             wide[c, :, cols:width] = pick_strips(total, c, row_in, RIM, out_block, half, h)
-        to_x[c, :, width : width + BLK] = own[c, :, cols:width]
+        probe_here[c, :, modes * PATCH :] = own[c, :, cols:width]
 
 
 def column_cuts(sx, cols):
@@ -376,7 +376,7 @@
             ref[(k - 1) * 2 * h : k * 2 * h, :] = part.astype(ref.dtype)
 
 
-def fold_kernel(h, grad, from_x, from_y, from_d, from_core, out):
+def fold_kernel(h, grad, from_x, rim_x, from_y, from_d, from_core, out):
     sy, sx = lax.axis_index("sy"), lax.axis_index("sx")
     f32 = jnp.float32
     rows, cols = out.shape[1], out.shape[2]
@@ -386,7 +386,7 @@
     for c in range(2):
         out[c] = grad[c, RIM : RIM + rows, BLK : BLK + cols]
         add_strips(out, c, 0, rows, edge, sx, h, from_x[c, :, cols : cols + BLK].astype(f32))
-        add_strips(out, c, 0, rows, edge, 1 - sx, h, from_x[c, :, cols + BLK : cols + 2 * BLK].astype(f32))
+        add_strips(out, c, 0, rows, edge, 1 - sx, h, rim_x[c, :, rim_x.shape[2] - BLK :].astype(f32))
         add_strips(out, c, row, RIM, every, sx, h, from_y[c, :, 0:cols].astype(f32))
         add_strips(out, c, row, RIM, edge, sx, h, from_d[c, :, cols:].astype(f32))
         add_strips(out, c, row, RIM, every, 1 - sx, h, from_core[c].astype(f32))
@@ -417,7 +417,10 @@
 
 
 def probe_sum_kernel(after, kept, received, out):
-    out[...] = (kept[...].astype(jnp.float32) + received[...].astype(jnp.float32)).astype(out.dtype)
+    for m in range(out.shape[0]):
+        at = slice(m * PATCH, (m + 1) * PATCH)
+        total = kept[:, :, at].astype(jnp.float32) + received[:, :, at].astype(jnp.float32)
+        out[m] = total.astype(out.dtype)
 
 
 def last_kernel(h, after, *refs):
@@ -489,10 +492,10 @@
         (
             shape((2, rows + 2 * RIM + 8, cols + 2 * BLK), f32),
             shape((2, strip_rows, wide)),
-            shape((2, strip_rows, wide + BLK)),
+            shape((2, strip_rows, wide)),
             shape((2, RIM // 2, wide)),
             shape((2, RIM // 2, wide)),
-            shape((modes, 2, PATCH, PATCH)),
+            shape((2, PATCH, modes * PATCH + BLK)),
         ),
         (pos, weight, obj, halo_y, halo_x, halo_d, probe, measured, dft),
         [HBM, ANY] + [VMEM] * 7,
@@ -563,8 +566,8 @@
     object_grad = call(
         partial(fold_kernel, h),
         shape((2, rows, cols), f32),
-        (grad, from_x, from_y, from_d, from_core),
-        [VMEM] * 5, moved=6 * MIB,
+        (grad, from_x, probe_x, from_y, from_d, from_core),
+        [VMEM] * 6, moved=6 * MIB,
     )
     probe_grad = call(
         partial(probe_kernel, 1.0 / math.sqrt(patches * tiles)),

time: 42.7 us -> 42.7 us (level)
  no operation moved by 1% of the time
where the time goes in v6:
time: 42.7 us; the launch traced here: 42.5 us
  starting transfers between devices  16.6 us (39%)
  Pallas kernels  16.3 us (38%)
  waiting for transfers between devices  8.81 us (21%)
  between operations  0.74 us (2%)
    pallas_call x13, Pallas kernels, call(): pl.pallas_call(kernel, out_shape=outs, in_specs=specs, out_specs=jax.tree...  16.3 us
    ppermute x7, starting transfers between devices, swap(): return lax.ppermute(array, 'ang', [(i, i ^ d) for i in range(n)])  9.76 us
    ppermute x7, waiting for transfers between devices, swap(): return lax.ppermute(array, 'ang', [(i, i ^ d) for i in range(n)])  7.12 us
    ppermute x1, starting transfers between devices, body(): halo_d = lax.ppermute(to_d, ('sy', 'sx'), CROSS)  2.64 us
    ppermute x1, starting transfers between devices, body(): probe_y = lax.ppermute(probe_here, 'sy', SWAP)  1.57 us
    ppermute x1, starting transfers between devices, body(): from_y = lax.ppermute(to_y, 'sy', SWAP)  1.51 us
    ppermute x1, waiting for transfers between devices, body(): from_core = lax.ppermute(to_core, 'sx', SWAP)  1.25 us
  transfers between devices with their start and end apart: 16, of which 7 were waited for; matrix products, arithmetic and copies ran while one was open for 0% of the time, Pallas kernels for 24%

profile of v6, /device:TPU:0, one launch (start us, length us, event | category | flops | bytes accessed | tf_op | source)
XLA Modules:
  0.0 42.5 jit_solution(17664777884974428197)
XLA Ops:
  0.6 1.1 %shard_map.105 = (bf16[2,64,512]{2,1,0:T(8,128)(2,1)S(1)}, bf16[2,512,128]{2,1,0:T(8,128)(2,1)S(1)}, bf16[2,64,128]{2,1,0:T(8,128)(2,1)S(1)}) custom-call(bf16[2,512,512]{2,1,0:T(8,128)(2,1)} %bitcast.8), custom_call_target="tpu_custom_call" | custom-call | bytes 2097152 | tf_op jit(solution)/shard_map/pallas_call | solution.py:53
  1.8 0.5 %collective-permute-start.1 = (bf16[2,512,128]{2,1,0:T(8,128)(2,1)S(1)}, bf16[2,512,128]{2,1,0:T(8,128)(2,1)S(1)}, u32[]{:S(2)}, u32[]{:S(2)}) collective-permute-start(bf16[2,512,128]{2,1,0:T(8,128)(2,1)S(1)} %get-tuple-element.32), channel_id=1, source_target_pairs={{0,1},{1,0},{2,3},{3,2},{4,5},{5,4},{6,7},{7,6},{8,9},{9,8},{10,11... | collective-permute-start | bytes 786440 | tf_op jit(solution)/shard_map/ppermute | solution.py:461
  2.3 2.6 %collective-permute-start.2 = (bf16[2,64,128]{2,1,0:T(8,128)(2,1)S(1)}, bf16[2,64,128]{2,1,0:T(8,128)(2,1)S(1)}, u32[]{:S(2)}, u32[]{:S(2)}) collective-permute-start(bf16[2,64,128]{2,1,0:T(8,128)(2,1)S(1)} %get-tuple-element.33), channel_id=1, source_target_pairs={{0,3},{3,0},{1,2},{2,1},{4,7},{7,4},{5,6},{6,5},{8,11},{11,8},{9,1... | collective-permute-start | bytes 98312 | tf_op jit(solution)/shard_map/ppermute | solution.py:460
  4.9 0.0 copy-start
  4.9 0.1 collective-permute-start
  5.0 2.7 %shard_map.103.matrix = bf16[1024,1024]{1,0:T(8,128)(2,1)S(1)} custom-call(s32[8,16]{1,0:T(8,128)} %index.1, bf16[8,16,128,128]{3,2,1,0:T(8,128)(2,1)} %values.1), custom_call_target="tpu_custom_call" | custom-call | flops 1048576 | bytes 4194304 | tf_op jit(solution)/shard_map/pallas_call | solution.py:53
  7.7 0.0 copy-done
  7.7 2.4 %shard_map.104 = (bf16[1024,1024]{1,0:T(8,128)(2,1)S(1)}, bf16[2,512,512]{2,1,0:T(8,128)(2,1)S(1)}, f32[2,2,256,256]{3,2,1,0:T(8,128)S(1)}, bf16[2,256,256]{2,1,0:T(8,128)(2,1)S(1)}, bf16[2,512,512]{2,1,0:T(8,128)(2,1)S(1)}) custom-call(bf16[1024,1024]{1,0:T(8,128)(2,1)S(1)} %shard_map.103.matrix, bf16[128,1920]{1,0:T(8,128)(2,1)S(1)} %copy-done, ...), custom_call_target="tpu_custom_call" | custom-call | flops 2147483648 | bytes 6291456 | tf_op jit(solution)/shard_map/pallas_call | solution.py:53
  10.1 0.0 collective-permute-done.2.from_d
  10.1 0.3 collective-permute-done.from_y
  10.4 0.0 collective-permute-done.1.from_x
  10.4 4.1 %shard_map.106 = (f32[2,648,768]{2,1,0:T(8,128)S(1)}, bf16[2,256,640]{2,1,0:T(8,128)(2,1)S(1)}, bf16[2,256,640]{2,1,0:T(8,128)(2,1)S(1)}, bf16[2,32,640]{2,1,0:T...) custom-call(s32[2,2]{1,0:T(2,128)} %bitcast.12, ...), custom_call_target="tpu_custom_call" | custom-call | flops 2147483648 | bytes 8388608 | tf_op jit(solution)/shard_map/pallas_call | solution.py:53
  14.5 0.1 collective-permute-start.3
  14.6 0.5 %collective-permute-start.4 = (bf16[2,256,640]{2,1,0:T(8,128)(2,1)S(1)}, bf16[2,256,640]{2,1,0:T(8,128)(2,1)S(1)}, u32[]{:S(2)}, u32[]{:S(2)}) collective-permute-start(bf16[2,256,640]{2,1,0:T(8,128)(2,1)S(1)} %get-tuple-element.39.kept), channel_id=1, source_target_pairs={{0,1},{1,0},{2,3},{3,2},{4,5},{5,4},{6,7},{7,6},{8,9},{9,8},{10,11... | collective-permute-start | bytes 1966088 | tf_op jit(solution)/shard_map/ppermute | solution.py:513
  15.1 1.5 %collective-permute-start.5 = (bf16[2,32,640]{2,1,0:T(8,128)(2,1)S(1)}, bf16[2,32,640]{2,1,0:T(8,128)(2,1)S(1)}, u32[]{:S(2)}, u32[]{:S(2)}) collective-permute-start(bf16[2,32,640]{2,1,0:T(8,128)(2,1)S(1)} %get-tuple-element.40), channel_id=1, source_target_pairs={{0,2},{2,0},{1,3},{3,1},{4,6},{6,4},{5,7},{7,5},{8,10},{10,8},{9,1... | collective-permute-start | bytes 245768 | tf_op jit(solution)/shard_map/ppermute | solution.py:514
  16.6 0.0 collective-permute-start.6
  16.6 0.1 collective-permute-done.3.from_x
  16.7 0.9 %shard_map.107 = (f32[4,64,1024]{2,1,0:T(8,128)S(1)}, f32[64,1024]{1,0:T(8,128)S(1)}, bf16[64,1024]{1,0:T(8,128)(2,1)S(1)}, bf16[64,1024]{1,0:T(8,128)(2,1)S(1)}, bf16[64,1024]{1,0:T(8,128)(2,1)S(1)}) custom-call(bf16[1024,1024]{1,0:T(8,128)(2,1)S(1)} %get-tuple-element.29.ahead.after.weight, bf16[2,256,640]{2,1,0:T(8,128)(2,1)S(1)} %get-tuple-element.42.own, ...), custom_call_target="tpu_custom_call" | custom-call | flops 536870912 | bytes 8388608 | tf_op jit(solution)/shard_map/pallas_call | solution.py:53
  17.6 1.5 %collective-permute-start.7 = (bf16[64,1024]{1,0:T(8,128)(2,1)S(1)}, bf16[64,1024]{1,0:T(8,128)(2,1)S(1)}, u32[]{:S(2)}, u32[]{:S(2)}) collective-permute-start(bf16[64,1024]{1,0:T(8,128)(2,1)S(1)} %get-tuple-element.44), channel_id=1, source_target_pairs={{0,4},{4,0},{8,12},{12,8},{16,20},{20,16},{24,28},{28,24},{1,5},{5... | collective-permute-start | bytes 393224 | tf_op jit(solution)/shard_map/ppermute | solution.py:550
  19.1 1.6 %collective-permute-start.8 = (bf16[64,1024]{1,0:T(8,128)(2,1)S(1)}, bf16[64,1024]{1,0:T(8,128)(2,1)S(1)}, u32[]{:S(2)}, u32[]{:S(2)}) collective-permute-start(bf16[64,1024]{1,0:T(8,128)(2,1)S(1)} %get-tuple-element.45), channel_id=1, source_target_pairs={{0,8},{4,12},{8,0},{12,4},{16,24},{20,28},{24,16},{28,20},{1,9},{5... | collective-permute-start | bytes 393224 | tf_op jit(solution)/shard_map/ppermute | solution.py:550
  20.7 0.0 collective-permute-done.4.received.rim_x
  20.7 0.4 %collective-permute-start.9 = (bf16[64,1024]{1,0:T(8,128)(2,1)S(1)}, bf16[64,1024]{1,0:T(8,128)(2,1)S(1)}, u32[]{:S(2)}, u32[]{:S(2)}) collective-permute-start(bf16[64,1024]{1,0:T(8,128)(2,1)S(1)} %get-tuple-element.46), channel_id=1, source_target_pairs={{0,12},{4,8},{8,4},{12,0},{16,28},{20,24},{24,20},{28,16},{1,13},{... | collective-permute-start | bytes 393224 | tf_op jit(solution)/shard_map/ppermute | solution.py:550
  21.1 0.1 shard_map.109.after.mine
  21.2 0.8 %shard_map.110.chunks = f32[4,64,1024]{2,1,0:T(8,128)S(1)} custom-call(f32[4,64,1024]{2,1,0:T(8,128)S(1)} %get-tuple-element.47.after, bf16[2,256,640]{2,1,0:T(8,128)(2,1)S(1)} %get-tuple-element.42.own, bf16[2,256,640]{2,1,0:T(8,128)(2,1)S(1)} %collective-permute-done.3.from_x, bf16[1024,1024]{1,0:T(8,128)(2,1)S(1)} %get-tuple-element.29.ahead.after.weight), custom_call_target="tpu_custom_call" | custom-call | flops 536870912 | bytes 8388608 | tf_op jit(solution)/shard_map/pallas_call | solution.py:53
  22.1 0.0 collective-permute-done.5.from_y
  22.1 1.6 %collective-permute-start.14 = (bf16[2,2,256,256]{3,2,1,0:T(8,128)(2,1)S(1)}, bf16[2,2,256,256]{3,2,1,0:T(8,128)(2,1)S(1)}, u32[]{:S(2)}, u32[]{:S(2)}) collective-permute-start(bf16[2,2,256,256]{3,2,1,0:T(8,128)(2,1)S(1)} %shard_map.109.after.mine), channel_id=1, source_target_pairs={{0,2},{2,0},{1,3},{3,1},{4,6},{6,4},{5,7},{7,5},{8,10},{10,8},{9,1... | collective-permute-start | bytes 1572872 | tf_op jit(solution)/shard_map/ppermute | solution.py:564
  23.6 0.0 collective-permute-done.6.from_d
  23.6 0.5 %shard_map.111 = (f32[64,1024]{1,0:T(8,128)S(1)}, bf16[64,1024]{1,0:T(8,128)(2,1)S(1)}, bf16[64,1024]{1,0:T(8,128)(2,1)S(1)}, bf16[64,1024]{1,0:T(8,128)(2,1)S(1)}) custom-call(bf16[2,2,256,256]{3,2,1,0:T(8,128)(2,1)S(1)} %shard_map.109.after.mine, bf16[2,32,640]{2,1,0:T(8,128)(2,1)S(1)} %collective-permute-done.5.from_y, ...), custom_call_target="tpu_custom_call" | custom-call | flops 12884901888 | bytes 4194304 | tf_op jit(solution)/shard_map/pallas_call | solution.py:53
  24.2 1.5 %collective-permute-start.10 = (bf16[64,1024]{1,0:T(8,128)(2,1)S(1)}, bf16[64,1024]{1,0:T(8,128)(2,1)S(1)}, u32[]{:S(2)}, u32[]{:S(2)}) collective-permute-start(bf16[64,1024]{1,0:T(8,128)(2,1)S(1)} %get-tuple-element.49), channel_id=1, source_target_pairs={{0,4},{4,0},{8,12},{12,8},{16,20},{20,16},{24,28},{28,24},{1,5},{5... | collective-permute-start | bytes 393224 | tf_op jit(solution)/shard_map/ppermute | solution.py:550
  25.7 0.0 collective-permute-done.7.refs_1_
  25.7 1.6 %collective-permute-start.11 = (bf16[64,1024]{1,0:T(8,128)(2,1)S(1)}, bf16[64,1024]{1,0:T(8,128)(2,1)S(1)}, u32[]{:S(2)}, u32[]{:S(2)}) collective-permute-start(bf16[64,1024]{1,0:T(8,128)(2,1)S(1)} %get-tuple-element.50), channel_id=1, source_target_pairs={{0,8},{4,12},{8,0},{12,4},{16,24},{20,28},{24,16},{28,20},{1,9},{5... | collective-permute-start | bytes 393224 | tf_op jit(solution)/shard_map/ppermute | solution.py:550
  27.3 0.0 collective-permute-done.8.refs_2_
  27.3 0.4 %collective-permute-start.12 = (bf16[64,1024]{1,0:T(8,128)(2,1)S(1)}, bf16[64,1024]{1,0:T(8,128)(2,1)S(1)}, u32[]{:S(2)}, u32[]{:S(2)}) collective-permute-start(bf16[64,1024]{1,0:T(8,128)(2,1)S(1)} %get-tuple-element.51), channel_id=1, source_target_pairs={{0,12},{4,8},{8,4},{12,0},{16,28},{20,24},{24,20},{28,16},{1,13},{... | collective-permute-start | bytes 393224 | tf_op jit(solution)/shard_map/ppermute | solution.py:550
  27.8 0.0 collective-permute-done.9.refs_3_
  27.8 0.1 shard_map.108.early
  27.8 3.3 %collective-permute-done.10.refs_1_ = bf16[64,1024]{1,0:T(8,128)(2,1)S(1)} collective-permute-done((bf16[64,1024]{1,0:T(8,128)(2,1)S(1)}, bf16[64,1024]{1,0:T(8,128)(2,1)S(1)}, u32[]{:S(2)}, u32[]{:S(2)}) %collective-permute-start.10) | collective-permute-done | bytes 131104 | tf_op jit(solution)/shard_map/ppermute | solution.py:550
  31.1 0.6 %collective-permute-done.11.refs_2_ = bf16[64,1024]{1,0:T(8,128)(2,1)S(1)} collective-permute-done((bf16[64,1024]{1,0:T(8,128)(2,1)S(1)}, bf16[64,1024]{1,0:T(8,128)(2,1)S(1)}, u32[]{:S(2)}, u32[]{:S(2)}) %collective-permute-start.11) | collective-permute-done | bytes 131104 | tf_op jit(solution)/shard_map/ppermute | solution.py:550
  31.8 1.7 %collective-permute-done.12.refs_3_ = bf16[64,1024]{1,0:T(8,128)(2,1)S(1)} collective-permute-done((bf16[64,1024]{1,0:T(8,128)(2,1)S(1)}, bf16[64,1024]{1,0:T(8,128)(2,1)S(1)}, u32[]{:S(2)}, u32[]{:S(2)}) %collective-permute-start.12) | collective-permute-done | bytes 131104 | tf_op jit(solution)/shard_map/ppermute | solution.py:550
  33.5 0.1 shard_map.112
  33.6 2.6 %collective-permute-start.15 = (bf16[64,1024]{1,0:T(8,128)(2,1)S(1)}, bf16[64,1024]{1,0:T(8,128)(2,1)S(1)}, u32[]{:S(2)}, u32[]{:S(2)}) collective-permute-start(bf16[64,1024]{1,0:T(8,128)(2,1)S(1)} %get-tuple-element.54), channel_id=1, source_target_pairs={{0,16},{4,20},{8,24},{12,28},{16,0},{20,4},{24,8},{28,12},{1,17},{... | collective-permute-start | bytes 393224 | tf_op jit(solution)/shard_map/ppermute | solution.py:550
  36.2 0.0 collective-permute-start.13
  36.2 1.3 %collective-permute-done.13.from_core = bf16[2,32,512]{2,1,0:T(8,128)(2,1)S(1)} collective-permute-done((bf16[2,32,512]{2,1,0:T(8,128)(2,1)S(1)}, bf16[2,32,512]{2,1,0:T(8,128)(2,1)S(1)}, u32[]{:S(2)}, u32[]{:S(2)}) %collective-permute-start.13) | collective-permute-done | bytes 65568 | tf_op jit(solution)/shard_map/ppermute | solution.py:565
  37.5 1.7 %shard_map.113 = f32[2,512,512]{2,1,0:T(8,128)} custom-call(f32[2,648,768]{2,1,0:T(8,128)S(1)} %get-tuple-element.37.grad, bf16[2,256,640]{2,1,0:T(8,128)(2,1)S(1)} %collective-permute-done.3.from_x, bf16[2,256,640]{2,1,0:T(8,128)(2,1)S(1)} %collective-permute-done.4.received.rim_x, bf16[2,32,640]{2,1,0:T(8,128)(2,1)S(1)} %collective-permute-done.5.from_y, ...), custom_call_target="tpu_custom_call" | custom-call | bytes 6291456 | tf_op jit(solution)/shard_map/pallas_call | solution.py:53
  39.2 0.0 collective-permute-done.14.other
  39.2 1.1 %shard_map.114.after = f32[2,2,256,256]{3,2,1,0:T(8,128)} custom-call(bf16[2,2,256,256]{3,2,1,0:T(8,128)(2,1)S(1)} %shard_map.109.after.mine, bf16[2,2,256,256]{3,2,1,0:T(8,128)(2,1)S(1)} %collective-permute-done.14.other), custom_call_target="tpu_custom_call" | custom-call | bytes 2097152 | tf_op jit(solution)/shard_map/pallas_call | solution.py:53
  40.3 1.4 %collective-permute-done.15.refs_1_ = bf16[64,1024]{1,0:T(8,128)(2,1)S(1)} collective-permute-done((bf16[64,1024]{1,0:T(8,128)(2,1)S(1)}, bf16[64,1024]{1,0:T(8,128)(2,1)S(1)}, u32[]{:S(2)}, u32[]{:S(2)}) %collective-permute-start.15) | collective-permute-done | bytes 131104 | tf_op jit(solution)/shard_map/ppermute | solution.py:550
  41.7 0.8 %shard_map.115 = f32[32,2,1024]{2,1,0:T(2,128)} custom-call(f32[2,2,256,256]{3,2,1,0:T(8,128)} %shard_map.114.after, f32[64,1024]{1,0:T(8,128)S(1)} %get-tuple-element.53.refs_0_, bf16[64,1024]{1,0:T(8,128)(2,1)S(1)} %collective-permute-done.15.refs_1_), custom_call_target="tpu_custom_call" | custom-call | bytes 1048576 | tf_op jit(solution)/shard_map/pallas_call | solution.py:53
Async XLA Ops:
  1.8 8.6 %collective-permute-start.1 = (bf16[2,512,128]{2,1,0:T(8,128)(2,1)S(1)}, bf16[2,512,128]{2,1,0:T(8,128)(2,1)S(1)}, u32[]{:S(2)}, u32[]{:S(2)}) collective-permute-start(bf16[2,512,128]{2,1,0:T(8,128)(2,1)S(1)} %get-tuple-element.32), channel_id=1, source_target_pairs={{0,1},{1,0},{2,3},{3,2},{4,5},{5,4},{6,7},{7,6},{8,9},{9,8},{10,11... | collective-permute-start | bytes 786440 | tf_op jit(solution)/shard_map/ppermute | solution.py:461
  2.3 7.8 %collective-permute-start.2 = (bf16[2,64,128]{2,1,0:T(8,128)(2,1)S(1)}, bf16[2,64,128]{2,1,0:T(8,128)(2,1)S(1)}, u32[]{:S(2)}, u32[]{:S(2)}) collective-permute-start(bf16[2,64,128]{2,1,0:T(8,128)(2,1)S(1)} %get-tuple-element.33), channel_id=1, source_target_pairs={{0,3},{3,0},{1,2},{2,1},{4,7},{7,4},{5,6},{6,5},{8,11},{11,8},{9,1... | collective-permute-start | bytes 98312 | tf_op jit(solution)/shard_map/ppermute | solution.py:460
  4.9 2.7 %copy-start = (bf16[128,1920]{1,0:T(8,128)(2,1)S(1)}, bf16[128,1920]{1,0:T(8,128)(2,1)}, u32[]{:S(2)}) copy-start(bf16[128,1920]{1,0:T(8,128)(2,1)} %constant.5.clone.strip) | copy-start | bytes 1474564
  4.9 5.5 %collective-permute-start = (bf16[2,64,512]{2,1,0:T(8,128)(2,1)S(1)}, bf16[2,64,512]{2,1,0:T(8,128)(2,1)S(1)}, u32[]{:S(2)}, u32[]{:S(2)}) collective-permute-start(bf16[2,64,512]{2,1,0:T(8,128)(2,1)S(1)} %get-tuple-element.31), channel_id=1, source_target_pairs={{0,2},{2,0},{1,3},{3,1},{4,6},{6,4},{5,7},{7,5},{8,10},{10,8},{9,1... | collective-permute-start | bytes 393224 | tf_op jit(solution)/shard_map/ppermute | solution.py:459
  14.5 2.2 %collective-permute-start.3 = (bf16[2,256,640]{2,1,0:T(8,128)(2,1)S(1)}, bf16[2,256,640]{2,1,0:T(8,128)(2,1)S(1)}, u32[]{:S(2)}, u32[]{:S(2)}) collective-permute-start(bf16[2,256,640]{2,1,0:T(8,128)(2,1)S(1)} %get-tuple-element.38), channel_id=1, source_target_pairs={{0,1},{1,0},{2,3},{3,2},{4,5},{5,4},{6,7},{7,6},{8,9},{9,8},{10,11... | collective-permute-start | bytes 1966088 | tf_op jit(solution)/shard_map/ppermute | solution.py:512
  14.6 6.1 %collective-permute-start.4 = (bf16[2,256,640]{2,1,0:T(8,128)(2,1)S(1)}, bf16[2,256,640]{2,1,0:T(8,128)(2,1)S(1)}, u32[]{:S(2)}, u32[]{:S(2)}) collective-permute-start(bf16[2,256,640]{2,1,0:T(8,128)(2,1)S(1)} %get-tuple-element.39.kept), channel_id=1, source_target_pairs={{0,1},{1,0},{2,3},{3,2},{4,5},{5,4},{6,7},{7,6},{8,9},{9,8},{10,11... | collective-permute-start | bytes 1966088 | tf_op jit(solution)/shard_map/ppermute | solution.py:513
  15.1 7.0 %collective-permute-start.5 = (bf16[2,32,640]{2,1,0:T(8,128)(2,1)S(1)}, bf16[2,32,640]{2,1,0:T(8,128)(2,1)S(1)}, u32[]{:S(2)}, u32[]{:S(2)}) collective-permute-start(bf16[2,32,640]{2,1,0:T(8,128)(2,1)S(1)} %get-tuple-element.40), channel_id=1, source_target_pairs={{0,2},{2,0},{1,3},{3,1},{4,6},{6,4},{5,7},{7,5},{8,10},{10,8},{9,1... | collective-permute-start | bytes 245768 | tf_op jit(solution)/shard_map/ppermute | solution.py:514
  16.6 7.1 %collective-permute-start.6 = (bf16[2,32,640]{2,1,0:T(8,128)(2,1)S(1)}, bf16[2,32,640]{2,1,0:T(8,128)(2,1)S(1)}, u32[]{:S(2)}, u32[]{:S(2)}) collective-permute-start(bf16[2,32,640]{2,1,0:T(8,128)(2,1)S(1)} %get-tuple-element.41), channel_id=1, source_target_pairs={{0,3},{3,0},{1,2},{2,1},{4,7},{7,4},{5,6},{6,5},{8,11},{11,8},{9,1... | collective-permute-start | bytes 245768 | tf_op jit(solution)/shard_map/ppermute | solution.py:515
  17.6 8.2 %collective-permute-start.7 = (bf16[64,1024]{1,0:T(8,128)(2,1)S(1)}, bf16[64,1024]{1,0:T(8,128)(2,1)S(1)}, u32[]{:S(2)}, u32[]{:S(2)}) collective-permute-start(bf16[64,1024]{1,0:T(8,128)(2,1)S(1)} %get-tuple-element.44), channel_id=1, source_target_pairs={{0,4},{4,0},{8,12},{12,8},{16,20},{20,16},{24,28},{28,24},{1,5},{5... | collective-permute-start | bytes 393224 | tf_op jit(solution)/shard_map/ppermute | solution.py:550
  19.1 8.2 %collective-permute-start.8 = (bf16[64,1024]{1,0:T(8,128)(2,1)S(1)}, bf16[64,1024]{1,0:T(8,128)(2,1)S(1)}, u32[]{:S(2)}, u32[]{:S(2)}) collective-permute-start(bf16[64,1024]{1,0:T(8,128)(2,1)S(1)} %get-tuple-element.45), channel_id=1, source_target_pairs={{0,8},{4,12},{8,0},{12,4},{16,24},{20,28},{24,16},{28,20},{1,9},{5... | collective-permute-start | bytes 393224 | tf_op jit(solution)/shard_map/ppermute | solution.py:550
  20.7 7.1 %collective-permute-start.9 = (bf16[64,1024]{1,0:T(8,128)(2,1)S(1)}, bf16[64,1024]{1,0:T(8,128)(2,1)S(1)}, u32[]{:S(2)}, u32[]{:S(2)}) collective-permute-start(bf16[64,1024]{1,0:T(8,128)(2,1)S(1)} %get-tuple-element.46), channel_id=1, source_target_pairs={{0,12},{4,8},{8,4},{12,0},{16,28},{20,24},{24,20},{28,16},{1,13},{... | collective-permute-start | bytes 393224 | tf_op jit(solution)/shard_map/ppermute | solution.py:550
  22.1 17.1 %collective-permute-start.14 = (bf16[2,2,256,256]{3,2,1,0:T(8,128)(2,1)S(1)}, bf16[2,2,256,256]{3,2,1,0:T(8,128)(2,1)S(1)}, u32[]{:S(2)}, u32[]{:S(2)}) collective-permute-start(bf16[2,2,256,256]{3,2,1,0:T(8,128)(2,1)S(1)} %shard_map.109.after.mine), channel_id=1, source_target_pairs={{0,2},{2,0},{1,3},{3,1},{4,6},{6,4},{5,7},{7,5},{8,10},{10,8},{9,1... | collective-permute-start | bytes 1572872 | tf_op jit(solution)/shard_map/ppermute | solution.py:564
  24.2 7.0 %collective-permute-start.10 = (bf16[64,1024]{1,0:T(8,128)(2,1)S(1)}, bf16[64,1024]{1,0:T(8,128)(2,1)S(1)}, u32[]{:S(2)}, u32[]{:S(2)}) collective-permute-start(bf16[64,1024]{1,0:T(8,128)(2,1)S(1)} %get-tuple-element.49), channel_id=1, source_target_pairs={{0,4},{4,0},{8,12},{12,8},{16,20},{20,16},{24,28},{28,24},{1,5},{5... | collective-permute-start | bytes 393224 | tf_op jit(solution)/shard_map/ppermute | solution.py:550
  25.7 6.1 %collective-permute-start.11 = (bf16[64,1024]{1,0:T(8,128)(2,1)S(1)}, bf16[64,1024]{1,0:T(8,128)(2,1)S(1)}, u32[]{:S(2)}, u32[]{:S(2)}) collective-permute-start(bf16[64,1024]{1,0:T(8,128)(2,1)S(1)} %get-tuple-element.50), channel_id=1, source_target_pairs={{0,8},{4,12},{8,0},{12,4},{16,24},{20,28},{24,16},{28,20},{1,9},{5... | collective-permute-start | bytes 393224 | tf_op jit(solution)/shard_map/ppermute | solution.py:550
  27.3 6.2 %collective-permute-start.12 = (bf16[64,1024]{1,0:T(8,128)(2,1)S(1)}, bf16[64,1024]{1,0:T(8,128)(2,1)S(1)}, u32[]{:S(2)}, u32[]{:S(2)}) collective-permute-start(bf16[64,1024]{1,0:T(8,128)(2,1)S(1)} %get-tuple-element.51), channel_id=1, source_target_pairs={{0,12},{4,8},{8,4},{12,0},{16,28},{20,24},{24,20},{28,16},{1,13},{... | collective-permute-start | bytes 393224 | tf_op jit(solution)/shard_map/ppermute | solution.py:550
  33.6 8.1 %collective-permute-start.15 = (bf16[64,1024]{1,0:T(8,128)(2,1)S(1)}, bf16[64,1024]{1,0:T(8,128)(2,1)S(1)}, u32[]{:S(2)}, u32[]{:S(2)}) collective-permute-start(bf16[64,1024]{1,0:T(8,128)(2,1)S(1)} %get-tuple-element.54), channel_id=1, source_target_pairs={{0,16},{4,20},{8,24},{12,28},{16,0},{20,4},{24,8},{28,12},{1,17},{... | collective-permute-start | bytes 393224 | tf_op jit(solution)/shard_map/ppermute | solution.py:550
  36.2 1.3 %collective-permute-start.13 = (bf16[2,32,512]{2,1,0:T(8,128)(2,1)S(1)}, bf16[2,32,512]{2,1,0:T(8,128)(2,1)S(1)}, u32[]{:S(2)}, u32[]{:S(2)}) collective-permute-start(bf16[2,32,512]{2,1,0:T(8,128)(2,1)S(1)} %get-tuple-element.52), channel_id=1, source_target_pairs={{0,1},{1,0},{2,3},{3,2},{4,5},{5,4},{6,7},{7,6},{8,9},{9,8},{10,11... | collective-permute-start | bytes 196616 | tf_op jit(solution)/shard_map/ppermute | solution.py:565
